TPU v7x, 256 devices: a whole 4x4x8 slice. The times are simulated.
256 devices in a mesh: row: 32 (over z, x_lo, core), col: 8 (over x_hi, y).
Axes of the slice: x: 4 (x_hi: 2, x_lo: 2; x = x_hi * 2 + x_lo), y: 4, z: 8, core: 2. Of those that a mesh axis runs over, the one named last changes fastest.
Arguments:
- features: bfloat16 [65536, 128], P(('row', 'col')), may hold values from -6 to 6
- tiles: bfloat16 [32, 8, 96, 128, 128], P('row', 'col'), may hold values from -0.09375 to 0.09375
- tile_src: int32 [32, 8, 96], P('row', 'col'), may hold values from 0 to 15
- tile_dst: int32 [32, 8, 96], P('row', 'col'), may hold values from 0 to 63
- tile_count: int32 [32, 8], P('row', 'col'), may hold values from 12 to 96, as said below
- degree: int32 [65536], P(('row', 'col')), may hold values from 1 to 8
- w_self: bfloat16 [128, 128], replicated, may hold values from -0.5 to 0.5
- w_neigh: bfloat16 [128, 128], replicated, may hold values from -0.5 to 0.5
- bias: float32 [128], replicated, may hold values from -3 to 3
- upstream: bfloat16 [65536, 128], P(('row', 'col')), may hold values from -6 to 6
Outputs:
- hidden: bfloat16 [65536, 128], P(('row', 'col'))
- grad_features: bfloat16 [65536, 128], P(('row', 'col'))
- grad_self: float32 [128, 128], replicated
- grad_neigh: float32 [128, 128], replicated
- grad_bias: float32 [128], replicated
Inputs may be any that keep to these rules, and one draw needn't show every extreme that they name: Slots at or past tile_count hold no edges; some device has all 96 slots live in every draw.
All inputs are finite; a program needn't handle non-finite values.
Results may differ from a plain program's by a relative error of at most 0.039.
The roundings to bfloat16 on the way count: a program that leaves them out, or rounds other values in their place, can miss the bound.
Values may be sent and summed in bfloat16 or wider, within the bound.
No kernel may reach another device: no remote copies, remote signals or barrier semaphores. Data moves between devices by JAX's collectives and lax.ppermute only.
A program may use at most 64 MiB of HBM per device.

v0:
```python
import jax
import jax.numpy as jnp
from jax import lax
from jax.sharding import PartitionSpec as P

TILE = 128


def source_side(field, tiles, src_ids, dst_ids, live):
    fdim = field.shape[-1]
    nsrc = field.shape[0] * lax.axis_size("col") // TILE
    gathered = lax.all_gather(field, "row", axis=0, tiled=True)
    targets = gathered.reshape(-1, TILE, fdim)[dst_ids]
    behind = jnp.einsum("tab,taf->tbf", tiles, targets, preferred_element_type=jnp.float32)
    part = jax.ops.segment_sum(behind, jnp.where(live, src_ids, nsrc), nsrc + 1)[:nsrc]
    return lax.psum_scatter(part.reshape(nsrc * TILE, fdim), "col", scatter_dimension=0, tiled=True)


def target_side(field, tiles, src_ids, dst_ids, live):
    fdim = field.shape[-1]
    owned = field.shape[0]
    ndst = owned * lax.axis_size("row") // TILE
    gathered = lax.all_gather(field, "col", axis=0, tiled=True)
    sources = gathered.reshape(-1, TILE, fdim)[src_ids]
    ahead = jnp.einsum("tab,tbf->taf", tiles, sources, preferred_element_type=jnp.float32)
    part = jax.ops.segment_sum(ahead, jnp.where(live, dst_ids, ndst), ndst + 1)[:ndst]
    return lax.psum_scatter(part.reshape(ndst * TILE, fdim), "row", scatter_dimension=0, tiled=True)


def aggregate(field, tiles, src_ids, dst_ids, live):
    first = target_side(field, tiles, src_ids, dst_ids, live)
    second = source_side(field, tiles, src_ids, dst_ids, live)
    return first + second


def body(features, tiles, tile_src, tile_dst, tile_count, degree, w_self, w_neigh, bias, upstream):
    held = tiles[0, 0]
    src_ids = tile_src[0, 0]
    dst_ids = tile_dst[0, 0]
    live = jnp.arange(held.shape[0], dtype=jnp.int32) < tile_count[0, 0]
    inverse = 1.0 / degree.astype(jnp.float32)
    summed = aggregate(features, held, src_ids, dst_ids, live)
    agg = (summed * inverse[:, None]).astype(jnp.bfloat16)
    pre = (
        jnp.dot(features, w_self, preferred_element_type=jnp.float32)
        + jnp.dot(agg, w_neigh, preferred_element_type=jnp.float32)
        + bias
    )
    hidden = jnp.maximum(pre, 0.0).astype(jnp.bfloat16)
    dpre = jnp.where(pre > 0, upstream.astype(jnp.float32), 0.0).astype(jnp.bfloat16)
    local_self = jnp.dot(features.T, dpre, preferred_element_type=jnp.float32)
    local_neigh = jnp.dot(agg.T, dpre, preferred_element_type=jnp.float32)
    local_bias = jnp.sum(dpre.astype(jnp.float32), axis=0)
    grad_self, grad_neigh, grad_bias = lax.psum(
        (local_self, local_neigh, local_bias), ("row", "col")
    )
    scaled = (
        jnp.dot(dpre, w_neigh.T, preferred_element_type=jnp.float32) * inverse[:, None]
    ).astype(jnp.bfloat16)
    carried = aggregate(scaled, held, src_ids, dst_ids, live)
    grad_features = (jnp.dot(dpre, w_self.T, preferred_element_type=jnp.float32) + carried).astype(
        jnp.bfloat16
    )
    return (hidden, grad_features, grad_self, grad_neigh, grad_bias)


def solution(mesh):
    return jax.shard_map(
        body,
        mesh=mesh,
        in_specs=(
            P(("row", "col"), None),
            P("row", "col", None, None, None),
            P("row", "col", None),
            P("row", "col", None),
            P("row", "col"),
            P(("row", "col")),
            P(),
            P(),
            P(),
            P(("row", "col"), None),
        ),
        out_specs=(P(("row", "col"), None), P(("row", "col"), None), P(), P(), P()),
        check_vma=False,
    )
```

profile of v0, /device:TPU:1, one launch (start us, length us, event | category | flops | bytes accessed | tf_op | source)
XLA Modules:
  0.0 851.9 jit_solution(3414292055938994618)
XLA Ops:
  7.2 0.0 copy-start
  7.2 0.0 all-gather.3.cloned.1.call-start
  7.2 0.7 all-gather.3.cloned.1.call-update
  7.9 0.0 reduce-scatter.7.cloned.1.call-start
  8.8 0.7 fusion.24
  9.5 69.3 %all-gather.3.cloned.1.call-done = bf16[8192,128]{1,0:T(8,128)(2,1)} async-done(((bf16[256,128]{1,0:T(8,128)(2,1)}), bf16[8192,128]{1,0:T(8,128)(2,1)}) %all-gather.3.cloned.1.call-update) | async-done | bytes 2097168 | tf_op jit(solution)/shard_map/all_gather | solution.py:12
  78.8 4.3 gather_fusion.1
  83.1 0.0 copy-done
  83.1 5.7 fusion.11
  88.8 6.6 copy.23
  95.4 1.1 broadcast.74.clone
  96.5 21.6 %scatter_fusion.1 = f32[17,128,128]{2,1,0:T(8,128)} fusion(f32[17,128,128]{2,1,0:T(8,128)} %broadcast.74.clone, s32[96]{0:T(128)S(1)} %get-tuple-element.21, f32[96,128,128]{2,1,0:T(8,128)} %copy.23), kind=kCustom, calls=%fused_computation.5 | custom fusion | flops 1572864 | bytes 18874752 | tf_op jit(solution)/shard_map/scatter-add | solution.py:15
  118.1 2.4 slice.25
  120.5 0.0 reduce-scatter.7.cloned.1.call-update
  120.5 0.0 reduce-scatter.5.cloned.1.call-start
  120.6 31.1 %all_gather.12 = bf16[2048,128]{1,0:T(8,128)(2,1)} all-gather(bf16[256,128]{1,0:T(8,128)(2,1)S(1)} %copy-done.1), channel_id=1, replica_groups=mesh['row'=32,'col'=8] {'col'}, dimensions={0}, use_global_device_ids=true | all-gather | bytes 589824 | tf_op jit(solution)/shard_map/all_gather | solution.py:23
  151.7 3.8 gather_fusion
  155.4 6.9 fusion.8
  162.3 6.6 copy.21
  168.9 2.6 broadcast.71.clone
  171.4 22.6 %scatter_fusion = f32[65,128,128]{2,1,0:T(8,128)} fusion(f32[65,128,128]{2,1,0:T(8,128)} %broadcast.71.clone, s32[96]{0:T(128)S(1)} %get-tuple-element.25, f32[96,128,128]{2,1,0:T(8,128)} %copy.21), kind=kCustom, calls=%fused_computation.4 | custom fusion | flops 1572864 | bytes 18874752 | tf_op jit(solution)/shard_map/scatter-add | solution.py:26
  194.0 4.6 slice.24
  198.7 0.0 reduce-scatter.5.cloned.1.call-update
  198.7 0.0 all-gather.5.cloned.1.call-start
  198.7 0.6 copy-done.7
  199.3 0.1 copy-done.4
  199.4 0.1 fusion.27
  199.6 0.0 reduce-scatter.7.cloned.1.call-done
  199.6 123.6 %reduce-scatter.5.cloned.1.call-done = f32[256,128]{1,0:T(8,128)} async-done(((f32[8192,128]{1,0:T(8,128)}), f32[256,128]{1,0:T(8,128)}) %reduce-scatter.5.cloned.1.call-update) | async-done | bytes 131088 | tf_op jit(solution)/shard_map/reduce_scatter | solution.py:27
  323.2 1.1 multiply_convert_fusion
  324.3 0.8 maximum_convert_fusion
  325.1 0.9 convert_reduce_fusion
  326.0 0.8 fusion.22
  326.8 0.0 all-gather.5.cloned.1.call-update
  326.8 0.0 all-reduce.3.cloned.1.call-start
  326.8 0.8 fusion.28
  327.7 0.8 convolution_bitcast_fusion
  328.5 0.0 all-reduce.3.cloned.1.call-update
  328.5 0.0 reduce-scatter.11.cloned.1.call-start
  328.6 65.6 %all-gather.5.cloned.1.call-done = bf16[8192,128]{1,0:T(8,128)(2,1)} async-done(((bf16[256,128]{1,0:T(8,128)(2,1)}), bf16[8192,128]{1,0:T(8,128)(2,1)}) %all-gather.5.cloned.1.call-update) | async-done | bytes 2097168 | tf_op jit(solution)/shard_map/all_gather | solution.py:12
  394.2 4.3 gather_fusion.3
  398.4 5.7 fusion.17
  404.2 6.6 copy.27
  410.8 1.1 broadcast.74
  411.9 21.6 %scatter_fusion.3 = f32[17,128,128]{2,1,0:T(8,128)} fusion(f32[17,128,128]{2,1,0:T(8,128)} %broadcast.74, s32[96]{0:T(128)S(1)} %copy-done.6, f32[96,128,128]{2,1,0:T(8,128)} %copy.27), kind=kCustom, calls=%fused_computation.7 | custom fusion | flops 1572864 | bytes 18874752 | tf_op jit(solution)/shard_map/scatter-add | solution.py:15
  433.5 2.4 slice.27
  435.9 0.0 reduce-scatter.11.cloned.1.call-update
  435.9 0.0 reduce-scatter.9.cloned.1.call-start
  435.9 0.0 copy-done.2
  436.0 31.1 %all_gather.14 = bf16[2048,128]{1,0:T(8,128)(2,1)} all-gather(bf16[256,128]{1,0:T(8,128)(2,1)S(1)} %copy-done.2), channel_id=1, replica_groups=mesh['row'=32,'col'=8] {'col'}, dimensions={0}, use_global_device_ids=true | all-gather | bytes 589824 | tf_op jit(solution)/shard_map/all_gather | solution.py:23
  467.0 3.7 gather_fusion.2
  470.8 6.9 fusion.14
  477.7 6.6 copy.25
  484.3 2.6 broadcast.71
  486.8 22.6 %scatter_fusion.2 = f32[65,128,128]{2,1,0:T(8,128)} fusion(f32[65,128,128]{2,1,0:T(8,128)} %broadcast.71, s32[96]{0:T(128)S(1)} %get-tuple-element.25, f32[96,128,128]{2,1,0:T(8,128)} %copy.25), kind=kCustom, calls=%fused_computation.6 | custom fusion | flops 1572864 | bytes 18874752 | tf_op jit(solution)/shard_map/scatter-add | solution.py:26
  509.4 4.6 slice.26
  514.0 0.0 reduce-scatter.9.cloned.1.call-update
  514.1 79.5 %psum.23 = f32[128]{0:T(128)} all-reduce(f32[128]{0:T(128)S(1)} %get-tuple-element.17), channel_id=1, replica_groups=mesh['row'=32,'col'=8] {'row','col'}, use_global_device_ids=true, to_apply=%region_11.12 | all-reduce | flops 128 | bytes 1024 | tf_op jit(solution)/shard_map/psum | solution.py:54
  593.6 48.0 %all-reduce.3.cloned.1.call-done = (f32[128,128]{0,1:T(8,128)}, f32[128,128]{1,0:T(8,128)}) async-done(((f32[128,128]{0,1:T(8,128)}, f32[128,128]{1,0:T(8,128)}), (f32[128,128]{0,1:T(8,128)}, f32[128,128]{1,0:T(8,128)})) %all-reduce.3.cloned.1.call-update) | async-done | bytes 131088 | tf_op jit(solution)/shard_map/psum | solution.py:54
  641.6 1.6 copy.28
  643.2 75.3 %reduce-scatter.11.cloned.1.call-done = f32[256,128]{1,0:T(8,128)} async-done(((f32[2048,128]{1,0:T(8,128)}), f32[256,128]{1,0:T(8,128)}) %reduce-scatter.11.cloned.1.call-update) | async-done | bytes 131088 | tf_op jit(solution)/shard_map/reduce_scatter | solution.py:16
  718.5 123.3 %reduce-scatter.9.cloned.1.call-done = f32[256,128]{1,0:T(8,128)} async-done(((f32[8192,128]{1,0:T(8,128)}), f32[256,128]{1,0:T(8,128)}) %reduce-scatter.9.cloned.1.call-update) | async-done | bytes 131088 | tf_op jit(solution)/shard_map/reduce_scatter | solution.py:27
  841.8 1.8 fusion.21
  843.6 1.5 copy.40
  (16 shorter events, 0.0 us)
Async XLA Ops:
  7.2 75.9 %copy-start = (bf16[1,1,96,128,128]{4,3,2,1,0:T(8,128)(2,1)S(1)}, bf16[1,1,96,128,128]{4,3,2,1,0:T(8,128)(2,1)}, u32[]{:S(2)}) copy-start(bf16[1,1,96,128,128]{4,3,2,1,0:T(8,128)(2,1)} %param.11) | copy-start | bytes 9437188
  7.2 71.6 %all-gather.3.cloned.1.call-start = ((), (), s32[]{:S(2)}) async-start(), calls=%async_computation.5 | async-start | bytes 2162688 | tf_op jit(solution)/shard_map/all_gather | solution.py:12
  7.9 191.7 %reduce-scatter.7.cloned.1.call-start = ((), (), s32[]{:S(2)}) async-start(), calls=%async_computation.6 | async-start | bytes 1179648 | tf_op jit(solution)/shard_map/reduce_scatter | solution.py:16
  9.5 87.1 %copy-start.5 = (s32[96]{0:T(128)}, s32[96]{0:T(128)S(1)}, u32[]{:S(2)}) copy-start(s32[96]{0:T(128)S(1)} %get-tuple-element.21) | copy-start | bytes 1156
  118.1 2.5 copy-start.1
  120.5 202.7 %reduce-scatter.5.cloned.1.call-start = ((), (), s32[]{:S(2)}) async-start(), calls=%async_computation.4 | async-start | bytes 4325376 | tf_op jit(solution)/shard_map/reduce_scatter | solution.py:27
  198.7 0.7 copy-start.7
  198.7 0.8 copy-start.4
  198.7 125.6 %copy-start.3 = (bf16[128,128]{1,0:T(8,128)(2,1)S(1)}, bf16[128,128]{1,0:T(8,128)(2,1)}, u32[]{:S(2)}) copy-start(bf16[128,128]{1,0:T(8,128)(2,1)} %param.17) | copy-start | bytes 98308
  198.7 125.6 %copy-start.8 = (f32[128]{0:T(128)S(1)}, f32[128]{0:T(128)}, u32[]{:S(2)}) copy-start(f32[128]{0:T(128)} %param.18) | copy-start | bytes 1540
  198.7 195.5 %all-gather.5.cloned.1.call-start = ((), (), s32[]{:S(2)}) async-start(), calls=%async_computation.8 | async-start | bytes 2162688 | tf_op jit(solution)/shard_map/all_gather | solution.py:12
  326.8 314.8 %all-reduce.3.cloned.1.call-start = ((), (), s32[]{:S(2)}) async-start(), calls=%async_computation.10 | async-start | bytes 262144 | tf_op jit(solution)/shard_map/psum | solution.py:54
  328.5 390.0 %reduce-scatter.11.cloned.1.call-start = ((), (), s32[]{:S(2)}) async-start(), calls=%async_computation.9 | async-start | bytes 1179648 | tf_op jit(solution)/shard_map/reduce_scatter | solution.py:16
  404.2 7.7 copy-start.6
  433.5 2.5 copy-start.2
  435.9 405.9 %reduce-scatter.9.cloned.1.call-start = ((), (), s32[]{:S(2)}) async-start(), calls=%async_computation.7 | async-start | bytes 4325376 | tf_op jit(solution)/shard_map/reduce_scatter | solution.py:27
Sparse Core Ops, SparseCore 0:
  9.9 68.8 all-gather.2
  120.6 74.1 reduce-scatter.6
  198.8 124.3 reduce-scatter.4
  326.9 67.1 all-gather.4
  401.1 240.4 all-reduce.2
  645.8 72.6 reduce-scatter.10
  721.0 120.7 reduce-scatter.8
where the time goes:
time: 856 us; the launch traced here: 852 us
  waiting for transfers between devices  506 us (59%)
  blocking collectives  142 us (17%)
  other arithmetic  90.9 us (11%)
  local copies, waits for them, and re-layouts  67.6 us (8%)
  matrix products  30.4 us (4%)
  between operations  15 us (2%)
    reduce_scatter x2, waiting for transfers between devices, target_side(): lax.psum_scatter(part.reshape(ndst * TILE, fdim), 'row', scatter_dimensio...  247 us
    all_gather x2, waiting for transfers between devices, source_side(): gathered = lax.all_gather(field, 'row', axis=0, tiled=True)  135 us
    psum x1, blocking collectives, body(): lax.psum((local_self, local_neigh, local_bias), ('row', 'col'))  79.5 us
    reduce_scatter x2, waiting for transfers between devices, source_side(): lax.psum_scatter(part.reshape(nsrc * TILE, fdim), 'col', scatter_dimensio...  75.3 us
    all_gather x2, blocking collectives, target_side(): gathered = lax.all_gather(field, 'col', axis=0, tiled=True)  62.1 us
    psum x1, waiting for transfers between devices, body(): lax.psum((local_self, local_neigh, local_bias), ('row', 'col'))  48 us
    scatter-add x2, other arithmetic, target_side(): jax.ops.segment_sum(ahead, jnp.where(live, dst_ids, ndst), ndst + 1)[:ndst]  45.2 us
    scatter-add x2, other arithmetic, source_side(): jax.ops.segment_sum(behind, jnp.where(live, src_ids, nsrc), nsrc + 1)[:nsrc]  43.1 us
  transfers between devices with their start and end apart: 7, of which 6 were waited for; matrix products, arithmetic and copies ran while one was open for 16% of the time, Pallas kernels for 0%

commit v1 on v0

v1 whole, which is shorter than its diff:
```python
import functools

import jax
import jax.numpy as jnp
from jax import lax
from jax.experimental import pallas as pl
from jax.experimental.pallas import tpu as pltpu
from jax.sharding import Mesh
from jax.sharding import PartitionSpec as P

TILE = 128
GROUP = 16
UNROLL = 8
ROW = ("z", "xl", "co")
COL = ("xh", "y")
SWAP = ((0, 1), (1, 0))
VMEM_LIMIT = 48 * 1024 * 1024


def whole(shape):
    return pl.BlockSpec(shape, lambda *_: (0,) * len(shape))


def steps(count, i):
    live = jnp.clip(count - i * GROUP, 0, GROUP)
    return (live + UNROLL - 1) // UNROLL


def ahead_kernel(src_ref, slot_ref, count_ref, field_ref, tiles_ref, keep_ref, send_ref, acc_ref):
    i = pl.program_id(0)
    half = keep_ref.shape[0]

    @pl.when(i == 0)
    def _():
        acc_ref[...] = jnp.zeros_like(acc_ref)

    def step(k, carry):
        outs = []
        for u in range(UNROLL):
            j = k * UNROLL + u
            t = i * GROUP + j
            outs.append(
                jnp.dot(
                    tiles_ref[j],
                    field_ref[jnp.minimum(src_ref[t], 15)],
                    preferred_element_type=jnp.float32,
                )
            )
        for u in range(UNROLL):
            t = i * GROUP + k * UNROLL + u
            acc_ref[slot_ref[t]] += outs[u]
        return carry

    lax.fori_loop(0, steps(count_ref[0], i), step, 0)

    @pl.when(i == pl.num_programs(0) - 1)
    def _():
        keep_ref[...] = acc_ref[:half]
        send_ref[...] = acc_ref[half : 2 * half].astype(send_ref.dtype)


def ahead(field, tiles, src, slot, count):
    n = tiles.shape[0]
    half = 32
    return pl.pallas_call(
        ahead_kernel,
        grid_spec=pltpu.PrefetchScalarGridSpec(
            num_scalar_prefetch=3,
            grid=(n // GROUP,),
            in_specs=[whole(field.shape), pl.BlockSpec((GROUP, TILE, TILE), lambda i, *_: (i, 0, 0))],
            out_specs=[whole((half, TILE, TILE))] * 2,
            scratch_shapes=[pltpu.VMEM((2 * half + 1, TILE, TILE), jnp.float32)],
        ),
        out_shape=[
            jax.ShapeDtypeStruct((half, TILE, TILE), jnp.float32),
            jax.ShapeDtypeStruct((half, TILE, TILE), jnp.bfloat16),
        ],
        compiler_params=pltpu.CompilerParams(vmem_limit_bytes=VMEM_LIMIT),
        cost_estimate=pl.CostEstimate(flops=2 * n * TILE**3, bytes_accessed=n * TILE * TILE * 2, transcendentals=0),
    )(src, slot, count, field, tiles)


def behind_kernel(src_ref, slot_ref, count_ref, g0, g1, g2, g3, tiles_ref, out_ref, field_ref, acc_ref):
    i = pl.program_id(0)
    n = g0.shape[0]

    @pl.when(i == 0)
    def _():
        acc_ref[...] = jnp.zeros_like(acc_ref)
        for k, g in enumerate((g0, g1, g2, g3)):
            field_ref[k * n : (k + 1) * n] = g[...]
        field_ref[4 * n] = jnp.zeros_like(field_ref[4 * n])

    def step(k, carry):
        outs = []
        for u in range(UNROLL):
            j = k * UNROLL + u
            t = i * GROUP + j
            outs.append(
                jnp.dot(field_ref[slot_ref[t]], tiles_ref[j], preferred_element_type=jnp.float32)
            )
        for u in range(UNROLL):
            t = i * GROUP + k * UNROLL + u
            acc_ref[src_ref[t]] += outs[u]
        return carry

    lax.fori_loop(0, steps(count_ref[0], i), step, 0)

    @pl.when(i == pl.num_programs(0) - 1)
    def _():
        for k in range(out_ref.shape[0]):
            out_ref[k] = acc_ref[k].T.astype(out_ref.dtype)


def behind(parts, tiles, src, slot, count):
    n = tiles.shape[0]
    nsrc = 16
    return pl.pallas_call(
        behind_kernel,
        grid_spec=pltpu.PrefetchScalarGridSpec(
            num_scalar_prefetch=3,
            grid=(n // GROUP,),
            in_specs=[whole(p.shape) for p in parts]
            + [pl.BlockSpec((GROUP, TILE, TILE), lambda i, *_: (i, 0, 0))],
            out_specs=whole((nsrc, TILE, TILE)),
            scratch_shapes=[
                pltpu.VMEM((65, TILE, TILE), jnp.bfloat16),
                pltpu.VMEM((nsrc + 1, TILE, TILE), jnp.float32),
            ],
        ),
        out_shape=jax.ShapeDtypeStruct((nsrc, TILE, TILE), jnp.bfloat16),
        compiler_params=pltpu.CompilerParams(vmem_limit_bytes=VMEM_LIMIT),
        cost_estimate=pl.CostEstimate(flops=2 * n * TILE**3, bytes_accessed=n * TILE * TILE * 2, transcendentals=0),
    )(src, slot, count, *parts, tiles)


def swap(x, axis):
    return lax.ppermute(x, axis, SWAP)


def spread(x, axes, n):
    return lax.all_to_all(jnp.broadcast_to(x[None], (n,) + x.shape), axes, 0, 0, tiled=True)


def turned(x):
    return x.reshape(-1, TILE, TILE).swapaxes(1, 2)


def aggregate(field, field_t, tiles, src, slot, count):
    with jax.named_scope("gather_col"):
        sources = spread(field.reshape(-1, TILE, TILE), COL, 8).reshape(-1, TILE, TILE)
    with jax.named_scope("gather_row"):
        g00 = spread(field_t, "z", 8).reshape(-1, TILE, TILE)
        g01 = swap(g00, "xl")
        g10 = swap(g00, "co")
        g11 = swap(g01, "co")
    with jax.named_scope("ahead"):
        keep, send = ahead(sources, tiles, src, slot, count)
    with jax.named_scope("behind"):
        back = behind((g00, g01, g10, g11), tiles, src, slot, count)
    with jax.named_scope("scatter_row"):
        got = swap(send, "co")
        both = keep + got.astype(jnp.float32)
        got = swap(both[16:].astype(jnp.bfloat16), "xl")
        four = both[:16] + got.astype(jnp.float32)
        first = lax.all_to_all(
            four.astype(jnp.bfloat16).reshape(8, -1, TILE), "z", 0, 0, tiled=True
        )
    with jax.named_scope("scatter_col"):
        second = lax.all_to_all(back.reshape(8, -1, TILE), COL, 0, 0, tiled=True)
    return first, second


def total(first, second):
    return jnp.sum(first.astype(jnp.float32), axis=0) + jnp.sum(second.astype(jnp.float32), axis=0)


def body(features, tiles, tile_src, tile_dst, tile_count, degree, w_self, w_neigh, bias, upstream):
    held = tiles[0, 0]
    count = tile_count[0]
    live = jnp.arange(held.shape[0], dtype=jnp.int32) < count[0]
    src = jnp.where(live, tile_src[0, 0], 16)
    dst = tile_dst[0, 0]
    other_co = ((dst // 2) % 2) ^ lax.axis_index("co")
    other_xl = ((dst // 4) % 2) ^ lax.axis_index("xl")
    slot = (other_co * 2 + other_xl) * 16 + (dst // 8) * 2 + dst % 2
    slot = jnp.where(live, slot, 64)
    inverse = 1.0 / degree.astype(jnp.float32)

    first, second = aggregate(features, turned(features), held, src, slot, count)
    agg = (total(first, second) * inverse[:, None]).astype(jnp.bfloat16)
    pre = (
        jnp.dot(features, w_self, preferred_element_type=jnp.float32)
        + jnp.dot(agg, w_neigh, preferred_element_type=jnp.float32)
        + bias
    )
    hidden = jnp.maximum(pre, 0.0).astype(jnp.bfloat16)
    dpre = jnp.where(pre > 0, upstream.astype(jnp.float32), 0.0).astype(jnp.bfloat16)
    scaled = (
        jnp.dot(dpre, w_neigh.T, preferred_element_type=jnp.float32) * inverse[:, None]
    ).astype(jnp.bfloat16)
    with jax.named_scope("weights"):
        local = jnp.concatenate(
            [
                jnp.dot(features.T, dpre, preferred_element_type=jnp.float32),
                jnp.dot(agg.T, dpre, preferred_element_type=jnp.float32),
                jnp.broadcast_to(jnp.sum(dpre.astype(jnp.float32), axis=0)[None] / 8, (8, TILE)),
            ]
        )
        for axis, n in (("co", 2), ("xl", 2), ("z", 8), ("xh", 2), ("y", 4)):
            d = 1
            while d < n:
                local = local + lax.ppermute(local, axis, [(i, i ^ d) for i in range(n)])
                d *= 2
    first, second = aggregate(scaled, turned(scaled), held, src, slot, count)
    carried = total(first, second)
    grad_features = (jnp.dot(dpre, w_self.T, preferred_element_type=jnp.float32) + carried).astype(
        jnp.bfloat16
    )
    return (
        hidden,
        grad_features,
        local[:TILE],
        local[TILE : 2 * TILE],
        jnp.sum(local[2 * TILE :], axis=0),
    )


def solution(mesh):
    fine = Mesh(mesh.devices.reshape(8, 2, 2, 2, 4), ROW + COL)
    nodes = P(ROW + COL, None)
    return jax.shard_map(
        body,
        mesh=fine,
        in_specs=(
            nodes,
            P(ROW, COL, None, None, None),
            P(ROW, COL, None),
            P(ROW, COL, None),
            P(ROW, COL),
            P(ROW + COL),
            P(),
            P(),
            P(),
            nodes,
        ),
        out_specs=(nodes, nodes, P(), P(), P()),
        check_vma=False,
    )
```

time: 856 us -> 228 us (0.27)
  the two profiles are of different devices: /device:TPU:1 before, /device:TPU:54 now
where the time goes in v1:
time: 228 us; the launch traced here: 226 us
  waiting for transfers between devices  114 us (50%)
  starting transfers between devices  71.7 us (31%)
  Pallas kernels  20.4 us (9%)
  other arithmetic  8.46 us (4%)
  local copies, waits for them, and re-layouts  7.61 us (3%)
  matrix products  2.29 us (1%)
    ppermute x8, waiting for transfers between devices, body(): local = local + lax.ppermute(local, axis, [(i, i ^ d) for i in range(n)])  38.8 us
    all_to_all x4, waiting for transfers between devices, spread(): lax.all_to_all(jnp.broadcast_to(x[None], (n,) + x.shape), axes, 0, 0, til...  30.5 us
    all_to_all x4, starting transfers between devices, spread(): lax.all_to_all(jnp.broadcast_to(x[None], (n,) + x.shape), axes, 0, 0, til...  29.4 us
    ppermute x10, waiting for transfers between devices, swap(): return lax.ppermute(x, axis, SWAP)  24 us
    all_to_all x2, waiting for transfers between devices, aggregate(): lax.all_to_all(four.astype(jnp.bfloat16).reshape(8, -1, TILE), 'z', 0, 0,...  16.3 us
    all_to_all x2, starting transfers between devices, aggregate(): lax.all_to_all(four.astype(jnp.bfloat16).reshape(8, -1, TILE), 'z', 0, 0,...  15.8 us
    all_to_all x2, starting transfers between devices, aggregate(): second = lax.all_to_all(back.reshape(8, -1, TILE), COL, 0, 0, tiled=True)  14.5 us
    pallas_call x2, Pallas kernels, ahead(): pl.pallas_call(ahead_kernel, grid_spec=pltpu.PrefetchScalarGridSpec(num_s...  12.6 us
  transfers between devices with their start and end apart: 26, of which 14 were waited for; matrix products, arithmetic and copies ran while one was open for 5% of the time, Pallas kernels for 9%

profile of v1, /device:TPU:54, one launch (start us, length us, event | category | flops | bytes accessed | tf_op | source)
XLA Modules:
  0.0 226.1 jit_solution(8189003542044688778)
XLA Ops:
  0.7 1.8 broadcast_in_dim.47
  2.4 7.2 %all-to-all-start = ((bf16[8,2,128,128]{3,2,1,0:T(8,128)(2,1)}), bf16[8,2,128,128]{3,2,1,0:T(8,128)(2,1)S(1)}, u32[]{:S(2)}, u32[]{:S(2)}) async-start(bf16[8,2,128,128]{3,2,1,0:T(8,128)(2,1)} %broadcast_in_dim.47), calls=%async_computation | async-start | bytes 1048576 | tf_op jit(solution)/shard_map/gather_col/all_to_all | solution.py:142
  9.6 0.9 copy.15
  10.6 5.6 %all-to-all-done = bf16[8,2,128,128]{3,2,1,0:T(8,128)(2,1)S(1)} async-done(((bf16[8,2,128,128]{3,2,1,0:T(8,128)(2,1)}), bf16[8,2,128,128]{3,2,1,0:T(8,128)(2,1)S(1)}, u32[]{:S(2)}, u32[]{:S(2)}) %all-to-all-start) | async-done | bytes 524320 | tf_op jit(solution)/shard_map/gather_col/all_to_all | solution.py:142
  16.1 0.9 broadcast_in_dim.48
  17.0 8.6 %all-to-all-start.2 = ((bf16[8,2,128,128]{3,2,1,0:T(8,128)(2,1)}), bf16[8,2,128,128]{3,2,1,0:T(8,128)(2,1)}, u32[]{:S(2)}, u32[]{:S(2)}) async-start(bf16[8,2,128,128]{3,2,1,0:T(8,128)(2,1)} %broadcast_in_dim.48), calls=%async_computation.2 | async-start | bytes 1048576 | tf_op jit(solution)/shard_map/gather_row/all_to_all | solution.py:142
  26.3 6.3 %ahead.2 = (f32[32,128,128]{2,1,0:T(8,128)S(1)}, bf16[32,128,128]{2,1,0:T(8,128)(2,1)}) custom-call(s32[96]{0:T(128)S(1)} %get-tuple-element.20.src_ref, s32[96]{0:T(128)S(1)} %get-tuple-element.19.slot_ref, s32[1]{0:T(128)} %bitcast.54.count_ref, bf16[16,128,128]{2,1,0:T(8,128)(2,1)S(1)} %bitcast.65, bf16[96,128,128]{2,1,0:T(8,128)(2,1)} %bitcast.58), custom_call_target="tpu_custom_call" | custom-call | flops 402653184 | bytes 3145728 | tf_op jit(solution)/shard_map/ahead/pallas_call | solution.py:65
  32.6 9.3 %all-to-all-done.2 = bf16[8,2,128,128]{3,2,1,0:T(8,128)(2,1)} async-done(((bf16[8,2,128,128]{3,2,1,0:T(8,128)(2,1)}), bf16[8,2,128,128]{3,2,1,0:T(8,128)(2,1)}, u32[]{:S(2)}, u32[]{:S(2)}) %all-to-all-start.2) | async-done | bytes 524320 | tf_op jit(solution)/shard_map/gather_row/all_to_all | solution.py:142
  41.9 0.8 collective-permute-start.2
  42.8 11.0 %collective-permute-done.2.g1 = bf16[16,128,128]{2,1,0:T(8,128)(2,1)S(1)} collective-permute-done((bf16[16,128,128]{2,1,0:T(8,128)(2,1)}, bf16[16,128,128]{2,1,0:T(8,128)(2,1)S(1)}, u32[]{:S(2)}, u32[]{:S(2)}) %collective-permute-start.2) | collective-permute-done | bytes 524320 | tf_op jit(solution)/shard_map/gather_row/ppermute | solution.py:138
  53.8 1.7 convert_add_fusion.1
  55.5 0.1 slice.47
  55.6 0.9 collective-permute-start.1
  56.5 0.3 copy-done.5
  56.8 4.5 %behind.2 = bf16[16,128,128]{2,1,0:T(8,128)(2,1)} custom-call(s32[96]{0:T(128)S(1)} %get-tuple-element.20.src_ref, s32[96]{0:T(128)S(1)} %get-tuple-element.19.slot_ref, s32[1]{0:T(128)} %bitcast.55.count_ref, bf16[16,128,128]{2,1,0:T(8,128)(2,1)} %bitcast.9.g0, bf16[16,128,128]{2,1,0:T(8,128)(2,1)S(1)} %collective-permute-done.2.g1, ...), custom_call_target="tpu_custom_call" | custom-call | flops 402653184 | bytes 3145728 | tf_op jit(solution)/shard_map/behind/pallas_call | solution.py:118
  61.3 7.3 %all-to-all-start.3 = ((bf16[8,256,128]{2,1,0:T(8,128)(2,1)}), bf16[8,256,128]{2,1,0:T(8,128)(2,1)S(1)}, u32[]{:S(2)}, u32[]{:S(2)}) async-start(bf16[8,256,128]{2,1,0:T(8,128)(2,1)} %bitcast.10), calls=%async_computation.3 | async-start | bytes 1048576 | tf_op jit(solution)/shard_map/scatter_col/all_to_all | solution.py:170
  68.6 1.5 collective-permute-done.1
  70.1 2.0 fusion.4
  72.1 4.4 %all-to-all-done.3 = bf16[8,256,128]{2,1,0:T(8,128)(2,1)S(1)} async-done(((bf16[8,256,128]{2,1,0:T(8,128)(2,1)}), bf16[8,256,128]{2,1,0:T(8,128)(2,1)S(1)}, u32[]{:S(2)}, u32[]{:S(2)}) %all-to-all-start.3) | async-done | bytes 524320 | tf_op jit(solution)/shard_map/scatter_col/all_to_all | solution.py:170
  76.5 7.5 %all-to-all-start.1 = ((bf16[8,256,128]{2,1,0:T(8,128)(2,1)}), bf16[8,256,128]{2,1,0:T(8,128)(2,1)S(1)}, u32[]{:S(2)}, u32[]{:S(2)}) async-start(bf16[8,256,128]{2,1,0:T(8,128)(2,1)} %bitcast.7), calls=%async_computation.1 | async-start | bytes 1048576 | tf_op jit(solution)/shard_map/scatter_row/all_to_all | solution.py:166
  84.0 0.1 fusion.15
  84.2 0.1 convert_reduce_fusion.2
  84.2 16.3 %all-to-all-done.1 = bf16[8,256,128]{2,1,0:T(8,128)(2,1)S(1)} async-done(((bf16[8,256,128]{2,1,0:T(8,128)(2,1)}), bf16[8,256,128]{2,1,0:T(8,128)(2,1)S(1)}, u32[]{:S(2)}, u32[]{:S(2)}) %all-to-all-start.1) | async-done | bytes 524320 | tf_op jit(solution)/shard_map/scatter_row/all_to_all | solution.py:166
  100.6 0.1 convert_reduce_fusion.3
  100.6 0.1 multiply_convert_fusion
  100.7 0.8 maximum_convert_fusion
  101.6 0.2 fusion.2
  101.8 0.9 broadcast_in_dim.50
  102.7 7.8 %all-to-all-start.4 = ((bf16[8,2,128,128]{3,2,1,0:T(8,128)(2,1)}), bf16[8,2,128,128]{3,2,1,0:T(8,128)(2,1)S(1)}, u32[]{:S(2)}, u32[]{:S(2)}) async-start(bf16[8,2,128,128]{3,2,1,0:T(8,128)(2,1)} %broadcast_in_dim.50), calls=%async_computation.4 | async-start | bytes 1048576 | tf_op jit(solution)/shard_map/gather_col/all_to_all | solution.py:142
  110.5 0.1 copy.16
  110.6 5.6 %all-to-all-done.4 = bf16[8,2,128,128]{3,2,1,0:T(8,128)(2,1)S(1)} async-done(((bf16[8,2,128,128]{3,2,1,0:T(8,128)(2,1)}), bf16[8,2,128,128]{3,2,1,0:T(8,128)(2,1)S(1)}, u32[]{:S(2)}, u32[]{:S(2)}) %all-to-all-start.4) | async-done | bytes 524320 | tf_op jit(solution)/shard_map/gather_col/all_to_all | solution.py:142
  116.2 0.9 broadcast_in_dim.51
  117.1 5.8 %all-to-all-start.6 = ((bf16[8,2,128,128]{3,2,1,0:T(8,128)(2,1)}), bf16[8,2,128,128]{3,2,1,0:T(8,128)(2,1)S(1)}, u32[]{:S(2)}, u32[]{:S(2)}) async-start(bf16[8,2,128,128]{3,2,1,0:T(8,128)(2,1)} %broadcast_in_dim.51), calls=%async_computation.6 | async-start | bytes 1048576 | tf_op jit(solution)/shard_map/gather_row/all_to_all | solution.py:142
  122.9 6.3 %ahead.3 = (f32[32,128,128]{2,1,0:T(8,128)S(1)}, bf16[32,128,128]{2,1,0:T(8,128)(2,1)}) custom-call(s32[96]{0:T(128)S(1)} %get-tuple-element.20.src_ref, s32[96]{0:T(128)S(1)} %get-tuple-element.19.slot_ref, s32[1]{0:T(128)} %bitcast.56.count_ref, bf16[16,128,128]{2,1,0:T(8,128)(2,1)S(1)} %bitcast.66, bf16[96,128,128]{2,1,0:T(8,128)(2,1)} %bitcast.59), custom_call_target="tpu_custom_call" | custom-call | flops 402653184 | bytes 3145728 | tf_op jit(solution)/shard_map/ahead/pallas_call | solution.py:65
  129.2 0.2 fusion.16
  129.4 10.0 %all-to-all-done.6 = bf16[8,2,128,128]{3,2,1,0:T(8,128)(2,1)S(1)} async-done(((bf16[8,2,128,128]{3,2,1,0:T(8,128)(2,1)}), bf16[8,2,128,128]{3,2,1,0:T(8,128)(2,1)S(1)}, u32[]{:S(2)}, u32[]{:S(2)}) %all-to-all-start.6) | async-done | bytes 524320 | tf_op jit(solution)/shard_map/gather_row/all_to_all | solution.py:142
  139.5 0.5 collective-permute-start.7
  140.0 0.2 convolution_bitcast_fusion
  140.2 0.1 collective-permute-start.10
  140.3 0.5 collective-permute-start.8
  140.8 11.5 %collective-permute-done.7.g1 = bf16[16,128,128]{2,1,0:T(8,128)(2,1)S(1)} collective-permute-done((bf16[16,128,128]{2,1,0:T(8,128)(2,1)S(1)}, bf16[16,128,128]{2,1,0:T(8,128)(2,1)S(1)}, u32[]{:S(2)}, u32[]{:S(2)}) %collective-permute-start.7) | collective-permute-done | bytes 524320 | tf_op jit(solution)/shard_map/gather_row/ppermute | solution.py:138
  152.3 1.7 convert_add_fusion
  154.0 1.0 slice.46
  155.0 0.5 collective-permute-start.6
  155.5 1.6 collective-permute-start.11
  157.1 15.3 %collective-permute-done.11 = f32[264,128]{1,0:T(8,128)S(1)} collective-permute-done((f32[264,128]{1,0:T(8,128)S(1)}, f32[264,128]{1,0:T(8,128)S(1)}, u32[]{:S(2)}, u32[]{:S(2)}) %collective-permute-start.11) | collective-permute-done | bytes 135200 | tf_op jit(solution)/shard_map/weights/ppermute | solution.py:213
  172.4 2.7 %collective-permute-start.12 = (f32[264,128]{1,0:T(8,128)S(1)}, f32[264,128]{1,0:T(8,128)S(1)}, u32[]{:S(2)}, u32[]{:S(2)}) collective-permute-start(f32[264,128]{1,0:T(8,128)S(1)} %add.99), channel_id=1, source_target_pairs={{0,32},{32,0},{64,96},{96,64},{128,160},{160,128},{192,224},{224,1... | collective-permute-start | bytes 405512 | tf_op jit(solution)/shard_map/weights/ppermute | solution.py:213
  175.2 3.3 %behind.3 = bf16[16,128,128]{2,1,0:T(8,128)(2,1)} custom-call(s32[96]{0:T(128)S(1)} %get-tuple-element.20.src_ref, s32[96]{0:T(128)S(1)} %get-tuple-element.19.slot_ref, s32[1]{0:T(128)} %bitcast.57.count_ref, bf16[16,128,128]{2,1,0:T(8,128)(2,1)S(1)} %bitcast.64, bf16[16,128,128]{2,1,0:T(8,128)(2,1)S(1)} %collective-permute-done.7.g1, ...), custom_call_target="tpu_custom_call" | custom-call | flops 402653184 | bytes 3145728 | tf_op jit(solution)/shard_map/behind/pallas_call | solution.py:118
  178.5 7.2 %all-to-all-start.7 = ((bf16[8,256,128]{2,1,0:T(8,128)(2,1)}), bf16[8,256,128]{2,1,0:T(8,128)(2,1)S(1)}, u32[]{:S(2)}, u32[]{:S(2)}) async-start(bf16[8,256,128]{2,1,0:T(8,128)(2,1)} %bitcast.16), calls=%async_computation.7 | async-start | bytes 1048576 | tf_op jit(solution)/shard_map/scatter_col/all_to_all | solution.py:170
  185.8 0.1 collective-permute-start.13
  185.9 6.5 %collective-permute-done.13 = f32[264,128]{1,0:T(8,128)S(1)} collective-permute-done((f32[264,128]{1,0:T(8,128)S(1)}, f32[264,128]{1,0:T(8,128)S(1)}, u32[]{:S(2)}, u32[]{:S(2)}) %collective-permute-start.13) | collective-permute-done | bytes 135200 | tf_op jit(solution)/shard_map/weights/ppermute | solution.py:213
  192.4 2.1 collective-permute-start.14
  194.5 2.0 fusion.3
  196.5 8.3 %all-to-all-start.5 = ((bf16[8,256,128]{2,1,0:T(8,128)(2,1)}), bf16[8,256,128]{2,1,0:T(8,128)(2,1)S(1)}, u32[]{:S(2)}, u32[]{:S(2)}) async-start(bf16[8,256,128]{2,1,0:T(8,128)(2,1)} %bitcast.13), calls=%async_computation.5 | async-start | bytes 1048576 | tf_op jit(solution)/shard_map/scatter_row/all_to_all | solution.py:166
  204.8 0.6 collective-permute-start.15
  205.5 6.0 %collective-permute-done.15 = f32[264,128]{1,0:T(8,128)S(1)} collective-permute-done((f32[264,128]{1,0:T(8,128)S(1)}, f32[264,128]{1,0:T(8,128)S(1)}, u32[]{:S(2)}, u32[]{:S(2)}) %collective-permute-start.15) | collective-permute-done | bytes 135200 | tf_op jit(solution)/shard_map/weights/ppermute | solution.py:213
  211.4 1.3 collective-permute-start.16
  212.7 4.6 %collective-permute-done.16 = f32[264,128]{1,0:T(8,128)S(1)} collective-permute-done((f32[264,128]{1,0:T(8,128)S(1)}, f32[264,128]{1,0:T(8,128)S(1)}, u32[]{:S(2)}, u32[]{:S(2)}) %collective-permute-start.16) | collective-permute-done | bytes 135200 | tf_op jit(solution)/shard_map/weights/ppermute | solution.py:213
  217.3 0.1 collective-permute-start.17
  217.4 6.5 %collective-permute-done.17 = f32[264,128]{1,0:T(8,128)S(1)} collective-permute-done((f32[264,128]{1,0:T(8,128)S(1)}, f32[264,128]{1,0:T(8,128)S(1)}, u32[]{:S(2)}, u32[]{:S(2)}) %collective-permute-start.17) | collective-permute-done | bytes 135200 | tf_op jit(solution)/shard_map/weights/ppermute | solution.py:213
  223.9 0.5 slice_reduce_fusion
  224.5 0.7 fusion.14
  225.2 0.1 convert_reduce_fusion.1
  225.3 0.8 fusion.1
  (59 shorter events, 0.4 us)
Async XLA Ops:
  0.6 100.1 %copy-start = (bf16[128,128]{1,0:T(8,128)(2,1)S(1)}, bf16[128,128]{1,0:T(8,128)(2,1)}, u32[]{:S(2)}) copy-start(bf16[128,128]{1,0:T(8,128)(2,1)} %param.17) | copy-start | bytes 98308
  0.6 25.6 %copy-start.12 = (s32[1,1,96]{2,1,0:T(1,128)S(1)}, s32[1,1,96]{2,1,0:T(1,128)}, u32[]{:S(2)}) copy-start(s32[1,1,96]{2,1,0:T(1,128)} %param.13) | copy-start | bytes 1156
  0.7 25.6 %copy-start.13 = (s32[1,1,96]{2,1,0:T(1,128)S(1)}, s32[1,1,96]{2,1,0:T(1,128)}, u32[]{:S(2)}) copy-start(s32[1,1,96]{2,1,0:T(1,128)} %param.12) | copy-start | bytes 1156
  2.4 13.7 %all-to-all-start = ((bf16[8,2,128,128]{3,2,1,0:T(8,128)(2,1)}), bf16[8,2,128,128]{3,2,1,0:T(8,128)(2,1)S(1)}, u32[]{:S(2)}, u32[]{:S(2)}) async-start(bf16[8,2,128,128]{3,2,1,0:T(8,128)(2,1)} %broadcast_in_dim.47), calls=%async_computation | async-start | bytes 1048576 | tf_op jit(solution)/shard_map/gather_col/all_to_all | solution.py:142
  17.0 24.9 %all-to-all-start.2 = ((bf16[8,2,128,128]{3,2,1,0:T(8,128)(2,1)}), bf16[8,2,128,128]{3,2,1,0:T(8,128)(2,1)}, u32[]{:S(2)}, u32[]{:S(2)}) async-start(bf16[8,2,128,128]{3,2,1,0:T(8,128)(2,1)} %broadcast_in_dim.48), calls=%async_computation.2 | async-start | bytes 1048576 | tf_op jit(solution)/shard_map/gather_row/all_to_all | solution.py:142
  32.6 21.2 %collective-permute-start = (bf16[32,128,128]{2,1,0:T(8,128)(2,1)}, bf16[32,128,128]{2,1,0:T(8,128)(2,1)}, u32[]{:S(2)}, u32[]{:S(2)}) collective-permute-start(bf16[32,128,128]{2,1,0:T(8,128)(2,1)} %get-tuple-element.10), channel_id=1, source_target_pairs={{0,8},{8,0},{1,9},{9,1},{2,10},{10,2},{3,11},{11,3},{4,12},{12,4},... | collective-permute-start | bytes 3145736 | tf_op jit(solution)/shard_map/scatter_row/ppermute | solution.py:138
  41.9 11.9 %collective-permute-start.2 = (bf16[16,128,128]{2,1,0:T(8,128)(2,1)}, bf16[16,128,128]{2,1,0:T(8,128)(2,1)S(1)}, u32[]{:S(2)}, u32[]{:S(2)}) collective-permute-start(bf16[16,128,128]{2,1,0:T(8,128)(2,1)} %bitcast.9.g0), channel_id=1, source_target_pairs={{0,16},{16,0},{1,17},{17,1},{2,18},{18,2},{3,19},{19,3},{4,20},{20... | collective-permute-start | bytes 1572872 | tf_op jit(solution)/shard_map/gather_row/ppermute | solution.py:138
  42.8 13.7 %collective-permute-start.3 = (bf16[16,128,128]{2,1,0:T(8,128)(2,1)}, bf16[16,128,128]{2,1,0:T(8,128)(2,1)S(1)}, u32[]{:S(2)}, u32[]{:S(2)}) collective-permute-start(bf16[16,128,128]{2,1,0:T(8,128)(2,1)} %bitcast.9.g0), channel_id=1, source_target_pairs={{0,8},{8,0},{1,9},{9,1},{2,10},{10,2},{3,11},{11,3},{4,12},{12,4},... | collective-permute-start | bytes 1572872 | tf_op jit(solution)/shard_map/gather_row/ppermute | solution.py:138
  53.8 2.7 %collective-permute-start.4 = (bf16[16,128,128]{2,1,0:T(8,128)(2,1)S(1)}, bf16[16,128,128]{2,1,0:T(8,128)(2,1)S(1)}, u32[]{:S(2)}, u32[]{:S(2)}) collective-permute-start(bf16[16,128,128]{2,1,0:T(8,128)(2,1)S(1)} %collective-permute-done.2.g1), channel_id=1, source_target_pairs={{0,8},{8,0},{1,9},{9,1},{2,10},{10,2},{3,11},{11,3},{4,12},{12,4},... | collective-permute-start | bytes 1572872 | tf_op jit(solution)/shard_map/gather_row/ppermute | solution.py:138
  53.8 3.0 %copy-start.1 = (bf16[1,1,96,128,128]{4,3,2,1,0:T(8,128)(2,1)S(1)}, bf16[1,1,96,128,128]{4,3,2,1,0:T(8,128)(2,1)}, u32[]{:S(2)}) copy-start(bf16[1,1,96,128,128]{4,3,2,1,0:T(8,128)(2,1)} %param.11) | copy-start | bytes 9437188
  55.5 1.3 copy-start.5
  55.6 14.5 %collective-permute-start.1 = (bf16[16,128,128]{2,1,0:T(8,128)(2,1)S(1)}, bf16[16,128,128]{2,1,0:T(8,128)(2,1)}, u32[]{:S(2)}, u32[]{:S(2)}) collective-permute-start(bf16[16,128,128]{2,1,0:T(8,128)(2,1)S(1)} %slice.47), channel_id=1, source_target_pairs={{0,16},{16,0},{1,17},{17,1},{2,18},{18,2},{3,19},{19,3},{4,20},{20... | collective-permute-start | bytes 1572872 | tf_op jit(solution)/shard_map/scatter_row/ppermute | solution.py:138
  56.8 13.3 %copy-start.6 = (f32[32,128,128]{2,1,0:T(8,128)S(1)}, f32[32,128,128]{2,1,0:T(8,128)}, u32[]{:S(2)}) copy-start(f32[32,128,128]{2,1,0:T(8,128)} %copy-done.5) | copy-start | bytes 6291460
  61.3 22.7 %copy-start.10 = (s32[256]{0:T(256)S(1)}, s32[256]{0:T(256)}, u32[]{:S(2)}) copy-start(s32[256]{0:T(256)} %param.15) | copy-start | bytes 3076
  61.3 22.7 %copy-start.7 = (bf16[256,128]{1,0:T(8,128)(2,1)S(1)}, bf16[256,128]{1,0:T(8,128)(2,1)}, u32[]{:S(2)}) copy-start(bf16[256,128]{1,0:T(8,128)(2,1)} %param.10) | copy-start | bytes 196612
  61.3 22.7 %copy-start.8 = (bf16[128,128]{1,0:T(8,128)(2,1)S(1)}, bf16[128,128]{1,0:T(8,128)(2,1)}, u32[]{:S(2)}) copy-start(bf16[128,128]{1,0:T(8,128)(2,1)} %param.16) | copy-start | bytes 98308
  61.3 15.2 %all-to-all-start.3 = ((bf16[8,256,128]{2,1,0:T(8,128)(2,1)}), bf16[8,256,128]{2,1,0:T(8,128)(2,1)S(1)}, u32[]{:S(2)}, u32[]{:S(2)}) async-start(bf16[8,256,128]{2,1,0:T(8,128)(2,1)} %bitcast.10), calls=%async_computation.3 | async-start | bytes 1048576 | tf_op jit(solution)/shard_map/scatter_col/all_to_all | solution.py:170
  68.6 32.1 %copy-start.11 = (f32[128]{0:T(128)S(1)}, f32[128]{0:T(128)}, u32[]{:S(2)}) copy-start(f32[128]{0:T(128)} %param.18) | copy-start | bytes 1540
  72.1 29.4 %copy-start.9 = (bf16[256,128]{1,0:T(8,128)(2,1)S(1)}, bf16[256,128]{1,0:T(8,128)(2,1)}, u32[]{:S(2)}) copy-start(bf16[256,128]{1,0:T(8,128)(2,1)} %param.19) | copy-start | bytes 196612
  76.5 24.0 %all-to-all-start.1 = ((bf16[8,256,128]{2,1,0:T(8,128)(2,1)}), bf16[8,256,128]{2,1,0:T(8,128)(2,1)S(1)}, u32[]{:S(2)}, u32[]{:S(2)}) async-start(bf16[8,256,128]{2,1,0:T(8,128)(2,1)} %bitcast.7), calls=%async_computation.1 | async-start | bytes 1048576 | tf_op jit(solution)/shard_map/scatter_row/all_to_all | solution.py:166
  102.7 13.5 %all-to-all-start.4 = ((bf16[8,2,128,128]{3,2,1,0:T(8,128)(2,1)}), bf16[8,2,128,128]{3,2,1,0:T(8,128)(2,1)S(1)}, u32[]{:S(2)}, u32[]{:S(2)}) async-start(bf16[8,2,128,128]{3,2,1,0:T(8,128)(2,1)} %broadcast_in_dim.50), calls=%async_computation.4 | async-start | bytes 1048576 | tf_op jit(solution)/shard_map/gather_col/all_to_all | solution.py:142
  117.1 22.4 %all-to-all-start.6 = ((bf16[8,2,128,128]{3,2,1,0:T(8,128)(2,1)}), bf16[8,2,128,128]{3,2,1,0:T(8,128)(2,1)S(1)}, u32[]{:S(2)}, u32[]{:S(2)}) async-start(bf16[8,2,128,128]{3,2,1,0:T(8,128)(2,1)} %broadcast_in_dim.51), calls=%async_computation.6 | async-start | bytes 1048576 | tf_op jit(solution)/shard_map/gather_row/all_to_all | solution.py:142
  129.2 23.1 %collective-permute-start.5 = (bf16[32,128,128]{2,1,0:T(8,128)(2,1)}, bf16[32,128,128]{2,1,0:T(8,128)(2,1)}, u32[]{:S(2)}, u32[]{:S(2)}) collective-permute-start(bf16[32,128,128]{2,1,0:T(8,128)(2,1)} %get-tuple-element.12), channel_id=1, source_target_pairs={{0,8},{8,0},{1,9},{9,1},{2,10},{10,2},{3,11},{11,3},{4,12},{12,4},... | collective-permute-start | bytes 3145736 | tf_op jit(solution)/shard_map/scatter_row/ppermute | solution.py:138
  139.5 12.8 %collective-permute-start.7 = (bf16[16,128,128]{2,1,0:T(8,128)(2,1)S(1)}, bf16[16,128,128]{2,1,0:T(8,128)(2,1)S(1)}, u32[]{:S(2)}, u32[]{:S(2)}) collective-permute-start(bf16[16,128,128]{2,1,0:T(8,128)(2,1)S(1)} %bitcast.62), channel_id=1, source_target_pairs={{0,16},{16,0},{1,17},{17,1},{2,18},{18,2},{3,19},{19,3},{4,20},{20... | collective-permute-start | bytes 1572872 | tf_op jit(solution)/shard_map/gather_row/ppermute | solution.py:138
  140.2 15.3 %collective-permute-start.10 = (f32[264,128]{1,0:T(8,128)S(1)}, f32[264,128]{1,0:T(8,128)S(1)}, u32[]{:S(2)}, u32[]{:S(2)}) collective-permute-start(f32[264,128]{1,0:T(8,128)S(1)} %pad_maximum_fusion), channel_id=1, source_target_pairs={{0,8},{8,0},{1,9},{9,1},{2,10},{10,2},{3,11},{11,3},{4,12},{12,4},... | collective-permute-start | bytes 405512 | tf_op jit(solution)/shard_map/weights/ppermute | solution.py:213
  140.3 34.8 %collective-permute-start.8 = (bf16[16,128,128]{2,1,0:T(8,128)(2,1)S(1)}, bf16[16,128,128]{2,1,0:T(8,128)(2,1)S(1)}, u32[]{:S(2)}, u32[]{:S(2)}) collective-permute-start(bf16[16,128,128]{2,1,0:T(8,128)(2,1)S(1)} %bitcast.63), channel_id=1, source_target_pairs={{0,8},{8,0},{1,9},{9,1},{2,10},{10,2},{3,11},{11,3},{4,12},{12,4},... | collective-permute-start | bytes 1572872 | tf_op jit(solution)/shard_map/gather_row/ppermute | solution.py:138
  152.3 22.9 %collective-permute-start.9 = (bf16[16,128,128]{2,1,0:T(8,128)(2,1)S(1)}, bf16[16,128,128]{2,1,0:T(8,128)(2,1)S(1)}, u32[]{:S(2)}, u32[]{:S(2)}) collective-permute-start(bf16[16,128,128]{2,1,0:T(8,128)(2,1)S(1)} %collective-permute-done.7.g1), channel_id=1, source_target_pairs={{0,8},{8,0},{1,9},{9,1},{2,10},{10,2},{3,11},{11,3},{4,12},{12,4},... | collective-permute-start | bytes 1572872 | tf_op jit(solution)/shard_map/gather_row/ppermute | solution.py:138
  152.3 22.9 %copy-start.2 = (bf16[1,1,96,128,128]{4,3,2,1,0:T(8,128)(2,1)S(1)}, bf16[1,1,96,128,128]{4,3,2,1,0:T(8,128)(2,1)}, u32[]{:S(2)}) copy-start(bf16[1,1,96,128,128]{4,3,2,1,0:T(8,128)(2,1)} %param.11) | copy-start | bytes 9437188
  154.0 21.2 %copy-start.3 = (f32[32,128,128]{2,1,0:T(8,128)}, f32[32,128,128]{2,1,0:T(8,128)S(1)}, u32[]{:S(2)}) copy-start(f32[32,128,128]{2,1,0:T(8,128)S(1)} %convert_add_fusion) | copy-start | bytes 6291460
  155.0 39.5 %collective-permute-start.6 = (bf16[16,128,128]{2,1,0:T(8,128)(2,1)}, bf16[16,128,128]{2,1,0:T(8,128)(2,1)}, u32[]{:S(2)}, u32[]{:S(2)}) collective-permute-start(bf16[16,128,128]{2,1,0:T(8,128)(2,1)} %slice.46), channel_id=1, source_target_pairs={{0,16},{16,0},{1,17},{17,1},{2,18},{18,2},{3,19},{19,3},{4,20},{20... | collective-permute-start | bytes 1572872 | tf_op jit(solution)/shard_map/scatter_row/ppermute | solution.py:138
  155.5 16.9 %collective-permute-start.11 = (f32[264,128]{1,0:T(8,128)S(1)}, f32[264,128]{1,0:T(8,128)S(1)}, u32[]{:S(2)}, u32[]{:S(2)}) collective-permute-start(f32[264,128]{1,0:T(8,128)S(1)} %fusion.13), channel_id=1, source_target_pairs={{0,16},{16,0},{1,17},{17,1},{2,18},{18,2},{3,19},{19,3},{4,20},{20... | collective-permute-start | bytes 405512 | tf_op jit(solution)/shard_map/weights/ppermute | solution.py:213
  172.4 13.3 %collective-permute-start.12 = (f32[264,128]{1,0:T(8,128)S(1)}, f32[264,128]{1,0:T(8,128)S(1)}, u32[]{:S(2)}, u32[]{:S(2)}) collective-permute-start(f32[264,128]{1,0:T(8,128)S(1)} %add.99), channel_id=1, source_target_pairs={{0,32},{32,0},{64,96},{96,64},{128,160},{160,128},{192,224},{224,1... | collective-permute-start | bytes 405512 | tf_op jit(solution)/shard_map/weights/ppermute | solution.py:213
  175.2 19.3 %copy-start.4 = (f32[32,128,128]{2,1,0:T(8,128)S(1)}, f32[32,128,128]{2,1,0:T(8,128)}, u32[]{:S(2)}) copy-start(f32[32,128,128]{2,1,0:T(8,128)} %copy-done.3) | copy-start | bytes 6291460
  178.5 18.0 %all-to-all-start.7 = ((bf16[8,256,128]{2,1,0:T(8,128)(2,1)}), bf16[8,256,128]{2,1,0:T(8,128)(2,1)S(1)}, u32[]{:S(2)}, u32[]{:S(2)}) async-start(bf16[8,256,128]{2,1,0:T(8,128)(2,1)} %bitcast.16), calls=%async_computation.7 | async-start | bytes 1048576 | tf_op jit(solution)/shard_map/scatter_col/all_to_all | solution.py:170
  185.8 6.6 %collective-permute-start.13 = (f32[264,128]{1,0:T(8,128)S(1)}, f32[264,128]{1,0:T(8,128)S(1)}, u32[]{:S(2)}, u32[]{:S(2)}) collective-permute-start(f32[264,128]{1,0:T(8,128)S(1)} %add.100), channel_id=1, source_target_pairs={{0,64},{32,96},{64,0},{96,32},{128,192},{160,224},{192,128},{224,1... | collective-permute-start | bytes 405512 | tf_op jit(solution)/shard_map/weights/ppermute | solution.py:213
  192.4 12.4 %collective-permute-start.14 = (f32[264,128]{1,0:T(8,128)S(1)}, f32[264,128]{1,0:T(8,128)S(1)}, u32[]{:S(2)}, u32[]{:S(2)}) collective-permute-start(f32[264,128]{1,0:T(8,128)S(1)} %add.101), channel_id=1, source_target_pairs={{0,128},{32,160},{64,192},{96,224},{128,0},{160,32},{192,64},{224,... | collective-permute-start | bytes 405512 | tf_op jit(solution)/shard_map/weights/ppermute | solution.py:213
  196.5 28.7 %all-to-all-start.5 = ((bf16[8,256,128]{2,1,0:T(8,128)(2,1)}), bf16[8,256,128]{2,1,0:T(8,128)(2,1)S(1)}, u32[]{:S(2)}, u32[]{:S(2)}) async-start(bf16[8,256,128]{2,1,0:T(8,128)(2,1)} %bitcast.13), calls=%async_computation.5 | async-start | bytes 1048576 | tf_op jit(solution)/shard_map/scatter_row/all_to_all | solution.py:166
  204.8 6.6 %collective-permute-start.15 = (f32[264,128]{1,0:T(8,128)S(1)}, f32[264,128]{1,0:T(8,128)S(1)}, u32[]{:S(2)}, u32[]{:S(2)}) collective-permute-start(f32[264,128]{1,0:T(8,128)S(1)} %add.102), channel_id=1, source_target_pairs={{0,4},{4,0},{1,5},{5,1},{2,6},{6,2},{3,7},{7,3},{8,12},{12,8},{9,1... | collective-permute-start | bytes 405512 | tf_op jit(solution)/shard_map/weights/ppermute | solution.py:213
  211.4 5.8 %collective-permute-start.16 = (f32[264,128]{1,0:T(8,128)S(1)}, f32[264,128]{1,0:T(8,128)S(1)}, u32[]{:S(2)}, u32[]{:S(2)}) collective-permute-start(f32[264,128]{1,0:T(8,128)S(1)} %add.103), channel_id=1, source_target_pairs={{0,1},{1,0},{2,3},{3,2},{4,5},{5,4},{6,7},{7,6},{8,9},{9,8},{10,11... | collective-permute-start | bytes 405512 | tf_op jit(solution)/shard_map/weights/ppermute | solution.py:213
  217.3 6.6 %collective-permute-start.17 = (f32[264,128]{1,0:T(8,128)S(1)}, f32[264,128]{1,0:T(8,128)S(1)}, u32[]{:S(2)}, u32[]{:S(2)}) collective-permute-start(f32[264,128]{1,0:T(8,128)S(1)} %add.104), channel_id=1, source_target_pairs={{0,2},{1,3},{2,0},{3,1},{4,6},{5,7},{6,4},{7,5},{8,10},{9,11},{10,... | collective-permute-start | bytes 405512 | tf_op jit(solution)/shard_map/weights/ppermute | solution.py:213

commit v2 on v0

v2 whole, which is shorter than its diff:
```python
import jax
import jax.numpy as jnp
from jax import lax
from jax.experimental import pallas as pl
from jax.experimental.pallas import tpu as pltpu
from jax.sharding import Mesh
from jax.sharding import PartitionSpec as P

TILE = 128
UNROLL = 8
GROUP = 16
ROW = ("z", "xl", "co")
COL = ("xh", "y")
HALF_SCALE = 2.0
VMEM_LIMIT = 16 * 1024 * 1024


def whole(shape):
    return pl.BlockSpec(shape, lambda *_: (0,) * len(shape))


def multiply(tiles_hbm, tiles_ref, sems, count_ref, acc_ref, ids_ref, prepare, product):
    count = count_ref[0]
    groups = tiles_ref.shape[0] // GROUP

    def chunk(i):
        part = pl.ds(i * GROUP, GROUP)
        return pltpu.make_async_copy(tiles_hbm.at[part], tiles_ref.at[part], sems.at[i])

    for i in range(groups):
        chunk(i).start()
    prepare()
    acc_ref[...] = jnp.zeros_like(acc_ref)

    def step(k, carry):
        base = k * UNROLL
        outs = [product(base + u) for u in range(UNROLL)]
        for u in range(UNROLL):
            acc_ref[ids_ref[base + u]] += outs[u]
        return carry

    last = (count + UNROLL - 1) // UNROLL
    per = GROUP // UNROLL
    for i in range(groups):
        chunk(i).wait()
        lax.fori_loop(jnp.minimum(i * per, last), jnp.minimum((i + 1) * per, last), step, 0)


def ahead_kernel(src_ref, slot_ref, count_ref, f0, f1, f2, f3, tiles_hbm,
                 keep_ref, send_ref, field_ref, acc_ref, tiles_ref, sems):
    def prepare():
        for k, f in enumerate((f0, f1, f2, f3)):
            for h in range(2):
                field_ref[k * 4 + h * 2 : k * 4 + h * 2 + 2] = f[h]
        field_ref[16] = jnp.zeros_like(field_ref[16])

    def product(t):
        return jnp.dot(tiles_ref[t], field_ref[src_ref[t]], preferred_element_type=jnp.float32)

    multiply(tiles_hbm, tiles_ref, sems, count_ref, acc_ref, slot_ref, prepare, product)
    send_ref[...] = acc_ref[32:64].astype(send_ref.dtype)
    keep_ref[...] = acc_ref[:32]


def behind_kernel(src_ref, slot_ref, count_ref, g0, g1, tiles_hbm,
                  keep_ref, s1, s2, s3, field_ref, acc_ref, tiles_ref, sems):
    n = g0.shape[0]

    def prepare():
        field_ref[:n] = g0[...]
        field_ref[n : 2 * n] = g1[...]
        field_ref[2 * n] = jnp.zeros_like(field_ref[2 * n])

    def product(t):
        return jnp.dot(field_ref[slot_ref[t]], tiles_ref[t], preferred_element_type=jnp.float32)

    multiply(tiles_hbm, tiles_ref, sems, count_ref, acc_ref, src_ref, prepare, product)
    for p, ref in enumerate((keep_ref, s1, s2, s3)):
        for k in range(4):
            ref[k] = acc_ref[p * 4 + k].T.astype(ref.dtype)


def products(kernel, parts, tiles, src, slot, count, nfield, nacc, outs, name):
    n = tiles.shape[0]
    return pl.pallas_call(
        kernel,
        in_specs=[pl.BlockSpec(memory_space=pltpu.SMEM)] * 3
        + [pl.BlockSpec(memory_space=pltpu.VMEM)] * len(parts)
        + [pl.BlockSpec(memory_space=pltpu.HBM)],
        out_specs=[pl.BlockSpec(memory_space=pltpu.VMEM) for _ in outs],
        out_shape=[jax.ShapeDtypeStruct((k, TILE, TILE), dtype) for k, dtype in outs],
        scratch_shapes=[
            pltpu.VMEM((nfield + 1, TILE, TILE), jnp.bfloat16),
            pltpu.VMEM((nacc + 1, TILE, TILE), jnp.float32),
            pltpu.VMEM((n, TILE, TILE), tiles.dtype),
            pltpu.SemaphoreType.DMA((n // GROUP,)),
        ],
        compiler_params=pltpu.CompilerParams(vmem_limit_bytes=VMEM_LIMIT),
        cost_estimate=pl.CostEstimate(
            flops=16 * n * TILE**3, bytes_accessed=n * TILE * TILE * 2, transcendentals=0
        ),
        name=name,
    )(src, slot, count, *parts, pltpu.with_memory_space_constraint(tiles, pltpu.HBM))


def flip(x, axis, d=1):
    n = lax.axis_size(axis)
    return lax.ppermute(x, axis, [(i, i ^ d) for i in range(n)])


def tie(*xs):
    return lax.optimization_barrier(xs)


def pack(x, exact):
    return (x * HALF_SCALE).astype(jnp.float16) if exact else x.astype(jnp.bfloat16)


def unpack(x):
    wide = x.astype(jnp.float32)
    return wide * (1.0 / HALF_SCALE) if x.dtype == jnp.float16 else wide


def aggregate(field, copies, tiles, src, slot, count, exact, side):
    with jax.named_scope("gather_row"):
        g0 = lax.all_to_all(copies, ("z", "xl"), 0, 0, tiled=True).reshape(-1, TILE, TILE)
    with jax.named_scope("gather_col"):
        (other,) = side(0, flip(field, "xh"))
        pair = jnp.stack([field, other])
        cols = side(1, pair, *(flip(pair, "y", k) for k in (1, 2, 3)))
    with jax.named_scope("ahead"):
        keep, send = products(
            ahead_kernel, cols, tiles, src, slot, count, 16, 64, ((32, jnp.float32), (32, jnp.bfloat16)), "ahead"
        )
        keep, send = side(2, keep, send)
    with jax.named_scope("scatter_row"):
        both = pack(keep + flip(send, "co").astype(jnp.float32), exact)
    g0, both = tie(*side(3, g0), both)
    with jax.named_scope("scatter_row"):
        first = lax.all_to_all(both.reshape(16, -1, TILE), ("z", "xl"), 0, 0, tiled=True)
    with jax.named_scope("gather_row"):
        (g1,) = side(4, flip(g0, "co"))
    with jax.named_scope("behind"):
        back, *sends = products(
            behind_kernel, (g0, g1), tiles, src, slot, count, 64, 16, ((4, jnp.float32),) + ((4, jnp.bfloat16),) * 3, "behind"
        )
        back, *sends = side(5, back, *sends)
    with jax.named_scope("scatter_col"):
        for k in (1, 2, 3):
            back = back + flip(sends[k - 1], "y", k).astype(jnp.float32)
        (back,) = side(6, back)
        last = flip(pack(back[2:], exact), "xh")
    (last,) = side(7, last)
    return first, back[:2].reshape(-1, TILE), last.reshape(-1, TILE)


def total(first, back, last):
    return jnp.sum(unpack(first), axis=0) + back + unpack(last)


def prepare_kernel(features_ref, copies_ref):
    for h in range(2):
        block = features_ref[h * TILE : (h + 1) * TILE].astype(jnp.float32).T.astype(jnp.bfloat16)
        for k in range(copies_ref.shape[0]):
            copies_ref[k, h] = block


def prepare(features):
    return pl.pallas_call(
        prepare_kernel,
        out_shape=jax.ShapeDtypeStruct((16, 2, TILE, TILE), jnp.bfloat16),
        compiler_params=pltpu.CompilerParams(vmem_limit_bytes=VMEM_LIMIT),
        name="prepare",
    )(features)


def middle_kernel(summed_ref, inverse_ref, features_ref, upstream_ref, w_self_ref, w_neigh_ref, bias_ref,
                  hidden_ref, scaled_ref, copies_ref, base_ref, local_ref):
    def dot(a, b, dims):
        return lax.dot_general(a, b, (dims, ((), ())), preferred_element_type=jnp.float32)

    features = features_ref[...]
    inverse = inverse_ref[...]
    w_self, w_neigh = w_self_ref[...], w_neigh_ref[...]
    agg = (summed_ref[...] * inverse).astype(jnp.bfloat16)
    pre = dot(features, w_self, ((1,), (0,))) + dot(agg, w_neigh, ((1,), (0,))) + bias_ref[...]
    hidden_ref[...] = jnp.maximum(pre, 0.0).astype(jnp.bfloat16)
    wide = jnp.where(pre > 0, upstream_ref[...].astype(jnp.float32), 0.0)
    dpre = wide.astype(jnp.bfloat16)
    scaled = (dot(dpre, w_neigh, ((1,), (1,))) * inverse).astype(jnp.bfloat16)
    scaled_ref[...] = scaled
    for h in range(2):
        block = scaled[h * TILE : (h + 1) * TILE].astype(jnp.float32).T.astype(jnp.bfloat16)
        for k in range(copies_ref.shape[0]):
            copies_ref[k, h] = block
    base_ref[...] = dot(dpre, w_self, ((1,), (1,)))
    local_ref[0, :TILE] = dot(features, dpre, ((0,), (0,)))
    local_ref[1, :TILE] = dot(agg, dpre, ((0,), (0,)))
    wide = wide.reshape(-1, 8, TILE)
    for h in range(2):
        local_ref[h, TILE:] = jnp.sum(wide, axis=0)


def middle(summed, inverse, features, upstream, w_self, w_neigh, bias):
    nodes = features.shape
    return pl.pallas_call(
        middle_kernel,
        out_shape=[
            jax.ShapeDtypeStruct(nodes, jnp.bfloat16),
            jax.ShapeDtypeStruct(nodes, jnp.bfloat16),
            jax.ShapeDtypeStruct((16, 2, TILE, TILE), jnp.bfloat16),
            jax.ShapeDtypeStruct(nodes, jnp.float32),
            jax.ShapeDtypeStruct((2, TILE + 8, TILE), jnp.float32),
        ],
        compiler_params=pltpu.CompilerParams(vmem_limit_bytes=VMEM_LIMIT),
        name="middle",
    )(summed, inverse, features, upstream, w_self, w_neigh, bias)


def final_kernel(co_ref, first_ref, back_ref, last_ref, base_ref, w_ref, grad_ref, self_ref, neigh_ref, bias_ref):
    carried = total(first_ref[...], back_ref[...], last_ref[...])
    grad_ref[...] = (base_ref[...] + carried).astype(grad_ref.dtype)
    co = co_ref[0]
    self_ref[...] = w_ref[co, :TILE]
    neigh_ref[...] = w_ref[1 - co, :TILE]
    bias_ref[...] = jnp.sum(w_ref[0, TILE:], axis=0, keepdims=True)


def final(co, first, back, last, base, weights):
    shapes = ((base.shape, jnp.bfloat16), ((TILE, TILE), jnp.float32), ((TILE, TILE), jnp.float32), ((1, TILE), jnp.float32))
    args = (first, back, last, base, weights)
    return pl.pallas_call(
        final_kernel,
        grid_spec=pltpu.PrefetchScalarGridSpec(
            num_scalar_prefetch=1,
            grid=(1,),
            in_specs=[whole(x.shape) for x in args],
            out_specs=[whole(x) for x, _ in shapes],
        ),
        out_shape=[jax.ShapeDtypeStruct(x, dtype) for x, dtype in shapes],
        compiler_params=pltpu.CompilerParams(vmem_limit_bytes=VMEM_LIMIT),
        name="final",
    )(co, *args)


STEPS = ((("co", 1),), (), (), (("z", 1, 2, 3),), (("xl", 1),), (("xh", 1),), (("y", 1, 2, 3),), (("z", 4),))


def body(features, tiles, tile_src, tile_dst, tile_count, degree, w_self, w_neigh, bias, upstream):
    held = tiles[0, 0]
    count = tile_count[0]
    co, xl, xh, y = (lax.axis_index(a) for a in ("co", "xl", "xh", "y"))
    live = jnp.arange(held.shape[0], dtype=jnp.int32) < count[0]
    src, dst = tile_src[0, 0], tile_dst[0, 0]
    src = ((((src // 2) % 4) ^ y) * 2 + ((src // 8) ^ xh)) * 2 + src % 2
    src = jnp.where(live, src, 16)
    other = ((dst // 2) % 2) ^ co
    slot = other * 32 + (dst // 4) * 2 + dst % 2
    slot = jnp.where(live, slot, 64)
    inverse = jnp.broadcast_to(1.0 / degree.astype(jnp.float32)[:, None], features.shape)

    blocks = features.reshape(-1, TILE, TILE)
    parts = aggregate(blocks, prepare(features), held, src, slot, count, True, lambda k, *xs: xs)
    hidden, scaled, copies, base, local = middle(
        total(*parts), inverse, features, upstream, w_self, w_neigh, bias.reshape(1, -1)
    )

    weights = [local]

    def side(k, *xs):
        with jax.named_scope("weights"):
            w = weights[0]
            if k == 0:
                mine = lax.dynamic_index_in_dim(w, co, 0, keepdims=False)
                w = mine + flip(lax.dynamic_index_in_dim(w, 1 - co, 0, keepdims=False), "co")
            else:
                for axis, *hops in STEPS[k]:
                    w = sum((flip(w, axis, d) for d in hops), w)
            *xs, weights[0] = tie(*xs, w)
        return xs

    parts = aggregate(scaled.reshape(-1, TILE, TILE), copies, held, src, slot, count, False, side)
    with jax.named_scope("weights"):
        pair = jnp.stack([weights[0], flip(weights[0], "co")])
    grad_features, grad_self, grad_neigh, grad_bias = final(co.reshape(1), *parts, base, pair)
    return hidden, grad_features, grad_self, grad_neigh, grad_bias[0]


def solution(mesh):
    fine = Mesh(mesh.devices.reshape(8, 2, 2, 2, 4), ROW + COL)
    nodes = P(ROW + COL, None)
    return jax.shard_map(
        body,
        mesh=fine,
        in_specs=(
            nodes,
            P(ROW, COL, None, None, None),
            P(ROW, COL, None),
            P(ROW, COL, None),
            P(ROW, COL),
            P(ROW + COL),
            P(),
            P(),
            P(),
            nodes,
        ),
        out_specs=(nodes, nodes, P(), P(), P()),
        check_vma=False,
    )
```

time: 856 us -> 164 us (0.19)
  waiting for transfers between devices: 506 us -> 60.9 us
  blocking collectives: 142 us -> 0 us
  other arithmetic: 90.9 us -> 3.19 us
  starting transfers between devices: 0.29 us -> 82.9 us
  local copies, waits for them, and re-layouts: 67.6 us -> 1.03 us
  matrix products: 30.4 us -> 0 us
  Pallas kernels: 0 us -> 14.2 us
  between operations: 15 us -> 1.6 us
    reduce_scatter x4 -> x0, waiting for transfers between devices: 322 us -> none  [the longest x2 247 us: target_side(): lax.psum_scatter(part.reshape(ndst * TILE, fdim), 'row', scatter_dimensio...]
    all_gather x2 -> x0, waiting for transfers between devices: 135 us -> none  [source_side(): gathered = lax.all_gather(field, 'row', axis=0, tiled=True)]
    scatter-add x4 -> x0, other arithmetic: 88.3 us -> none  [the longest x2 45.2 us: target_side(): jax.ops.segment_sum(ahead, jnp.where(live, dst_ids, ndst), ndst + 1)[:ndst]]
    psum x1 -> x0, blocking collectives: 79.5 us -> none  [body(): lax.psum((local_self, local_neigh, local_bias), ('row', 'col'))]
    all_gather x2 -> x0, blocking collectives: 62.1 us -> none  [target_side(): gathered = lax.all_gather(field, 'col', axis=0, tiled=True)]
    ppermute x0 -> x31, starting transfers between devices: none -> 60.8 us  [flip(): return lax.ppermute(x, axis, [(i, i ^ d) for i in range(n)])]
    ppermute x0 -> x31, waiting for transfers between devices: none -> 54.6 us  [flip(): return lax.ppermute(x, axis, [(i, i ^ d) for i in range(n)])]
    psum x1 -> x0, waiting for transfers between devices: 48 us -> none  [body(): lax.psum((local_self, local_neigh, local_bias), ('row', 'col'))]
  transfers between devices with their start and end apart: 7 -> 35, of which waited for: 6 -> 21; matrix products, arithmetic and copies ran while one was open for 16% -> 2% of each run, Pallas kernels for 0% -> 7%
where the time goes in v2:
time: 164 us
  starting transfers between devices  82.9 us (51%)
  waiting for transfers between devices  60.9 us (37%)
  Pallas kernels  14.2 us (9%)
  other arithmetic  3.19 us (2%)
    ppermute x31, starting transfers between devices, flip(): return lax.ppermute(x, axis, [(i, i ^ d) for i in range(n)])  60.8 us
    ppermute x31, waiting for transfers between devices, flip(): return lax.ppermute(x, axis, [(i, i ^ d) for i in range(n)])  54.6 us
    all_to_all x2, starting transfers between devices, aggregate(): lax.all_to_all(copies, ('z', 'xl'), 0, 0, tiled=True)  12.9 us
    pallas_call x4, Pallas kernels, products(): pl.pallas_call(kernel, in_specs=[pl.BlockSpec(memory_space=pltpu.SMEM)] *...  10.7 us
    all_to_all x2, starting transfers between devices, aggregate(): lax.all_to_all(both.reshape(16, -1, TILE), ('z', 'xl'), 0, 0, tiled=True)  9.2 us
    all_to_all x2, waiting for transfers between devices, aggregate(): lax.all_to_all(copies, ('z', 'xl'), 0, 0, tiled=True)  6.28 us
  transfers between devices with their start and end apart: 35, of which 21 were waited for; matrix products, arithmetic and copies ran while one was open for 2% of the time, Pallas kernels for 7%

profile of v2, /device:TPU:1, one launch (start us, length us, event | category | flops | bytes accessed | tf_op | source)
XLA Modules:
  0.0 163.8 jit_solution(1335800047858156715)
XLA Ops:
  0.7 3.7 %collective-permute-start = (bf16[2,128,128]{2,1,0:T(8,128)(2,1)}, bf16[2,128,128]{2,1,0:T(8,128)(2,1)S(1)}, u32[]{:S(2)}, u32[]{:S(2)}) collective-permute-start(bf16[2,128,128]{2,1,0:T(8,128)(2,1)} %bitcast.75), channel_id=1, source_target_pairs={{0,4},{4,0},{1,5},{5,1},{2,6},{6,2},{3,7},{7,3},{8,12},{12,8},{9,1... | collective-permute-start | bytes 196616 | tf_op jit(solution)/shard_map/gather_col/ppermute | solution.py:108
  4.3 0.9 copy-done
  5.2 1.2 prepare.1
  6.4 8.3 %all-to-all-start = ((bf16[16,2,128,128]{3,2,1,0:T(8,128)(2,1)}), bf16[16,2,128,128]{3,2,1,0:T(8,128)(2,1)S(1)}, u32[]{:S(2)}, u32[]{:S(2)}) async-start(bf16[16,2,128,128]{3,2,1,0:T(8,128)(2,1)} %prepare.1), calls=%async_computation | async-start | bytes 2097152 | tf_op jit(solution)/shard_map/gather_row/all_to_all | solution.py:126
  15.4 2.8 %collective-permute-start.3 = (bf16[2,2,128,128]{3,2,1,0:T(8,128)(2,1)S(1)}, bf16[2,2,128,128]{3,2,1,0:T(8,128)(2,1)S(1)}, u32[]{:S(2)}, u32[]{:S(2)}) collective-permute-start(bf16[2,2,128,128]{3,2,1,0:T(8,128)(2,1)S(1)} %pad_maximum_fusion.1.f0), channel_id=1, source_target_pairs={{0,3},{1,2},{2,1},{3,0},{4,7},{5,6},{6,5},{7,4},{8,11},{9,10},{10,... | collective-permute-start | bytes 393224 | tf_op jit(solution)/shard_map/gather_col/ppermute | solution.py:108
  18.2 0.3 collective-permute-start.2
  18.6 0.3 collective-permute-start.1
  18.9 4.7 %collective-permute-done.3.f3 = bf16[2,2,128,128]{3,2,1,0:T(8,128)(2,1)S(1)} collective-permute-done((bf16[2,2,128,128]{3,2,1,0:T(8,128)(2,1)S(1)}, bf16[2,2,128,128]{3,2,1,0:T(8,128)(2,1)S(1)}, u32[]{:S(2)}, u32[]{:S(2)}) %collective-permute-start.3) | collective-permute-done | bytes 131104 | tf_op jit(solution)/shard_map/gather_col/ppermute | solution.py:108
  23.6 0.2 collective-permute-done.2.f2
  23.9 0.1 collective-permute-done.1.f1
  24.0 2.7 %ahead.2 = (f32[32,128,128]{2,1,0:T(8,128)S(1)}, bf16[32,128,128]{2,1,0:T(8,128)(2,1)S(1)}) custom-call(s32[96]{0:T(128)S(1)} %get-tuple-element.104.src_ref, s32[96]{0:T(128)S(1)} %get-tuple-element.103.slot_ref, s32[1]{0:T(128)} %bitcast.67.count_ref, bf16[2,2,128,128]{3,2,1,0:T(8,128)(2,1)S(1)} %pad_maximum_fusion.1.f0, ...), custom_call_target="tpu_custom_call" | custom-call | flops 3221225472 | bytes 3145728 | tf_op jit(solution)/shard_map/ahead/ahead/pallas_call | solution.py:85
  26.6 3.2 %collective-permute-start.4 = (bf16[32,128,128]{2,1,0:T(8,128)(2,1)S(1)}, bf16[32,128,128]{2,1,0:T(8,128)(2,1)S(1)}, u32[]{:S(2)}, u32[]{:S(2)}) collective-permute-start(bf16[32,128,128]{2,1,0:T(8,128)(2,1)S(1)} %get-tuple-element.54), channel_id=1, source_target_pairs={{0,8},{8,0},{1,9},{9,1},{2,10},{10,2},{3,11},{11,3},{4,12},{12,4},... | collective-permute-start | bytes 3145736 | tf_op jit(solution)/shard_map/scatter_row/ppermute | solution.py:108
  29.8 2.3 %collective-permute-done.4 = bf16[32,128,128]{2,1,0:T(8,128)(2,1)S(1)} collective-permute-done((bf16[32,128,128]{2,1,0:T(8,128)(2,1)S(1)}, bf16[32,128,128]{2,1,0:T(8,128)(2,1)S(1)}, u32[]{:S(2)}, u32[]{:S(2)}) %collective-permute-start.4) | collective-permute-done | bytes 1048608 | tf_op jit(solution)/shard_map/scatter_row/ppermute | solution.py:108
  32.1 1.4 multiply_convert_fusion
  33.5 6.3 %all-to-all-done = bf16[16,2,128,128]{3,2,1,0:T(8,128)(2,1)S(1)} async-done(((bf16[16,2,128,128]{3,2,1,0:T(8,128)(2,1)}), bf16[16,2,128,128]{3,2,1,0:T(8,128)(2,1)S(1)}, u32[]{:S(2)}, u32[]{:S(2)}) %all-to-all-start) | async-done | bytes 1048608 | tf_op jit(solution)/shard_map/gather_row/all_to_all | solution.py:126
  39.7 4.3 %collective-permute-start.5 = (bf16[32,128,128]{2,1,0:T(8,128)(2,1)S(1)}, bf16[32,128,128]{2,1,0:T(8,128)(2,1)S(1)}, u32[]{:S(2)}, u32[]{:S(2)}) collective-permute-start(bf16[32,128,128]{2,1,0:T(8,128)(2,1)S(1)} %bitcast.73), channel_id=1, source_target_pairs={{0,8},{8,0},{1,9},{9,1},{2,10},{10,2},{3,11},{11,3},{4,12},{12,4},... | collective-permute-start | bytes 3145736 | tf_op jit(solution)/shard_map/gather_row/ppermute | solution.py:108
  44.0 3.7 %all-to-all-start.1 = ((f16[16,256,128]{2,1,0:T(8,128)(2,1)}), f16[16,256,128]{2,1,0:T(8,128)(2,1)S(1)}, u32[]{:S(2)}, u32[]{:S(2)}) async-start(f16[16,256,128]{2,1,0:T(8,128)(2,1)} %bitcast.83), calls=%async_computation.1 | async-start | bytes 2097152 | tf_op jit(solution)/shard_map/scatter_row/all_to_all | solution.py:140
  47.7 2.7 %behind.2 = (f32[4,128,128]{2,1,0:T(8,128)S(1)}, bf16[4,128,128]{2,1,0:T(8,128)(2,1)S(1)}, bf16[4,128,128]{2,1,0:T(8,128)(2,1)S(1)}, bf16[4,128,128]{2,1,0:T(8,128)(2,1)S(1)}) custom-call(s32[96]{0:T(128)S(1)} %get-tuple-element.104.src_ref, s32[96]{0:T(128)S(1)} %get-tuple-element.103.slot_ref, s32[1]{0:T(128)} %bitcast.68.count_ref, ...), custom_call_target="tpu_custom_call" | custom-call | flops 3221225472 | bytes 3145728 | tf_op jit(solution)/shard_map/behind/behind/pallas_call | solution.py:85
  50.4 2.4 %collective-permute-start.6 = (bf16[4,128,128]{2,1,0:T(8,128)(2,1)S(1)}, bf16[4,128,128]{2,1,0:T(8,128)(2,1)S(1)}, u32[]{:S(2)}, u32[]{:S(2)}) collective-permute-start(bf16[4,128,128]{2,1,0:T(8,128)(2,1)S(1)} %get-tuple-element.58), channel_id=1, source_target_pairs={{0,1},{1,0},{2,3},{3,2},{4,5},{5,4},{6,7},{7,6},{8,9},{9,8},{10,11... | collective-permute-start | bytes 393224 | tf_op jit(solution)/shard_map/scatter_col/ppermute | solution.py:108
  52.9 2.2 %collective-permute-start.7 = (bf16[4,128,128]{2,1,0:T(8,128)(2,1)S(1)}, bf16[4,128,128]{2,1,0:T(8,128)(2,1)S(1)}, u32[]{:S(2)}, u32[]{:S(2)}) collective-permute-start(bf16[4,128,128]{2,1,0:T(8,128)(2,1)S(1)} %get-tuple-element.59), channel_id=1, source_target_pairs={{0,2},{1,3},{2,0},{3,1},{4,6},{5,7},{6,4},{7,5},{8,10},{9,11},{10,... | collective-permute-start | bytes 393224 | tf_op jit(solution)/shard_map/scatter_col/ppermute | solution.py:108
  55.0 0.3 collective-permute-start.8
  55.3 1.1 collective-permute-done.6
  56.5 5.3 %collective-permute-done.7 = bf16[4,128,128]{2,1,0:T(8,128)(2,1)S(1)} collective-permute-done((bf16[4,128,128]{2,1,0:T(8,128)(2,1)S(1)}, bf16[4,128,128]{2,1,0:T(8,128)(2,1)S(1)}, u32[]{:S(2)}, u32[]{:S(2)}) %collective-permute-start.7) | collective-permute-done | bytes 131104 | tf_op jit(solution)/shard_map/scatter_col/ppermute | solution.py:108
  61.8 2.6 %collective-permute-done.8 = bf16[4,128,128]{2,1,0:T(8,128)(2,1)S(1)} collective-permute-done((bf16[4,128,128]{2,1,0:T(8,128)(2,1)S(1)}, bf16[4,128,128]{2,1,0:T(8,128)(2,1)S(1)}, u32[]{:S(2)}, u32[]{:S(2)}) %collective-permute-start.8) | collective-permute-done | bytes 131104 | tf_op jit(solution)/shard_map/scatter_col/ppermute | solution.py:108
  64.5 1.9 %collective-permute-start.9 = (f16[2,128,128]{2,1,0:T(8,128)(2,1)S(1)}, f16[2,128,128]{2,1,0:T(8,128)(2,1)S(1)}, u32[]{:S(2)}, u32[]{:S(2)}) collective-permute-start(f16[2,128,128]{2,1,0:T(8,128)(2,1)S(1)} %get-tuple-element.102), channel_id=1, source_target_pairs={{0,4},{4,0},{1,5},{5,1},{2,6},{6,2},{3,7},{7,3},{8,12},{12,8},{9,1... | collective-permute-start | bytes 196616 | tf_op jit(solution)/shard_map/scatter_col/ppermute | solution.py:108
  66.4 9.4 %collective-permute-done.9 = f16[2,128,128]{2,1,0:T(8,128)(2,1)S(1)} collective-permute-done((f16[2,128,128]{2,1,0:T(8,128)(2,1)S(1)}, f16[2,128,128]{2,1,0:T(8,128)(2,1)S(1)}, u32[]{:S(2)}, u32[]{:S(2)}) %collective-permute-start.9) | collective-permute-done | bytes 65568 | tf_op jit(solution)/shard_map/scatter_col/ppermute | solution.py:108
  75.8 0.2 multiply_reduce_fusion
  76.2 1.5 middle.1
  77.7 1.2 collective-permute-start.11
  78.9 4.6 %all-to-all-start.2 = ((bf16[16,2,128,128]{3,2,1,0:T(8,128)(2,1)}), bf16[16,2,128,128]{3,2,1,0:T(8,128)(2,1)S(1)}, u32[]{:S(2)}, u32[]{:S(2)}) async-start(bf16[16,2,128,128]{3,2,1,0:T(8,128)(2,1)} %get-tuple-element.62), calls=%async_computation.2 | async-start | bytes 2097152 | tf_op jit(solution)/shard_map/gather_row/all_to_all | solution.py:126
  83.5 2.8 %collective-permute-start.10 = (bf16[2,128,128]{2,1,0:T(8,128)(2,1)S(1)}, bf16[2,128,128]{2,1,0:T(8,128)(2,1)S(1)}, u32[]{:S(2)}, u32[]{:S(2)}) collective-permute-start(bf16[2,128,128]{2,1,0:T(8,128)(2,1)S(1)} %bitcast.79), channel_id=1, source_target_pairs={{0,4},{4,0},{1,5},{5,1},{2,6},{6,2},{3,7},{7,3},{8,12},{12,8},{9,1... | collective-permute-start | bytes 196616 | tf_op jit(solution)/shard_map/gather_col/ppermute | solution.py:108
  86.3 3.7 %collective-permute-done.10 = bf16[2,128,128]{2,1,0:T(8,128)(2,1)S(1)} collective-permute-done((bf16[2,128,128]{2,1,0:T(8,128)(2,1)S(1)}, bf16[2,128,128]{2,1,0:T(8,128)(2,1)S(1)}, u32[]{:S(2)}, u32[]{:S(2)}) %collective-permute-start.10) | collective-permute-done | bytes 65568 | tf_op jit(solution)/shard_map/gather_col/ppermute | solution.py:108
  90.0 2.8 %collective-permute-start.14 = (bf16[2,2,128,128]{3,2,1,0:T(8,128)(2,1)S(1)}, bf16[2,2,128,128]{3,2,1,0:T(8,128)(2,1)S(1)}, u32[]{:S(2)}, u32[]{:S(2)}) collective-permute-start(bf16[2,2,128,128]{3,2,1,0:T(8,128)(2,1)S(1)} %pad_maximum_fusion.2.f0), channel_id=1, source_target_pairs={{0,3},{1,2},{2,1},{3,0},{4,7},{5,6},{6,5},{7,4},{8,11},{9,10},{10,... | collective-permute-start | bytes 393224 | tf_op jit(solution)/shard_map/gather_col/ppermute | solution.py:108
  92.7 0.8 collective-permute-start.12
  93.5 4.3 %collective-permute-done.14.f3 = bf16[2,2,128,128]{3,2,1,0:T(8,128)(2,1)S(1)} collective-permute-done((bf16[2,2,128,128]{3,2,1,0:T(8,128)(2,1)S(1)}, bf16[2,2,128,128]{3,2,1,0:T(8,128)(2,1)S(1)}, u32[]{:S(2)}, u32[]{:S(2)}) %collective-permute-start.14) | collective-permute-done | bytes 131104 | tf_op jit(solution)/shard_map/gather_col/ppermute | solution.py:108
  97.8 0.5 collective-permute-done.13.f2
  98.3 0.5 collective-permute-done.12.f1
  98.8 2.7 %ahead.3 = (f32[32,128,128]{2,1,0:T(8,128)S(1)}, bf16[32,128,128]{2,1,0:T(8,128)(2,1)S(1)}) custom-call(s32[96]{0:T(128)S(1)} %get-tuple-element.104.src_ref, s32[96]{0:T(128)S(1)} %get-tuple-element.103.slot_ref, s32[1]{0:T(128)} %bitcast.69.count_ref, bf16[2,2,128,128]{3,2,1,0:T(8,128)(2,1)S(1)} %pad_maximum_fusion.2.f0, ...), custom_call_target="tpu_custom_call" | custom-call | flops 3221225472 | bytes 3145728 | tf_op jit(solution)/shard_map/ahead/ahead/pallas_call | solution.py:85
  101.5 2.8 %collective-permute-start.18 = (bf16[32,128,128]{2,1,0:T(8,128)(2,1)S(1)}, bf16[32,128,128]{2,1,0:T(8,128)(2,1)S(1)}, u32[]{:S(2)}, u32[]{:S(2)}) collective-permute-start(bf16[32,128,128]{2,1,0:T(8,128)(2,1)S(1)} %get-tuple-element.77), channel_id=1, source_target_pairs={{0,8},{8,0},{1,9},{9,1},{2,10},{10,2},{3,11},{11,3},{4,12},{12,4},... | collective-permute-start | bytes 3145736 | tf_op jit(solution)/shard_map/scatter_row/ppermute | solution.py:108
  104.3 3.0 %collective-permute-start.17 = (f32[136,128]{1,0:T(8,128)S(1)}, f32[136,128]{1,0:T(8,128)S(1)}, u32[]{:S(2)}, u32[]{:S(2)}) collective-permute-start(f32[136,128]{1,0:T(8,128)S(1)} %bitcast_add_fusion.2), channel_id=1, source_target_pairs={{0,96},{32,64},{64,32},{96,0},{128,224},{160,192},{192,160},{224,1... | collective-permute-start | bytes 208904 | tf_op jit(solution)/shard_map/weights/ppermute | solution.py:108
  107.3 0.7 collective-permute-start.16
  108.0 3.6 %collective-permute-done.17 = f32[136,128]{1,0:T(8,128)S(1)} collective-permute-done((f32[136,128]{1,0:T(8,128)S(1)}, f32[136,128]{1,0:T(8,128)S(1)}, u32[]{:S(2)}, u32[]{:S(2)}) %collective-permute-start.17) | collective-permute-done | bytes 69664 | tf_op jit(solution)/shard_map/weights/ppermute | solution.py:108
  111.6 3.6 %collective-permute-done.16 = f32[136,128]{1,0:T(8,128)S(1)} collective-permute-done((f32[136,128]{1,0:T(8,128)S(1)}, f32[136,128]{1,0:T(8,128)S(1)}, u32[]{:S(2)}, u32[]{:S(2)}) %collective-permute-start.16) | collective-permute-done | bytes 69664 | tf_op jit(solution)/shard_map/weights/ppermute | solution.py:108
  115.3 1.3 add_convert_fusion
  116.6 0.9 collective-permute-start.19
  117.4 5.5 %all-to-all-start.3 = ((bf16[16,256,128]{2,1,0:T(8,128)(2,1)}), bf16[16,256,128]{2,1,0:T(8,128)(2,1)S(1)}, u32[]{:S(2)}, u32[]{:S(2)}) async-start(bf16[16,256,128]{2,1,0:T(8,128)(2,1)} %bitcast.82), calls=%async_computation.3 | async-start | bytes 2097152 | tf_op jit(solution)/shard_map/scatter_row/all_to_all | solution.py:140
  123.0 1.4 collective-permute-start.20
  124.3 3.6 %collective-permute-done.20 = f32[136,128]{1,0:T(8,128)S(1)} collective-permute-done((f32[136,128]{1,0:T(8,128)S(1)}, f32[136,128]{1,0:T(8,128)S(1)}, u32[]{:S(2)}, u32[]{:S(2)}) %collective-permute-start.20) | collective-permute-done | bytes 69664 | tf_op jit(solution)/shard_map/gather_row/weights/ppermute | solution.py:108
  127.9 2.8 %collective-permute-start.21 = (f32[136,128]{1,0:T(8,128)S(1)}, f32[136,128]{1,0:T(8,128)S(1)}, u32[]{:S(2)}, u32[]{:S(2)}) collective-permute-start(f32[136,128]{1,0:T(8,128)S(1)} %add.123), channel_id=1, source_target_pairs={{0,4},{4,0},{1,5},{5,1},{2,6},{6,2},{3,7},{7,3},{8,12},{12,8},{9,1... | collective-permute-start | bytes 208904 | tf_op jit(solution)/shard_map/behind/weights/ppermute | solution.py:108
  130.7 2.7 %behind.3 = (f32[4,128,128]{2,1,0:T(8,128)S(1)}, bf16[4,128,128]{2,1,0:T(8,128)(2,1)S(1)}, bf16[4,128,128]{2,1,0:T(8,128)(2,1)S(1)}, bf16[4,128,128]{2,1,0:T(8,128)(2,1)S(1)}) custom-call(s32[96]{0:T(128)S(1)} %get-tuple-element.104.src_ref, s32[96]{0:T(128)S(1)} %get-tuple-element.103.slot_ref, s32[1]{0:T(128)} %bitcast.70.count_ref, ...), custom_call_target="tpu_custom_call" | custom-call | flops 3221225472 | bytes 3145728 | tf_op jit(solution)/shard_map/behind/behind/pallas_call | solution.py:85
  133.4 2.6 %collective-permute-start.27 = (f32[136,128]{1,0:T(8,128)S(1)}, f32[136,128]{1,0:T(8,128)S(1)}, u32[]{:S(2)}, u32[]{:S(2)}) collective-permute-start(f32[136,128]{1,0:T(8,128)S(1)} %add.124), channel_id=1, source_target_pairs={{0,3},{1,2},{2,1},{3,0},{4,7},{5,6},{6,5},{7,4},{8,11},{9,10},{10,... | collective-permute-start | bytes 208904 | tf_op jit(solution)/shard_map/scatter_col/weights/ppermute | solution.py:108
  136.0 1.1 collective-permute-start.26
  137.1 1.5 collective-permute-start.22
  138.6 1.9 %collective-permute-start.23 = (bf16[4,128,128]{2,1,0:T(8,128)(2,1)S(1)}, bf16[4,128,128]{2,1,0:T(8,128)(2,1)S(1)}, u32[]{:S(2)}, u32[]{:S(2)}) collective-permute-start(bf16[4,128,128]{2,1,0:T(8,128)(2,1)S(1)} %get-tuple-element.89), channel_id=1, source_target_pairs={{0,2},{1,3},{2,0},{3,1},{4,6},{5,7},{6,4},{7,5},{8,10},{9,11},{10,... | collective-permute-start | bytes 393224 | tf_op jit(solution)/shard_map/scatter_col/ppermute | solution.py:108
  140.4 1.0 collective-permute-start.24
  141.4 2.0 %collective-permute-done.22 = bf16[4,128,128]{2,1,0:T(8,128)(2,1)S(1)} collective-permute-done((bf16[4,128,128]{2,1,0:T(8,128)(2,1)S(1)}, bf16[4,128,128]{2,1,0:T(8,128)(2,1)S(1)}, u32[]{:S(2)}, u32[]{:S(2)}) %collective-permute-start.22) | collective-permute-done | bytes 131104 | tf_op jit(solution)/shard_map/scatter_col/ppermute | solution.py:108
  143.4 3.8 %collective-permute-done.23 = bf16[4,128,128]{2,1,0:T(8,128)(2,1)S(1)} collective-permute-done((bf16[4,128,128]{2,1,0:T(8,128)(2,1)S(1)}, bf16[4,128,128]{2,1,0:T(8,128)(2,1)S(1)}, u32[]{:S(2)}, u32[]{:S(2)}) %collective-permute-start.23) | collective-permute-done | bytes 131104 | tf_op jit(solution)/shard_map/scatter_col/ppermute | solution.py:108
  147.3 4.7 %collective-permute-start.29 = (f32[136,128]{1,0:T(8,128)S(1)}, f32[136,128]{1,0:T(8,128)S(1)}, u32[]{:S(2)}, u32[]{:S(2)}) collective-permute-start(f32[136,128]{1,0:T(8,128)S(1)} %add_add_fusion), channel_id=1, source_target_pairs={{0,128},{32,160},{64,192},{96,224},{128,0},{160,32},{192,64},{224,... | collective-permute-start | bytes 208904 | tf_op jit(solution)/shard_map/weights/ppermute | solution.py:108
  151.9 2.4 %collective-permute-start.28 = (bf16[2,128,128]{2,1,0:T(8,128)(2,1)S(1)}, bf16[2,128,128]{2,1,0:T(8,128)(2,1)S(1)}, u32[]{:S(2)}, u32[]{:S(2)}) collective-permute-start(bf16[2,128,128]{2,1,0:T(8,128)(2,1)S(1)} %slice.24), channel_id=1, source_target_pairs={{0,4},{4,0},{1,5},{5,1},{2,6},{6,2},{3,7},{7,3},{8,12},{12,8},{9,1... | collective-permute-start | bytes 196616 | tf_op jit(solution)/shard_map/scatter_col/ppermute | solution.py:108
  154.3 0.2 collective-permute-done.29
  154.5 2.1 %collective-permute-done.28 = bf16[2,128,128]{2,1,0:T(8,128)(2,1)S(1)} collective-permute-done((bf16[2,128,128]{2,1,0:T(8,128)(2,1)S(1)}, bf16[2,128,128]{2,1,0:T(8,128)(2,1)S(1)}, u32[]{:S(2)}, u32[]{:S(2)}) %collective-permute-start.28) | collective-permute-done | bytes 65568 | tf_op jit(solution)/shard_map/scatter_col/ppermute | solution.py:108
  156.7 5.4 %collective-permute-start.30 = (f32[136,128]{1,0:T(8,128)S(1)}, f32[136,128]{1,0:T(8,128)S(1)}, u32[]{:S(2)}, u32[]{:S(2)}) collective-permute-start(f32[136,128]{1,0:T(8,128)S(1)} %add.131), channel_id=1, source_target_pairs={{0,8},{8,0},{1,9},{9,1},{2,10},{10,2},{3,11},{11,3},{4,12},{12,4},... | collective-permute-start | bytes 208904 | tf_op jit(solution)/shard_map/weights/ppermute | solution.py:108
  162.0 0.9 collective-permute-done.30
  163.0 0.8 final.1
  (54 shorter events, 0.6 us)
Async XLA Ops:
  0.6 18.3 %copy-start.7 = (s32[1,1,96]{2,1,0:T(1,128)S(1)}, s32[1,1,96]{2,1,0:T(1,128)}, u32[]{:S(2)}) copy-start(s32[1,1,96]{2,1,0:T(1,128)} %param.13) | copy-start | bytes 1156
  0.6 18.3 %copy-start.8 = (s32[1,1,96]{2,1,0:T(1,128)S(1)}, s32[1,1,96]{2,1,0:T(1,128)}, u32[]{:S(2)}) copy-start(s32[1,1,96]{2,1,0:T(1,128)} %param.12) | copy-start | bytes 1156
  0.7 14.7 %collective-permute-start = (bf16[2,128,128]{2,1,0:T(8,128)(2,1)}, bf16[2,128,128]{2,1,0:T(8,128)(2,1)S(1)}, u32[]{:S(2)}, u32[]{:S(2)}) collective-permute-start(bf16[2,128,128]{2,1,0:T(8,128)(2,1)} %bitcast.75), channel_id=1, source_target_pairs={{0,4},{4,0},{1,5},{5,1},{2,6},{6,2},{3,7},{7,3},{8,12},{12,8},{9,1... | collective-permute-start | bytes 196616 | tf_op jit(solution)/shard_map/gather_col/ppermute | solution.py:108
  4.3 0.9 copy-start
  5.2 10.2 %copy-start.1 = (bf16[256,128]{1,0:T(8,128)(2,1)S(1)}, bf16[256,128]{1,0:T(8,128)(2,1)}, u32[]{:S(2)}) copy-start(bf16[256,128]{1,0:T(8,128)(2,1)} %features_ref.3) | copy-start | bytes 196612
  6.4 33.4 %all-to-all-start = ((bf16[16,2,128,128]{3,2,1,0:T(8,128)(2,1)}), bf16[16,2,128,128]{3,2,1,0:T(8,128)(2,1)S(1)}, u32[]{:S(2)}, u32[]{:S(2)}) async-start(bf16[16,2,128,128]{3,2,1,0:T(8,128)(2,1)} %prepare.1), calls=%async_computation | async-start | bytes 2097152 | tf_op jit(solution)/shard_map/gather_row/all_to_all | solution.py:126
  15.4 8.2 %collective-permute-start.3 = (bf16[2,2,128,128]{3,2,1,0:T(8,128)(2,1)S(1)}, bf16[2,2,128,128]{3,2,1,0:T(8,128)(2,1)S(1)}, u32[]{:S(2)}, u32[]{:S(2)}) collective-permute-start(bf16[2,2,128,128]{3,2,1,0:T(8,128)(2,1)S(1)} %pad_maximum_fusion.1.f0), channel_id=1, source_target_pairs={{0,3},{1,2},{2,1},{3,0},{4,7},{5,6},{6,5},{7,4},{8,11},{9,10},{10,... | collective-permute-start | bytes 393224 | tf_op jit(solution)/shard_map/gather_col/ppermute | solution.py:108
  18.2 5.6 %collective-permute-start.2 = (bf16[2,2,128,128]{3,2,1,0:T(8,128)(2,1)S(1)}, bf16[2,2,128,128]{3,2,1,0:T(8,128)(2,1)S(1)}, u32[]{:S(2)}, u32[]{:S(2)}) collective-permute-start(bf16[2,2,128,128]{3,2,1,0:T(8,128)(2,1)S(1)} %pad_maximum_fusion.1.f0), channel_id=1, source_target_pairs={{0,2},{1,3},{2,0},{3,1},{4,6},{5,7},{6,4},{7,5},{8,10},{9,11},{10,... | collective-permute-start | bytes 393224 | tf_op jit(solution)/shard_map/gather_col/ppermute | solution.py:108
  18.6 5.4 %collective-permute-start.1 = (bf16[2,2,128,128]{3,2,1,0:T(8,128)(2,1)S(1)}, bf16[2,2,128,128]{3,2,1,0:T(8,128)(2,1)S(1)}, u32[]{:S(2)}, u32[]{:S(2)}) collective-permute-start(bf16[2,2,128,128]{3,2,1,0:T(8,128)(2,1)S(1)} %pad_maximum_fusion.1.f0), channel_id=1, source_target_pairs={{0,1},{1,0},{2,3},{3,2},{4,5},{5,4},{6,7},{7,6},{8,9},{9,8},{10,11... | collective-permute-start | bytes 393224 | tf_op jit(solution)/shard_map/gather_col/ppermute | solution.py:108
  26.6 5.5 %collective-permute-start.4 = (bf16[32,128,128]{2,1,0:T(8,128)(2,1)S(1)}, bf16[32,128,128]{2,1,0:T(8,128)(2,1)S(1)}, u32[]{:S(2)}, u32[]{:S(2)}) collective-permute-start(bf16[32,128,128]{2,1,0:T(8,128)(2,1)S(1)} %get-tuple-element.54), channel_id=1, source_target_pairs={{0,8},{8,0},{1,9},{9,1},{2,10},{10,2},{3,11},{11,3},{4,12},{12,4},... | collective-permute-start | bytes 3145736 | tf_op jit(solution)/shard_map/scatter_row/ppermute | solution.py:108
  39.7 7.9 %collective-permute-start.5 = (bf16[32,128,128]{2,1,0:T(8,128)(2,1)S(1)}, bf16[32,128,128]{2,1,0:T(8,128)(2,1)S(1)}, u32[]{:S(2)}, u32[]{:S(2)}) collective-permute-start(bf16[32,128,128]{2,1,0:T(8,128)(2,1)S(1)} %bitcast.73), channel_id=1, source_target_pairs={{0,8},{8,0},{1,9},{9,1},{2,10},{10,2},{3,11},{11,3},{4,12},{12,4},... | collective-permute-start | bytes 3145736 | tf_op jit(solution)/shard_map/gather_row/ppermute | solution.py:108
  44.0 31.8 %all-to-all-start.1 = ((f16[16,256,128]{2,1,0:T(8,128)(2,1)}), f16[16,256,128]{2,1,0:T(8,128)(2,1)S(1)}, u32[]{:S(2)}, u32[]{:S(2)}) async-start(f16[16,256,128]{2,1,0:T(8,128)(2,1)} %bitcast.83), calls=%async_computation.1 | async-start | bytes 2097152 | tf_op jit(solution)/shard_map/scatter_row/all_to_all | solution.py:140
  47.7 18.7 %copy-start.6 = (s32[256]{0:T(256)S(1)}, s32[256]{0:T(256)}, u32[]{:S(2)}) copy-start(s32[256]{0:T(256)} %param.15) | copy-start | bytes 3076
  50.4 25.8 %copy-start.2 = (bf16[256,128]{1,0:T(8,128)(2,1)S(1)}, bf16[256,128]{1,0:T(8,128)(2,1)}, u32[]{:S(2)}) copy-start(bf16[256,128]{1,0:T(8,128)(2,1)} %upstream_ref.1) | copy-start | bytes 196612
  50.4 25.8 %copy-start.3 = (bf16[128,128]{1,0:T(8,128)(2,1)S(1)}, bf16[128,128]{1,0:T(8,128)(2,1)}, u32[]{:S(2)}) copy-start(bf16[128,128]{1,0:T(8,128)(2,1)} %w_self_ref.1) | copy-start | bytes 98308
  50.4 25.8 %copy-start.4 = (bf16[128,128]{1,0:T(8,128)(2,1)S(1)}, bf16[128,128]{1,0:T(8,128)(2,1)}, u32[]{:S(2)}) copy-start(bf16[128,128]{1,0:T(8,128)(2,1)} %w_neigh_ref.1) | copy-start | bytes 98308
  50.4 25.8 %copy-start.5 = (f32[128]{0:T(128)S(1)}, f32[128]{0:T(128)}, u32[]{:S(2)}) copy-start(f32[128]{0:T(128)} %param.18) | copy-start | bytes 1540
  50.4 6.1 %collective-permute-start.6 = (bf16[4,128,128]{2,1,0:T(8,128)(2,1)S(1)}, bf16[4,128,128]{2,1,0:T(8,128)(2,1)S(1)}, u32[]{:S(2)}, u32[]{:S(2)}) collective-permute-start(bf16[4,128,128]{2,1,0:T(8,128)(2,1)S(1)} %get-tuple-element.58), channel_id=1, source_target_pairs={{0,1},{1,0},{2,3},{3,2},{4,5},{5,4},{6,7},{7,6},{8,9},{9,8},{10,11... | collective-permute-start | bytes 393224 | tf_op jit(solution)/shard_map/scatter_col/ppermute | solution.py:108
  52.9 8.9 %collective-permute-start.7 = (bf16[4,128,128]{2,1,0:T(8,128)(2,1)S(1)}, bf16[4,128,128]{2,1,0:T(8,128)(2,1)S(1)}, u32[]{:S(2)}, u32[]{:S(2)}) collective-permute-start(bf16[4,128,128]{2,1,0:T(8,128)(2,1)S(1)} %get-tuple-element.59), channel_id=1, source_target_pairs={{0,2},{1,3},{2,0},{3,1},{4,6},{5,7},{6,4},{7,5},{8,10},{9,11},{10,... | collective-permute-start | bytes 393224 | tf_op jit(solution)/shard_map/scatter_col/ppermute | solution.py:108
  55.0 9.4 %collective-permute-start.8 = (bf16[4,128,128]{2,1,0:T(8,128)(2,1)S(1)}, bf16[4,128,128]{2,1,0:T(8,128)(2,1)S(1)}, u32[]{:S(2)}, u32[]{:S(2)}) collective-permute-start(bf16[4,128,128]{2,1,0:T(8,128)(2,1)S(1)} %get-tuple-element.60), channel_id=1, source_target_pairs={{0,3},{1,2},{2,1},{3,0},{4,7},{5,6},{6,5},{7,4},{8,11},{9,10},{10,... | collective-permute-start | bytes 393224 | tf_op jit(solution)/shard_map/scatter_col/ppermute | solution.py:108
  64.5 11.3 %collective-permute-start.9 = (f16[2,128,128]{2,1,0:T(8,128)(2,1)S(1)}, f16[2,128,128]{2,1,0:T(8,128)(2,1)S(1)}, u32[]{:S(2)}, u32[]{:S(2)}) collective-permute-start(f16[2,128,128]{2,1,0:T(8,128)(2,1)S(1)} %get-tuple-element.102), channel_id=1, source_target_pairs={{0,4},{4,0},{1,5},{5,1},{2,6},{6,2},{3,7},{7,3},{8,12},{12,8},{9,1... | collective-permute-start | bytes 196616 | tf_op jit(solution)/shard_map/scatter_col/ppermute | solution.py:108
  77.7 8.6 %collective-permute-start.11 = (f32[136,128]{1,0:T(8,128)S(1)}, f32[136,128]{1,0:T(8,128)S(1)}, u32[]{:S(2)}, u32[]{:S(2)}) collective-permute-start(f32[136,128]{1,0:T(8,128)S(1)} %dynamic-slice_bitcast_fusion), channel_id=1, source_target_pairs={{0,8},{8,0},{1,9},{9,1},{2,10},{10,2},{3,11},{11,3},{4,12},{12,4},... | collective-permute-start | bytes 208904 | tf_op jit(solution)/shard_map/gather_col/weights/ppermute | solution.py:108
  78.9 37.7 %all-to-all-start.2 = ((bf16[16,2,128,128]{3,2,1,0:T(8,128)(2,1)}), bf16[16,2,128,128]{3,2,1,0:T(8,128)(2,1)S(1)}, u32[]{:S(2)}, u32[]{:S(2)}) async-start(bf16[16,2,128,128]{3,2,1,0:T(8,128)(2,1)} %get-tuple-element.62), calls=%async_computation.2 | async-start | bytes 2097152 | tf_op jit(solution)/shard_map/gather_row/all_to_all | solution.py:126
  83.5 6.5 %collective-permute-start.10 = (bf16[2,128,128]{2,1,0:T(8,128)(2,1)S(1)}, bf16[2,128,128]{2,1,0:T(8,128)(2,1)S(1)}, u32[]{:S(2)}, u32[]{:S(2)}) collective-permute-start(bf16[2,128,128]{2,1,0:T(8,128)(2,1)S(1)} %bitcast.79), channel_id=1, source_target_pairs={{0,4},{4,0},{1,5},{5,1},{2,6},{6,2},{3,7},{7,3},{8,12},{12,8},{9,1... | collective-permute-start | bytes 196616 | tf_op jit(solution)/shard_map/gather_col/ppermute | solution.py:108
  90.0 7.9 %collective-permute-start.14 = (bf16[2,2,128,128]{3,2,1,0:T(8,128)(2,1)S(1)}, bf16[2,2,128,128]{3,2,1,0:T(8,128)(2,1)S(1)}, u32[]{:S(2)}, u32[]{:S(2)}) collective-permute-start(bf16[2,2,128,128]{3,2,1,0:T(8,128)(2,1)S(1)} %pad_maximum_fusion.2.f0), channel_id=1, source_target_pairs={{0,3},{1,2},{2,1},{3,0},{4,7},{5,6},{6,5},{7,4},{8,11},{9,10},{10,... | collective-permute-start | bytes 393224 | tf_op jit(solution)/shard_map/gather_col/ppermute | solution.py:108
  92.7 5.6 %collective-permute-start.13 = (bf16[2,2,128,128]{3,2,1,0:T(8,128)(2,1)S(1)}, bf16[2,2,128,128]{3,2,1,0:T(8,128)(2,1)S(1)}, u32[]{:S(2)}, u32[]{:S(2)}) collective-permute-start(bf16[2,2,128,128]{3,2,1,0:T(8,128)(2,1)S(1)} %pad_maximum_fusion.2.f0), channel_id=1, source_target_pairs={{0,2},{1,3},{2,0},{3,1},{4,6},{5,7},{6,4},{7,5},{8,10},{9,11},{10,... | collective-permute-start | bytes 393224 | tf_op jit(solution)/shard_map/gather_col/ppermute | solution.py:108
  92.7 6.1 %collective-permute-start.12 = (bf16[2,2,128,128]{3,2,1,0:T(8,128)(2,1)S(1)}, bf16[2,2,128,128]{3,2,1,0:T(8,128)(2,1)S(1)}, u32[]{:S(2)}, u32[]{:S(2)}) collective-permute-start(bf16[2,2,128,128]{3,2,1,0:T(8,128)(2,1)S(1)} %pad_maximum_fusion.2.f0), channel_id=1, source_target_pairs={{0,1},{1,0},{2,3},{3,2},{4,5},{5,4},{6,7},{7,6},{8,9},{9,8},{10,11... | collective-permute-start | bytes 393224 | tf_op jit(solution)/shard_map/gather_col/ppermute | solution.py:108
  101.5 13.8 %collective-permute-start.18 = (bf16[32,128,128]{2,1,0:T(8,128)(2,1)S(1)}, bf16[32,128,128]{2,1,0:T(8,128)(2,1)S(1)}, u32[]{:S(2)}, u32[]{:S(2)}) collective-permute-start(bf16[32,128,128]{2,1,0:T(8,128)(2,1)S(1)} %get-tuple-element.77), channel_id=1, source_target_pairs={{0,8},{8,0},{1,9},{9,1},{2,10},{10,2},{3,11},{11,3},{4,12},{12,4},... | collective-permute-start | bytes 3145736 | tf_op jit(solution)/shard_map/scatter_row/ppermute | solution.py:108
  104.3 7.3 %collective-permute-start.17 = (f32[136,128]{1,0:T(8,128)S(1)}, f32[136,128]{1,0:T(8,128)S(1)}, u32[]{:S(2)}, u32[]{:S(2)}) collective-permute-start(f32[136,128]{1,0:T(8,128)S(1)} %bitcast_add_fusion.2), channel_id=1, source_target_pairs={{0,96},{32,64},{64,32},{96,0},{128,224},{160,192},{192,160},{224,1... | collective-permute-start | bytes 208904 | tf_op jit(solution)/shard_map/weights/ppermute | solution.py:108
  107.3 8.0 %collective-permute-start.16 = (f32[136,128]{1,0:T(8,128)S(1)}, f32[136,128]{1,0:T(8,128)S(1)}, u32[]{:S(2)}, u32[]{:S(2)}) collective-permute-start(f32[136,128]{1,0:T(8,128)S(1)} %bitcast_add_fusion.2), channel_id=1, source_target_pairs={{0,64},{32,96},{64,0},{96,32},{128,192},{160,224},{192,128},{224,1... | collective-permute-start | bytes 208904 | tf_op jit(solution)/shard_map/weights/ppermute | solution.py:108
  108.0 7.3 %collective-permute-start.15 = (f32[136,128]{1,0:T(8,128)S(1)}, f32[136,128]{1,0:T(8,128)S(1)}, u32[]{:S(2)}, u32[]{:S(2)}) collective-permute-start(f32[136,128]{1,0:T(8,128)S(1)} %bitcast_add_fusion.2), channel_id=1, source_target_pairs={{0,32},{32,0},{64,96},{96,64},{128,160},{160,128},{192,224},{224,1... | collective-permute-start | bytes 208904 | tf_op jit(solution)/shard_map/weights/ppermute | solution.py:108
  116.6 11.4 %collective-permute-start.19 = (bf16[32,128,128]{2,1,0:T(8,128)(2,1)S(1)}, bf16[32,128,128]{2,1,0:T(8,128)(2,1)S(1)}, u32[]{:S(2)}, u32[]{:S(2)}) collective-permute-start(bf16[32,128,128]{2,1,0:T(8,128)(2,1)S(1)} %bitcast.71), channel_id=1, source_target_pairs={{0,8},{8,0},{1,9},{9,1},{2,10},{10,2},{3,11},{11,3},{4,12},{12,4},... | collective-permute-start | bytes 3145736 | tf_op jit(solution)/shard_map/gather_row/ppermute | solution.py:108
  117.4 45.5 %all-to-all-start.3 = ((bf16[16,256,128]{2,1,0:T(8,128)(2,1)}), bf16[16,256,128]{2,1,0:T(8,128)(2,1)S(1)}, u32[]{:S(2)}, u32[]{:S(2)}) async-start(bf16[16,256,128]{2,1,0:T(8,128)(2,1)} %bitcast.82), calls=%async_computation.3 | async-start | bytes 2097152 | tf_op jit(solution)/shard_map/scatter_row/all_to_all | solution.py:140
  123.0 4.9 %collective-permute-start.20 = (f32[136,128]{1,0:T(8,128)S(1)}, f32[136,128]{1,0:T(8,128)S(1)}, u32[]{:S(2)}, u32[]{:S(2)}) collective-permute-start(f32[136,128]{1,0:T(8,128)S(1)} %add_add_fusion.1), channel_id=1, source_target_pairs={{0,16},{16,0},{1,17},{17,1},{2,18},{18,2},{3,19},{19,3},{4,20},{20... | collective-permute-start | bytes 208904 | tf_op jit(solution)/shard_map/gather_row/weights/ppermute | solution.py:108
  127.9 5.5 %collective-permute-start.21 = (f32[136,128]{1,0:T(8,128)S(1)}, f32[136,128]{1,0:T(8,128)S(1)}, u32[]{:S(2)}, u32[]{:S(2)}) collective-permute-start(f32[136,128]{1,0:T(8,128)S(1)} %add.123), channel_id=1, source_target_pairs={{0,4},{4,0},{1,5},{5,1},{2,6},{6,2},{3,7},{7,3},{8,12},{12,8},{9,1... | collective-permute-start | bytes 208904 | tf_op jit(solution)/shard_map/behind/weights/ppermute | solution.py:108
  133.4 7.0 %collective-permute-start.27 = (f32[136,128]{1,0:T(8,128)S(1)}, f32[136,128]{1,0:T(8,128)S(1)}, u32[]{:S(2)}, u32[]{:S(2)}) collective-permute-start(f32[136,128]{1,0:T(8,128)S(1)} %add.124), channel_id=1, source_target_pairs={{0,3},{1,2},{2,1},{3,0},{4,7},{5,6},{6,5},{7,4},{8,11},{9,10},{10,... | collective-permute-start | bytes 208904 | tf_op jit(solution)/shard_map/scatter_col/weights/ppermute | solution.py:108
  136.0 5.4 %collective-permute-start.26 = (f32[136,128]{1,0:T(8,128)S(1)}, f32[136,128]{1,0:T(8,128)S(1)}, u32[]{:S(2)}, u32[]{:S(2)}) collective-permute-start(f32[136,128]{1,0:T(8,128)S(1)} %add.124), channel_id=1, source_target_pairs={{0,2},{1,3},{2,0},{3,1},{4,6},{5,7},{6,4},{7,5},{8,10},{9,11},{10,... | collective-permute-start | bytes 208904 | tf_op jit(solution)/shard_map/scatter_col/weights/ppermute | solution.py:108
  137.1 4.3 %collective-permute-start.25 = (f32[136,128]{1,0:T(8,128)S(1)}, f32[136,128]{1,0:T(8,128)S(1)}, u32[]{:S(2)}, u32[]{:S(2)}) collective-permute-start(f32[136,128]{1,0:T(8,128)S(1)} %add.124), channel_id=1, source_target_pairs={{0,1},{1,0},{2,3},{3,2},{4,5},{5,4},{6,7},{7,6},{8,9},{9,8},{10,11... | collective-permute-start | bytes 208904 | tf_op jit(solution)/shard_map/scatter_col/weights/ppermute | solution.py:108
  137.1 6.3 %collective-permute-start.22 = (bf16[4,128,128]{2,1,0:T(8,128)(2,1)S(1)}, bf16[4,128,128]{2,1,0:T(8,128)(2,1)S(1)}, u32[]{:S(2)}, u32[]{:S(2)}) collective-permute-start(bf16[4,128,128]{2,1,0:T(8,128)(2,1)S(1)} %get-tuple-element.88), channel_id=1, source_target_pairs={{0,1},{1,0},{2,3},{3,2},{4,5},{5,4},{6,7},{7,6},{8,9},{9,8},{10,11... | collective-permute-start | bytes 393224 | tf_op jit(solution)/shard_map/scatter_col/ppermute | solution.py:108
  138.6 8.6 %collective-permute-start.23 = (bf16[4,128,128]{2,1,0:T(8,128)(2,1)S(1)}, bf16[4,128,128]{2,1,0:T(8,128)(2,1)S(1)}, u32[]{:S(2)}, u32[]{:S(2)}) collective-permute-start(bf16[4,128,128]{2,1,0:T(8,128)(2,1)S(1)} %get-tuple-element.89), channel_id=1, source_target_pairs={{0,2},{1,3},{2,0},{3,1},{4,6},{5,7},{6,4},{7,5},{8,10},{9,11},{10,... | collective-permute-start | bytes 393224 | tf_op jit(solution)/shard_map/scatter_col/ppermute | solution.py:108
  140.4 6.8 %collective-permute-start.24 = (bf16[4,128,128]{2,1,0:T(8,128)(2,1)S(1)}, bf16[4,128,128]{2,1,0:T(8,128)(2,1)S(1)}, u32[]{:S(2)}, u32[]{:S(2)}) collective-permute-start(bf16[4,128,128]{2,1,0:T(8,128)(2,1)S(1)} %get-tuple-element.90), channel_id=1, source_target_pairs={{0,3},{1,2},{2,1},{3,0},{4,7},{5,6},{6,5},{7,4},{8,11},{9,10},{10,... | collective-permute-start | bytes 393224 | tf_op jit(solution)/shard_map/scatter_col/ppermute | solution.py:108
  147.3 7.3 %collective-permute-start.29 = (f32[136,128]{1,0:T(8,128)S(1)}, f32[136,128]{1,0:T(8,128)S(1)}, u32[]{:S(2)}, u32[]{:S(2)}) collective-permute-start(f32[136,128]{1,0:T(8,128)S(1)} %add_add_fusion), channel_id=1, source_target_pairs={{0,128},{32,160},{64,192},{96,224},{128,0},{160,32},{192,64},{224,... | collective-permute-start | bytes 208904 | tf_op jit(solution)/shard_map/weights/ppermute | solution.py:108
  151.9 4.7 %collective-permute-start.28 = (bf16[2,128,128]{2,1,0:T(8,128)(2,1)S(1)}, bf16[2,128,128]{2,1,0:T(8,128)(2,1)S(1)}, u32[]{:S(2)}, u32[]{:S(2)}) collective-permute-start(bf16[2,128,128]{2,1,0:T(8,128)(2,1)S(1)} %slice.24), channel_id=1, source_target_pairs={{0,4},{4,0},{1,5},{5,1},{2,6},{6,2},{3,7},{7,3},{8,12},{12,8},{9,1... | collective-permute-start | bytes 196616 | tf_op jit(solution)/shard_map/scatter_col/ppermute | solution.py:108
  156.7 6.3 %collective-permute-start.30 = (f32[136,128]{1,0:T(8,128)S(1)}, f32[136,128]{1,0:T(8,128)S(1)}, u32[]{:S(2)}, u32[]{:S(2)}) collective-permute-start(f32[136,128]{1,0:T(8,128)S(1)} %add.131), channel_id=1, source_target_pairs={{0,8},{8,0},{1,9},{9,1},{2,10},{10,2},{3,11},{11,3},{4,12},{12,4},... | collective-permute-start | bytes 208904 | tf_op jit(solution)/shard_map/weights/ppermute | solution.py:108

commit v3 on v2

--- a/solution.py
+++ b/solution.py
@@ -113,7 +113,7 @@
 
 
 def pack(x, exact):
-    return (x * HALF_SCALE).astype(jnp.float16) if exact else x.astype(jnp.bfloat16)
+    return (x.astype(jnp.float32) * HALF_SCALE).astype(jnp.float16) if exact else x.astype(jnp.bfloat16)
 
 
 def unpack(x):
@@ -122,6 +122,7 @@
 
 
 def aggregate(field, copies, tiles, src, slot, count, exact, side):
+    sent = jnp.float32 if exact else jnp.bfloat16
     with jax.named_scope("gather_row"):
         g0 = lax.all_to_all(copies, ("z", "xl"), 0, 0, tiled=True).reshape(-1, TILE, TILE)
     with jax.named_scope("gather_col"):
@@ -130,11 +131,11 @@
         cols = side(1, pair, *(flip(pair, "y", k) for k in (1, 2, 3)))
     with jax.named_scope("ahead"):
         keep, send = products(
-            ahead_kernel, cols, tiles, src, slot, count, 16, 64, ((32, jnp.float32), (32, jnp.bfloat16)), "ahead"
+            ahead_kernel, cols, tiles, src, slot, count, 16, 64, ((32, jnp.float32), (32, sent)), "ahead"
         )
         keep, send = side(2, keep, send)
     with jax.named_scope("scatter_row"):
-        both = pack(keep + flip(send, "co").astype(jnp.float32), exact)
+        both = pack(keep + unpack(flip(pack(send, exact), "co")), exact)
     g0, both = tie(*side(3, g0), both)
     with jax.named_scope("scatter_row"):
         first = lax.all_to_all(both.reshape(16, -1, TILE), ("z", "xl"), 0, 0, tiled=True)
@@ -142,12 +143,12 @@
         (g1,) = side(4, flip(g0, "co"))
     with jax.named_scope("behind"):
         back, *sends = products(
-            behind_kernel, (g0, g1), tiles, src, slot, count, 64, 16, ((4, jnp.float32),) + ((4, jnp.bfloat16),) * 3, "behind"
+            behind_kernel, (g0, g1), tiles, src, slot, count, 64, 16, ((4, jnp.float32),) + ((4, sent),) * 3, "behind"
         )
         back, *sends = side(5, back, *sends)
     with jax.named_scope("scatter_col"):
         for k in (1, 2, 3):
-            back = back + flip(sends[k - 1], "y", k).astype(jnp.float32)
+            back = back + unpack(flip(pack(sends[k - 1], exact), "y", k))
         (back,) = side(6, back)
         last = flip(pack(back[2:], exact), "xh")
     (last,) = side(7, last)
@@ -243,7 +244,7 @@
     )(co, *args)
 
 
-STEPS = ((("co", 1),), (), (), (("z", 1, 2, 3),), (("xl", 1),), (("xh", 1),), (("y", 1, 2, 3),), (("z", 4),))
+STEPS = ((("co", 1),), (("xh", 1),), (), (("z", 4),), (), (("xl", 1),), (("y", 1, 2, 3),), (("z", 1, 2, 3),))
 
 
 def body(features, tiles, tile_src, tile_dst, tile_count, degree, w_self, w_neigh, bias, upstream):

time: 164 us -> 157 us (0.957)
  starting transfers between devices: 82.9 us -> 76.8 us
  waiting for transfers between devices: 60.9 us -> 58.6 us
    ppermute x31, starting transfers between devices: 60.8 us -> 56 us  [flip(): return lax.ppermute(x, axis, [(i, i ^ d) for i in range(n)])]
    all_to_all x2, waiting for transfers between devices: 6.28 us -> 3.56 us  [aggregate(): lax.all_to_all(copies, ('z', 'xl'), 0, 0, tiled=True)]
    all_to_all x2, starting transfers between devices: 9.2 us -> 7.31 us  [aggregate(): lax.all_to_all(both.reshape(16, -1, TILE), ('z', 'xl'), 0, 0, tiled=True)]
  transfers between devices with their start and end apart: 35 -> 35, of which waited for: 21 -> 18; matrix products, arithmetic and copies ran while one was open for 2% -> 2% of each run, Pallas kernels for 7% -> 8%
where the time goes in v3:
time: 157 us
  starting transfers between devices  76.8 us (49%)
  waiting for transfers between devices  58.6 us (37%)
  Pallas kernels  15 us (10%)
  other arithmetic  3.73 us (2%)
  between operations  1.65 us (1%)
    ppermute x31, starting transfers between devices, flip(): return lax.ppermute(x, axis, [(i, i ^ d) for i in range(n)])  56 us
    ppermute x31, waiting for transfers between devices, flip(): return lax.ppermute(x, axis, [(i, i ^ d) for i in range(n)])  55 us
    all_to_all x2, starting transfers between devices, aggregate(): lax.all_to_all(copies, ('z', 'xl'), 0, 0, tiled=True)  13.5 us
    pallas_call x4, Pallas kernels, products(): pl.pallas_call(kernel, in_specs=[pl.BlockSpec(memory_space=pltpu.SMEM)] *...  11.5 us
    all_to_all x2, starting transfers between devices, aggregate(): lax.all_to_all(both.reshape(16, -1, TILE), ('z', 'xl'), 0, 0, tiled=True)  7.31 us
    all_to_all x2, waiting for transfers between devices, aggregate(): lax.all_to_all(copies, ('z', 'xl'), 0, 0, tiled=True)  3.56 us
  transfers between devices with their start and end apart: 35, of which 18 were waited for; matrix products, arithmetic and copies ran while one was open for 2% of the time, Pallas kernels for 8%

profile of v3, /device:TPU:1, one launch (start us, length us, event | category | flops | bytes accessed | tf_op | source)
XLA Modules:
  0.0 156.7 jit_solution(9877374910250924275)
XLA Ops:
  0.7 3.7 %collective-permute-start = (bf16[2,128,128]{2,1,0:T(8,128)(2,1)}, bf16[2,128,128]{2,1,0:T(8,128)(2,1)S(1)}, u32[]{:S(2)}, u32[]{:S(2)}) collective-permute-start(bf16[2,128,128]{2,1,0:T(8,128)(2,1)} %bitcast.75), channel_id=1, source_target_pairs={{0,4},{4,0},{1,5},{5,1},{2,6},{6,2},{3,7},{7,3},{8,12},{12,8},{9,1... | collective-permute-start | bytes 196616 | tf_op jit(solution)/shard_map/gather_col/ppermute | solution.py:108
  4.3 0.9 copy-done
  5.2 1.2 prepare.1
  6.4 8.3 %all-to-all-start = ((bf16[16,2,128,128]{3,2,1,0:T(8,128)(2,1)}), bf16[16,2,128,128]{3,2,1,0:T(8,128)(2,1)S(1)}, u32[]{:S(2)}, u32[]{:S(2)}) async-start(bf16[16,2,128,128]{3,2,1,0:T(8,128)(2,1)} %prepare.1), calls=%async_computation | async-start | bytes 2097152 | tf_op jit(solution)/shard_map/gather_row/all_to_all | solution.py:127
  15.4 1.4 collective-permute-start.1
  16.8 2.6 %collective-permute-start.2 = (bf16[2,2,128,128]{3,2,1,0:T(8,128)(2,1)S(1)}, bf16[2,2,128,128]{3,2,1,0:T(8,128)(2,1)S(1)}, u32[]{:S(2)}, u32[]{:S(2)}) collective-permute-start(bf16[2,2,128,128]{3,2,1,0:T(8,128)(2,1)S(1)} %pad_maximum_fusion.1.f0), channel_id=1, source_target_pairs={{0,2},{1,3},{2,0},{3,1},{4,6},{5,7},{6,4},{7,5},{8,10},{9,11},{10,... | collective-permute-start | bytes 393224 | tf_op jit(solution)/shard_map/gather_col/ppermute | solution.py:108
  19.5 0.1 collective-permute-done.1.f1
  19.6 4.8 %collective-permute-done.2.f2 = bf16[2,2,128,128]{3,2,1,0:T(8,128)(2,1)S(1)} collective-permute-done((bf16[2,2,128,128]{3,2,1,0:T(8,128)(2,1)S(1)}, bf16[2,2,128,128]{3,2,1,0:T(8,128)(2,1)S(1)}, u32[]{:S(2)}, u32[]{:S(2)}) %collective-permute-start.2) | collective-permute-done | bytes 131104 | tf_op jit(solution)/shard_map/gather_col/ppermute | solution.py:108
  24.4 2.6 %collective-permute-done.3.f3 = bf16[2,2,128,128]{3,2,1,0:T(8,128)(2,1)S(1)} collective-permute-done((bf16[2,2,128,128]{3,2,1,0:T(8,128)(2,1)S(1)}, bf16[2,2,128,128]{3,2,1,0:T(8,128)(2,1)S(1)}, u32[]{:S(2)}, u32[]{:S(2)}) %collective-permute-start.3) | collective-permute-done | bytes 131104 | tf_op jit(solution)/shard_map/gather_col/ppermute | solution.py:108
  27.0 2.9 %ahead.2 = (f32[32,128,128]{2,1,0:T(8,128)S(1)}, f32[32,128,128]{2,1,0:T(8,128)S(1)}) custom-call(s32[96]{0:T(128)S(1)} %get-tuple-element.104.src_ref, s32[96]{0:T(128)S(1)} %get-tuple-element.103.slot_ref, s32[1]{0:T(128)} %bitcast.67.count_ref, bf16[2,2,128,128]{3,2,1,0:T(8,128)(2,1)S(1)} %pad_maximum_fusion.1.f0, ...), custom_call_target="tpu_custom_call" | custom-call | flops 3221225472 | bytes 3145728 | tf_op jit(solution)/shard_map/ahead/ahead/pallas_call | solution.py:85
  29.9 0.3 multiply_convert_fusion.1
  30.2 2.3 %collective-permute-start.4 = (f16[32,128,128]{2,1,0:T(8,128)(2,1)S(1)}, f16[32,128,128]{2,1,0:T(8,128)(2,1)S(1)}, u32[]{:S(2)}, u32[]{:S(2)}) collective-permute-start(f16[32,128,128]{2,1,0:T(8,128)(2,1)S(1)} %multiply_convert_fusion.1), channel_id=1, source_target_pairs={{0,8},{8,0},{1,9},{9,1},{2,10},{10,2},{3,11},{11,3},{4,12},{12,4},... | collective-permute-start | bytes 3145736 | tf_op jit(solution)/shard_map/scatter_row/ppermute | solution.py:108
  32.5 2.3 %collective-permute-done.4 = f16[32,128,128]{2,1,0:T(8,128)(2,1)S(1)} collective-permute-done((f16[32,128,128]{2,1,0:T(8,128)(2,1)S(1)}, f16[32,128,128]{2,1,0:T(8,128)(2,1)S(1)}, u32[]{:S(2)}, u32[]{:S(2)}) %collective-permute-start.4) | collective-permute-done | bytes 1048608 | tf_op jit(solution)/shard_map/scatter_row/ppermute | solution.py:108
  34.8 1.4 multiply_convert_fusion
  36.2 3.6 %all-to-all-done = bf16[16,2,128,128]{3,2,1,0:T(8,128)(2,1)S(1)} async-done(((bf16[16,2,128,128]{3,2,1,0:T(8,128)(2,1)}), bf16[16,2,128,128]{3,2,1,0:T(8,128)(2,1)S(1)}, u32[]{:S(2)}, u32[]{:S(2)}) %all-to-all-start) | async-done | bytes 1048608 | tf_op jit(solution)/shard_map/gather_row/all_to_all | solution.py:127
  39.7 4.3 %collective-permute-start.5 = (bf16[32,128,128]{2,1,0:T(8,128)(2,1)S(1)}, bf16[32,128,128]{2,1,0:T(8,128)(2,1)S(1)}, u32[]{:S(2)}, u32[]{:S(2)}) collective-permute-start(bf16[32,128,128]{2,1,0:T(8,128)(2,1)S(1)} %bitcast.73), channel_id=1, source_target_pairs={{0,8},{8,0},{1,9},{9,1},{2,10},{10,2},{3,11},{11,3},{4,12},{12,4},... | collective-permute-start | bytes 3145736 | tf_op jit(solution)/shard_map/gather_row/ppermute | solution.py:108
  44.0 3.7 %all-to-all-start.1 = ((f16[16,256,128]{2,1,0:T(8,128)(2,1)}), f16[16,256,128]{2,1,0:T(8,128)(2,1)S(1)}, u32[]{:S(2)}, u32[]{:S(2)}) async-start(f16[16,256,128]{2,1,0:T(8,128)(2,1)} %bitcast.83), calls=%async_computation.1 | async-start | bytes 2097152 | tf_op jit(solution)/shard_map/scatter_row/all_to_all | solution.py:141
  47.7 2.9 %behind.2 = (f32[4,128,128]{2,1,0:T(8,128)S(1)}, f32[4,128,128]{2,1,0:T(8,128)S(1)}, f32[4,128,128]{2,1,0:T(8,128)S(1)}, f32[4,128,128]{2,1,0:T(8,128)S(1)}) custom-call(s32[96]{0:T(128)S(1)} %get-tuple-element.104.src_ref, s32[96]{0:T(128)S(1)} %get-tuple-element.103.slot_ref, s32[1]{0:T(128)} %bitcast.68.count_ref, bf16[32,128,128]{2,1,0:T(8,128)(2,1)S(1)} %bitcast.74, ...), custom_call_target="tpu_custom_call" | custom-call | flops 3221225472 | bytes 3145728 | tf_op jit(solution)/shard_map/behind/behind/pallas_call | solution.py:85
  50.6 1.2 collective-permute-start.6
  51.9 3.8 %collective-permute-start.7 = (f16[4,128,128]{2,1,0:T(8,128)(2,1)S(1)}, f16[4,128,128]{2,1,0:T(8,128)(2,1)S(1)}, u32[]{:S(2)}, u32[]{:S(2)}) collective-permute-start(f16[4,128,128]{2,1,0:T(8,128)(2,1)S(1)} %multiply_convert_fusion.3), channel_id=1, source_target_pairs={{0,2},{1,3},{2,0},{3,1},{4,6},{5,7},{6,4},{7,5},{8,10},{9,11},{10,... | collective-permute-start | bytes 393224 | tf_op jit(solution)/shard_map/scatter_col/ppermute | solution.py:108
  55.7 0.1 collective-permute-start.8
  55.8 6.2 %collective-permute-done.7 = f16[4,128,128]{2,1,0:T(8,128)(2,1)S(1)} collective-permute-done((f16[4,128,128]{2,1,0:T(8,128)(2,1)S(1)}, f16[4,128,128]{2,1,0:T(8,128)(2,1)S(1)}, u32[]{:S(2)}, u32[]{:S(2)}) %collective-permute-start.7) | collective-permute-done | bytes 131104 | tf_op jit(solution)/shard_map/scatter_col/ppermute | solution.py:108
  62.1 2.8 %collective-permute-done.8 = f16[4,128,128]{2,1,0:T(8,128)(2,1)S(1)} collective-permute-done((f16[4,128,128]{2,1,0:T(8,128)(2,1)S(1)}, f16[4,128,128]{2,1,0:T(8,128)(2,1)S(1)}, u32[]{:S(2)}, u32[]{:S(2)}) %collective-permute-start.8) | collective-permute-done | bytes 131104 | tf_op jit(solution)/shard_map/scatter_col/ppermute | solution.py:108
  64.9 0.1 multiply_add_fusion
  65.0 2.2 %collective-permute-start.9 = (f16[2,128,128]{2,1,0:T(8,128)(2,1)S(1)}, f16[2,128,128]{2,1,0:T(8,128)(2,1)S(1)}, u32[]{:S(2)}, u32[]{:S(2)}) collective-permute-start(f16[2,128,128]{2,1,0:T(8,128)(2,1)S(1)} %get-tuple-element.102), channel_id=1, source_target_pairs={{0,4},{4,0},{1,5},{5,1},{2,6},{6,2},{3,7},{7,3},{8,12},{12,8},{9,1... | collective-permute-start | bytes 196616 | tf_op jit(solution)/shard_map/scatter_col/ppermute | solution.py:108
  67.3 8.5 %collective-permute-done.9 = f16[2,128,128]{2,1,0:T(8,128)(2,1)S(1)} collective-permute-done((f16[2,128,128]{2,1,0:T(8,128)(2,1)S(1)}, f16[2,128,128]{2,1,0:T(8,128)(2,1)S(1)}, u32[]{:S(2)}, u32[]{:S(2)}) %collective-permute-start.9) | collective-permute-done | bytes 65568 | tf_op jit(solution)/shard_map/scatter_col/ppermute | solution.py:108
  75.8 0.2 multiply_reduce_fusion
  76.0 0.1 broadcast_in_dim.15.inverse_ref
  76.2 1.5 middle.1
  77.7 1.2 collective-permute-start.11
  78.9 1.7 %collective-permute-start.10 = (bf16[2,128,128]{2,1,0:T(8,128)(2,1)S(1)}, bf16[2,128,128]{2,1,0:T(8,128)(2,1)S(1)}, u32[]{:S(2)}, u32[]{:S(2)}) collective-permute-start(bf16[2,128,128]{2,1,0:T(8,128)(2,1)S(1)} %bitcast.79), channel_id=1, source_target_pairs={{0,4},{4,0},{1,5},{5,1},{2,6},{6,2},{3,7},{7,3},{8,12},{12,8},{9,1... | collective-permute-start | bytes 196616 | tf_op jit(solution)/shard_map/gather_col/ppermute | solution.py:108
  80.7 5.2 %all-to-all-start.2 = ((bf16[16,2,128,128]{3,2,1,0:T(8,128)(2,1)}), bf16[16,2,128,128]{3,2,1,0:T(8,128)(2,1)S(1)}, u32[]{:S(2)}, u32[]{:S(2)}) async-start(bf16[16,2,128,128]{3,2,1,0:T(8,128)(2,1)} %get-tuple-element.62), calls=%async_computation.2 | async-start | bytes 2097152 | tf_op jit(solution)/shard_map/gather_row/all_to_all | solution.py:127
  85.9 1.2 collective-permute-start.12
  87.1 2.6 %collective-permute-start.13 = (bf16[2,2,128,128]{3,2,1,0:T(8,128)(2,1)S(1)}, bf16[2,2,128,128]{3,2,1,0:T(8,128)(2,1)S(1)}, u32[]{:S(2)}, u32[]{:S(2)}) collective-permute-start(bf16[2,2,128,128]{3,2,1,0:T(8,128)(2,1)S(1)} %pad_maximum_fusion.2.f0), channel_id=1, source_target_pairs={{0,2},{1,3},{2,0},{3,1},{4,6},{5,7},{6,4},{7,5},{8,10},{9,11},{10,... | collective-permute-start | bytes 393224 | tf_op jit(solution)/shard_map/gather_col/ppermute | solution.py:108
  89.7 0.1 collective-permute-start.14
  89.8 1.7 %collective-permute-start.15 = (f32[136,128]{1,0:T(8,128)S(1)}, f32[136,128]{1,0:T(8,128)S(1)}, u32[]{:S(2)}, u32[]{:S(2)}) collective-permute-start(f32[136,128]{1,0:T(8,128)S(1)} %bitcast_add_fusion.2), channel_id=1, source_target_pairs={{0,4},{4,0},{1,5},{5,1},{2,6},{6,2},{3,7},{7,3},{8,12},{12,8},{9,1... | collective-permute-start | bytes 208904 | tf_op jit(solution)/shard_map/gather_col/weights/ppermute | solution.py:108
  91.6 3.2 %collective-permute-done.15 = f32[136,128]{1,0:T(8,128)S(1)} collective-permute-done((f32[136,128]{1,0:T(8,128)S(1)}, f32[136,128]{1,0:T(8,128)S(1)}, u32[]{:S(2)}, u32[]{:S(2)}) %collective-permute-start.15) | collective-permute-done | bytes 69664 | tf_op jit(solution)/shard_map/gather_col/weights/ppermute | solution.py:108
  94.8 0.6 collective-permute-done.13.f2
  95.4 2.5 %collective-permute-done.14.f3 = bf16[2,2,128,128]{3,2,1,0:T(8,128)(2,1)S(1)} collective-permute-done((bf16[2,2,128,128]{3,2,1,0:T(8,128)(2,1)S(1)}, bf16[2,2,128,128]{3,2,1,0:T(8,128)(2,1)S(1)}, u32[]{:S(2)}, u32[]{:S(2)}) %collective-permute-start.14) | collective-permute-done | bytes 131104 | tf_op jit(solution)/shard_map/gather_col/ppermute | solution.py:108
  98.0 2.8 %ahead.3 = (f32[32,128,128]{2,1,0:T(8,128)S(1)}, bf16[32,128,128]{2,1,0:T(8,128)(2,1)S(1)}) custom-call(s32[96]{0:T(128)S(1)} %get-tuple-element.104.src_ref, s32[96]{0:T(128)S(1)} %get-tuple-element.103.slot_ref, s32[1]{0:T(128)} %bitcast.69.count_ref, bf16[2,2,128,128]{3,2,1,0:T(8,128)(2,1)S(1)} %pad_maximum_fusion.2.f0, ...), custom_call_target="tpu_custom_call" | custom-call | flops 3221225472 | bytes 3145728 | tf_op jit(solution)/shard_map/ahead/ahead/pallas_call | solution.py:85
  100.8 2.0 %collective-permute-start.17 = (bf16[32,128,128]{2,1,0:T(8,128)(2,1)S(1)}, bf16[32,128,128]{2,1,0:T(8,128)(2,1)S(1)}, u32[]{:S(2)}, u32[]{:S(2)}) collective-permute-start(bf16[32,128,128]{2,1,0:T(8,128)(2,1)S(1)} %get-tuple-element.77), channel_id=1, source_target_pairs={{0,8},{8,0},{1,9},{9,1},{2,10},{10,2},{3,11},{11,3},{4,12},{12,4},... | collective-permute-start | bytes 3145736 | tf_op jit(solution)/shard_map/scatter_row/ppermute | solution.py:108
  102.8 4.7 %collective-permute-start.16 = (f32[136,128]{1,0:T(8,128)S(1)}, f32[136,128]{1,0:T(8,128)S(1)}, u32[]{:S(2)}, u32[]{:S(2)}) collective-permute-start(f32[136,128]{1,0:T(8,128)S(1)} %add.119), channel_id=1, source_target_pairs={{0,128},{32,160},{64,192},{96,224},{128,0},{160,32},{192,64},{224,... | collective-permute-start | bytes 208904 | tf_op jit(solution)/shard_map/weights/ppermute | solution.py:108
  107.4 8.4 %collective-permute-done.16 = f32[136,128]{1,0:T(8,128)S(1)} collective-permute-done((f32[136,128]{1,0:T(8,128)S(1)}, f32[136,128]{1,0:T(8,128)S(1)}, u32[]{:S(2)}, u32[]{:S(2)}) %collective-permute-start.16) | collective-permute-done | bytes 69664 | tf_op jit(solution)/shard_map/weights/ppermute | solution.py:108
  115.8 1.3 add_convert_fusion
  117.2 1.8 %collective-permute-start.18 = (bf16[32,128,128]{2,1,0:T(8,128)(2,1)S(1)}, bf16[32,128,128]{2,1,0:T(8,128)(2,1)S(1)}, u32[]{:S(2)}, u32[]{:S(2)}) collective-permute-start(bf16[32,128,128]{2,1,0:T(8,128)(2,1)S(1)} %bitcast.71), channel_id=1, source_target_pairs={{0,8},{8,0},{1,9},{9,1},{2,10},{10,2},{3,11},{11,3},{4,12},{12,4},... | collective-permute-start | bytes 3145736 | tf_op jit(solution)/shard_map/gather_row/ppermute | solution.py:108
  118.9 3.7 %all-to-all-start.3 = ((bf16[16,256,128]{2,1,0:T(8,128)(2,1)}), bf16[16,256,128]{2,1,0:T(8,128)(2,1)S(1)}, u32[]{:S(2)}, u32[]{:S(2)}) async-start(bf16[16,256,128]{2,1,0:T(8,128)(2,1)} %bitcast.82), calls=%async_computation.3 | async-start | bytes 2097152 | tf_op jit(solution)/shard_map/scatter_row/all_to_all | solution.py:141
  122.6 1.3 collective-permute-start.19
  123.9 2.8 %behind.3 = (f32[4,128,128]{2,1,0:T(8,128)S(1)}, bf16[4,128,128]{2,1,0:T(8,128)(2,1)S(1)}, bf16[4,128,128]{2,1,0:T(8,128)(2,1)S(1)}, bf16[4,128,128]{2,1,0:T(8,128)(2,1)S(1)}) custom-call(s32[96]{0:T(128)S(1)} %get-tuple-element.104.src_ref, s32[96]{0:T(128)S(1)} %get-tuple-element.103.slot_ref, s32[1]{0:T(128)} %bitcast.70.count_ref, ...), custom_call_target="tpu_custom_call" | custom-call | flops 3221225472 | bytes 3145728 | tf_op jit(solution)/shard_map/behind/behind/pallas_call | solution.py:85
  126.8 0.9 collective-permute-done.19
  127.7 1.2 collective-permute-start.23
  128.8 2.7 %collective-permute-start.24 = (f32[136,128]{1,0:T(8,128)S(1)}, f32[136,128]{1,0:T(8,128)S(1)}, u32[]{:S(2)}, u32[]{:S(2)}) collective-permute-start(f32[136,128]{1,0:T(8,128)S(1)} %add.122), channel_id=1, source_target_pairs={{0,2},{1,3},{2,0},{3,1},{4,6},{5,7},{6,4},{7,5},{8,10},{9,11},{10,... | collective-permute-start | bytes 208904 | tf_op jit(solution)/shard_map/scatter_col/weights/ppermute | solution.py:108
  131.5 0.1 collective-permute-start.25
  131.6 3.8 %collective-permute-start.21 = (bf16[4,128,128]{2,1,0:T(8,128)(2,1)S(1)}, bf16[4,128,128]{2,1,0:T(8,128)(2,1)S(1)}, u32[]{:S(2)}, u32[]{:S(2)}) collective-permute-start(bf16[4,128,128]{2,1,0:T(8,128)(2,1)S(1)} %get-tuple-element.89), channel_id=1, source_target_pairs={{0,2},{1,3},{2,0},{3,1},{4,6},{5,7},{6,4},{7,5},{8,10},{9,11},{10,... | collective-permute-start | bytes 393224 | tf_op jit(solution)/shard_map/scatter_col/ppermute | solution.py:108
  135.5 1.0 collective-permute-done.25
  136.5 3.2 %collective-permute-done.21 = bf16[4,128,128]{2,1,0:T(8,128)(2,1)S(1)} collective-permute-done((bf16[4,128,128]{2,1,0:T(8,128)(2,1)S(1)}, bf16[4,128,128]{2,1,0:T(8,128)(2,1)S(1)}, u32[]{:S(2)}, u32[]{:S(2)}) %collective-permute-start.21) | collective-permute-done | bytes 131104 | tf_op jit(solution)/shard_map/scatter_col/ppermute | solution.py:108
  139.7 2.9 %collective-permute-done.22 = bf16[4,128,128]{2,1,0:T(8,128)(2,1)S(1)} collective-permute-done((bf16[4,128,128]{2,1,0:T(8,128)(2,1)S(1)}, bf16[4,128,128]{2,1,0:T(8,128)(2,1)S(1)}, u32[]{:S(2)}, u32[]{:S(2)}) %collective-permute-start.22) | collective-permute-done | bytes 131104 | tf_op jit(solution)/shard_map/scatter_col/ppermute | solution.py:108
  142.6 1.2 collective-permute-start.27
  143.8 2.3 %collective-permute-start.28 = (f32[136,128]{1,0:T(8,128)S(1)}, f32[136,128]{1,0:T(8,128)S(1)}, u32[]{:S(2)}, u32[]{:S(2)}) collective-permute-start(f32[136,128]{1,0:T(8,128)S(1)} %add_add_fusion.1), channel_id=1, source_target_pairs={{0,64},{32,96},{64,0},{96,32},{128,192},{160,224},{192,128},{224,1... | collective-permute-start | bytes 208904 | tf_op jit(solution)/shard_map/weights/ppermute | solution.py:108
  146.1 0.2 collective-permute-start.29
  146.3 3.6 %collective-permute-start.26 = (bf16[2,128,128]{2,1,0:T(8,128)(2,1)S(1)}, bf16[2,128,128]{2,1,0:T(8,128)(2,1)S(1)}, u32[]{:S(2)}, u32[]{:S(2)}) collective-permute-start(bf16[2,128,128]{2,1,0:T(8,128)(2,1)S(1)} %slice.24), channel_id=1, source_target_pairs={{0,4},{4,0},{1,5},{5,1},{2,6},{6,2},{3,7},{7,3},{8,12},{12,8},{9,1... | collective-permute-start | bytes 196616 | tf_op jit(solution)/shard_map/scatter_col/ppermute | solution.py:108
  149.9 4.0 %collective-permute-done.29 = f32[136,128]{1,0:T(8,128)S(1)} collective-permute-done((f32[136,128]{1,0:T(8,128)S(1)}, f32[136,128]{1,0:T(8,128)S(1)}, u32[]{:S(2)}, u32[]{:S(2)}) %collective-permute-start.29) | collective-permute-done | bytes 69664 | tf_op jit(solution)/shard_map/weights/ppermute | solution.py:108
  153.9 1.0 collective-permute-start.30
  155.0 0.9 collective-permute-done.30
  155.9 0.8 final.1
  (58 shorter events, 0.6 us)
Async XLA Ops:
  0.6 18.8 %copy-start.8 = (s32[1,1,96]{2,1,0:T(1,128)S(1)}, s32[1,1,96]{2,1,0:T(1,128)}, u32[]{:S(2)}) copy-start(s32[1,1,96]{2,1,0:T(1,128)} %param.12) | copy-start | bytes 1156
  0.6 18.8 %copy-start.7 = (s32[1,1,96]{2,1,0:T(1,128)S(1)}, s32[1,1,96]{2,1,0:T(1,128)}, u32[]{:S(2)}) copy-start(s32[1,1,96]{2,1,0:T(1,128)} %param.13) | copy-start | bytes 1156
  0.7 14.7 %collective-permute-start = (bf16[2,128,128]{2,1,0:T(8,128)(2,1)}, bf16[2,128,128]{2,1,0:T(8,128)(2,1)S(1)}, u32[]{:S(2)}, u32[]{:S(2)}) collective-permute-start(bf16[2,128,128]{2,1,0:T(8,128)(2,1)} %bitcast.75), channel_id=1, source_target_pairs={{0,4},{4,0},{1,5},{5,1},{2,6},{6,2},{3,7},{7,3},{8,12},{12,8},{9,1... | collective-permute-start | bytes 196616 | tf_op jit(solution)/shard_map/gather_col/ppermute | solution.py:108
  4.3 0.9 copy-start
  5.2 10.2 %copy-start.1 = (bf16[256,128]{1,0:T(8,128)(2,1)S(1)}, bf16[256,128]{1,0:T(8,128)(2,1)}, u32[]{:S(2)}) copy-start(bf16[256,128]{1,0:T(8,128)(2,1)} %features_ref.3) | copy-start | bytes 196612
  6.4 33.4 %all-to-all-start = ((bf16[16,2,128,128]{3,2,1,0:T(8,128)(2,1)}), bf16[16,2,128,128]{3,2,1,0:T(8,128)(2,1)S(1)}, u32[]{:S(2)}, u32[]{:S(2)}) async-start(bf16[16,2,128,128]{3,2,1,0:T(8,128)(2,1)} %prepare.1), calls=%async_computation | async-start | bytes 2097152 | tf_op jit(solution)/shard_map/gather_row/all_to_all | solution.py:127
  15.4 4.2 %collective-permute-start.1 = (bf16[2,2,128,128]{3,2,1,0:T(8,128)(2,1)S(1)}, bf16[2,2,128,128]{3,2,1,0:T(8,128)(2,1)S(1)}, u32[]{:S(2)}, u32[]{:S(2)}) collective-permute-start(bf16[2,2,128,128]{3,2,1,0:T(8,128)(2,1)S(1)} %pad_maximum_fusion.1.f0), channel_id=1, source_target_pairs={{0,1},{1,0},{2,3},{3,2},{4,5},{5,4},{6,7},{7,6},{8,9},{9,8},{10,11... | collective-permute-start | bytes 393224 | tf_op jit(solution)/shard_map/gather_col/ppermute | solution.py:108
  16.8 7.6 %collective-permute-start.2 = (bf16[2,2,128,128]{3,2,1,0:T(8,128)(2,1)S(1)}, bf16[2,2,128,128]{3,2,1,0:T(8,128)(2,1)S(1)}, u32[]{:S(2)}, u32[]{:S(2)}) collective-permute-start(bf16[2,2,128,128]{3,2,1,0:T(8,128)(2,1)S(1)} %pad_maximum_fusion.1.f0), channel_id=1, source_target_pairs={{0,2},{1,3},{2,0},{3,1},{4,6},{5,7},{6,4},{7,5},{8,10},{9,11},{10,... | collective-permute-start | bytes 393224 | tf_op jit(solution)/shard_map/gather_col/ppermute | solution.py:108
  19.4 7.6 %collective-permute-start.3 = (bf16[2,2,128,128]{3,2,1,0:T(8,128)(2,1)S(1)}, bf16[2,2,128,128]{3,2,1,0:T(8,128)(2,1)S(1)}, u32[]{:S(2)}, u32[]{:S(2)}) collective-permute-start(bf16[2,2,128,128]{3,2,1,0:T(8,128)(2,1)S(1)} %pad_maximum_fusion.1.f0), channel_id=1, source_target_pairs={{0,3},{1,2},{2,1},{3,0},{4,7},{5,6},{6,5},{7,4},{8,11},{9,10},{10,... | collective-permute-start | bytes 393224 | tf_op jit(solution)/shard_map/gather_col/ppermute | solution.py:108
  30.2 4.6 %collective-permute-start.4 = (f16[32,128,128]{2,1,0:T(8,128)(2,1)S(1)}, f16[32,128,128]{2,1,0:T(8,128)(2,1)S(1)}, u32[]{:S(2)}, u32[]{:S(2)}) collective-permute-start(f16[32,128,128]{2,1,0:T(8,128)(2,1)S(1)} %multiply_convert_fusion.1), channel_id=1, source_target_pairs={{0,8},{8,0},{1,9},{9,1},{2,10},{10,2},{3,11},{11,3},{4,12},{12,4},... | collective-permute-start | bytes 3145736 | tf_op jit(solution)/shard_map/scatter_row/ppermute | solution.py:108
  39.7 7.9 %collective-permute-start.5 = (bf16[32,128,128]{2,1,0:T(8,128)(2,1)S(1)}, bf16[32,128,128]{2,1,0:T(8,128)(2,1)S(1)}, u32[]{:S(2)}, u32[]{:S(2)}) collective-permute-start(bf16[32,128,128]{2,1,0:T(8,128)(2,1)S(1)} %bitcast.73), channel_id=1, source_target_pairs={{0,8},{8,0},{1,9},{9,1},{2,10},{10,2},{3,11},{11,3},{4,12},{12,4},... | collective-permute-start | bytes 3145736 | tf_op jit(solution)/shard_map/gather_row/ppermute | solution.py:108
  44.0 31.8 %all-to-all-start.1 = ((f16[16,256,128]{2,1,0:T(8,128)(2,1)}), f16[16,256,128]{2,1,0:T(8,128)(2,1)S(1)}, u32[]{:S(2)}, u32[]{:S(2)}) async-start(f16[16,256,128]{2,1,0:T(8,128)(2,1)} %bitcast.83), calls=%async_computation.1 | async-start | bytes 2097152 | tf_op jit(solution)/shard_map/scatter_row/all_to_all | solution.py:141
  50.6 16.7 %copy-start.6 = (s32[256]{0:T(256)S(1)}, s32[256]{0:T(256)}, u32[]{:S(2)}) copy-start(s32[256]{0:T(256)} %param.15) | copy-start | bytes 3076
  50.6 5.2 %collective-permute-start.6 = (f16[4,128,128]{2,1,0:T(8,128)(2,1)S(1)}, f16[4,128,128]{2,1,0:T(8,128)(2,1)S(1)}, u32[]{:S(2)}, u32[]{:S(2)}) collective-permute-start(f16[4,128,128]{2,1,0:T(8,128)(2,1)S(1)} %multiply_convert_fusion.4), channel_id=1, source_target_pairs={{0,1},{1,0},{2,3},{3,2},{4,5},{5,4},{6,7},{7,6},{8,9},{9,8},{10,11... | collective-permute-start | bytes 393224 | tf_op jit(solution)/shard_map/scatter_col/ppermute | solution.py:108
  51.9 24.3 %copy-start.2 = (bf16[256,128]{1,0:T(8,128)(2,1)S(1)}, bf16[256,128]{1,0:T(8,128)(2,1)}, u32[]{:S(2)}) copy-start(bf16[256,128]{1,0:T(8,128)(2,1)} %upstream_ref.1) | copy-start | bytes 196612
  51.9 24.3 %copy-start.3 = (bf16[128,128]{1,0:T(8,128)(2,1)S(1)}, bf16[128,128]{1,0:T(8,128)(2,1)}, u32[]{:S(2)}) copy-start(bf16[128,128]{1,0:T(8,128)(2,1)} %w_self_ref.1) | copy-start | bytes 98308
  51.9 24.3 %copy-start.4 = (bf16[128,128]{1,0:T(8,128)(2,1)S(1)}, bf16[128,128]{1,0:T(8,128)(2,1)}, u32[]{:S(2)}) copy-start(bf16[128,128]{1,0:T(8,128)(2,1)} %w_neigh_ref.1) | copy-start | bytes 98308
  51.9 24.3 %copy-start.5 = (f32[128]{0:T(128)S(1)}, f32[128]{0:T(128)}, u32[]{:S(2)}) copy-start(f32[128]{0:T(128)} %param.18) | copy-start | bytes 1540
  51.9 10.2 %collective-permute-start.7 = (f16[4,128,128]{2,1,0:T(8,128)(2,1)S(1)}, f16[4,128,128]{2,1,0:T(8,128)(2,1)S(1)}, u32[]{:S(2)}, u32[]{:S(2)}) collective-permute-start(f16[4,128,128]{2,1,0:T(8,128)(2,1)S(1)} %multiply_convert_fusion.3), channel_id=1, source_target_pairs={{0,2},{1,3},{2,0},{3,1},{4,6},{5,7},{6,4},{7,5},{8,10},{9,11},{10,... | collective-permute-start | bytes 393224 | tf_op jit(solution)/shard_map/scatter_col/ppermute | solution.py:108
  55.7 9.1 %collective-permute-start.8 = (f16[4,128,128]{2,1,0:T(8,128)(2,1)S(1)}, f16[4,128,128]{2,1,0:T(8,128)(2,1)S(1)}, u32[]{:S(2)}, u32[]{:S(2)}) collective-permute-start(f16[4,128,128]{2,1,0:T(8,128)(2,1)S(1)} %multiply_convert_fusion.2), channel_id=1, source_target_pairs={{0,3},{1,2},{2,1},{3,0},{4,7},{5,6},{6,5},{7,4},{8,11},{9,10},{10,... | collective-permute-start | bytes 393224 | tf_op jit(solution)/shard_map/scatter_col/ppermute | solution.py:108
  65.0 10.8 %collective-permute-start.9 = (f16[2,128,128]{2,1,0:T(8,128)(2,1)S(1)}, f16[2,128,128]{2,1,0:T(8,128)(2,1)S(1)}, u32[]{:S(2)}, u32[]{:S(2)}) collective-permute-start(f16[2,128,128]{2,1,0:T(8,128)(2,1)S(1)} %get-tuple-element.102), channel_id=1, source_target_pairs={{0,4},{4,0},{1,5},{5,1},{2,6},{6,2},{3,7},{7,3},{8,12},{12,8},{9,1... | collective-permute-start | bytes 196616 | tf_op jit(solution)/shard_map/scatter_col/ppermute | solution.py:108
  77.7 8.1 %collective-permute-start.11 = (f32[136,128]{1,0:T(8,128)S(1)}, f32[136,128]{1,0:T(8,128)S(1)}, u32[]{:S(2)}, u32[]{:S(2)}) collective-permute-start(f32[136,128]{1,0:T(8,128)S(1)} %dynamic-slice_bitcast_fusion), channel_id=1, source_target_pairs={{0,8},{8,0},{1,9},{9,1},{2,10},{10,2},{3,11},{11,3},{4,12},{12,4},... | collective-permute-start | bytes 208904 | tf_op jit(solution)/shard_map/gather_col/weights/ppermute | solution.py:108
  78.9 6.9 %collective-permute-start.10 = (bf16[2,128,128]{2,1,0:T(8,128)(2,1)S(1)}, bf16[2,128,128]{2,1,0:T(8,128)(2,1)S(1)}, u32[]{:S(2)}, u32[]{:S(2)}) collective-permute-start(bf16[2,128,128]{2,1,0:T(8,128)(2,1)S(1)} %bitcast.79), channel_id=1, source_target_pairs={{0,4},{4,0},{1,5},{5,1},{2,6},{6,2},{3,7},{7,3},{8,12},{12,8},{9,1... | collective-permute-start | bytes 196616 | tf_op jit(solution)/shard_map/gather_col/ppermute | solution.py:108
  80.7 36.5 %all-to-all-start.2 = ((bf16[16,2,128,128]{3,2,1,0:T(8,128)(2,1)}), bf16[16,2,128,128]{3,2,1,0:T(8,128)(2,1)S(1)}, u32[]{:S(2)}, u32[]{:S(2)}) async-start(bf16[16,2,128,128]{3,2,1,0:T(8,128)(2,1)} %get-tuple-element.62), calls=%async_computation.2 | async-start | bytes 2097152 | tf_op jit(solution)/shard_map/gather_row/all_to_all | solution.py:127
  85.9 8.9 %collective-permute-start.12 = (bf16[2,2,128,128]{3,2,1,0:T(8,128)(2,1)S(1)}, bf16[2,2,128,128]{3,2,1,0:T(8,128)(2,1)S(1)}, u32[]{:S(2)}, u32[]{:S(2)}) collective-permute-start(bf16[2,2,128,128]{3,2,1,0:T(8,128)(2,1)S(1)} %pad_maximum_fusion.2.f0), channel_id=1, source_target_pairs={{0,1},{1,0},{2,3},{3,2},{4,5},{5,4},{6,7},{7,6},{8,9},{9,8},{10,11... | collective-permute-start | bytes 393224 | tf_op jit(solution)/shard_map/gather_col/ppermute | solution.py:108
  87.1 8.4 %collective-permute-start.13 = (bf16[2,2,128,128]{3,2,1,0:T(8,128)(2,1)S(1)}, bf16[2,2,128,128]{3,2,1,0:T(8,128)(2,1)S(1)}, u32[]{:S(2)}, u32[]{:S(2)}) collective-permute-start(bf16[2,2,128,128]{3,2,1,0:T(8,128)(2,1)S(1)} %pad_maximum_fusion.2.f0), channel_id=1, source_target_pairs={{0,2},{1,3},{2,0},{3,1},{4,6},{5,7},{6,4},{7,5},{8,10},{9,11},{10,... | collective-permute-start | bytes 393224 | tf_op jit(solution)/shard_map/gather_col/ppermute | solution.py:108
  89.7 8.3 %collective-permute-start.14 = (bf16[2,2,128,128]{3,2,1,0:T(8,128)(2,1)S(1)}, bf16[2,2,128,128]{3,2,1,0:T(8,128)(2,1)S(1)}, u32[]{:S(2)}, u32[]{:S(2)}) collective-permute-start(bf16[2,2,128,128]{3,2,1,0:T(8,128)(2,1)S(1)} %pad_maximum_fusion.2.f0), channel_id=1, source_target_pairs={{0,3},{1,2},{2,1},{3,0},{4,7},{5,6},{6,5},{7,4},{8,11},{9,10},{10,... | collective-permute-start | bytes 393224 | tf_op jit(solution)/shard_map/gather_col/ppermute | solution.py:108
  89.8 5.0 %collective-permute-start.15 = (f32[136,128]{1,0:T(8,128)S(1)}, f32[136,128]{1,0:T(8,128)S(1)}, u32[]{:S(2)}, u32[]{:S(2)}) collective-permute-start(f32[136,128]{1,0:T(8,128)S(1)} %bitcast_add_fusion.2), channel_id=1, source_target_pairs={{0,4},{4,0},{1,5},{5,1},{2,6},{6,2},{3,7},{7,3},{8,12},{12,8},{9,1... | collective-permute-start | bytes 208904 | tf_op jit(solution)/shard_map/gather_col/weights/ppermute | solution.py:108
  100.8 15.0 %collective-permute-start.17 = (bf16[32,128,128]{2,1,0:T(8,128)(2,1)S(1)}, bf16[32,128,128]{2,1,0:T(8,128)(2,1)S(1)}, u32[]{:S(2)}, u32[]{:S(2)}) collective-permute-start(bf16[32,128,128]{2,1,0:T(8,128)(2,1)S(1)} %get-tuple-element.77), channel_id=1, source_target_pairs={{0,8},{8,0},{1,9},{9,1},{2,10},{10,2},{3,11},{11,3},{4,12},{12,4},... | collective-permute-start | bytes 3145736 | tf_op jit(solution)/shard_map/scatter_row/ppermute | solution.py:108
  102.8 13.1 %collective-permute-start.16 = (f32[136,128]{1,0:T(8,128)S(1)}, f32[136,128]{1,0:T(8,128)S(1)}, u32[]{:S(2)}, u32[]{:S(2)}) collective-permute-start(f32[136,128]{1,0:T(8,128)S(1)} %add.119), channel_id=1, source_target_pairs={{0,128},{32,160},{64,192},{96,224},{128,0},{160,32},{192,64},{224,... | collective-permute-start | bytes 208904 | tf_op jit(solution)/shard_map/weights/ppermute | solution.py:108
  117.2 5.4 %collective-permute-start.18 = (bf16[32,128,128]{2,1,0:T(8,128)(2,1)S(1)}, bf16[32,128,128]{2,1,0:T(8,128)(2,1)S(1)}, u32[]{:S(2)}, u32[]{:S(2)}) collective-permute-start(bf16[32,128,128]{2,1,0:T(8,128)(2,1)S(1)} %bitcast.71), channel_id=1, source_target_pairs={{0,8},{8,0},{1,9},{9,1},{2,10},{10,2},{3,11},{11,3},{4,12},{12,4},... | collective-permute-start | bytes 3145736 | tf_op jit(solution)/shard_map/gather_row/ppermute | solution.py:108
  118.9 36.9 %all-to-all-start.3 = ((bf16[16,256,128]{2,1,0:T(8,128)(2,1)}), bf16[16,256,128]{2,1,0:T(8,128)(2,1)S(1)}, u32[]{:S(2)}, u32[]{:S(2)}) async-start(bf16[16,256,128]{2,1,0:T(8,128)(2,1)} %bitcast.82), calls=%async_computation.3 | async-start | bytes 2097152 | tf_op jit(solution)/shard_map/scatter_row/all_to_all | solution.py:141
  122.6 5.0 %collective-permute-start.19 = (f32[136,128]{1,0:T(8,128)S(1)}, f32[136,128]{1,0:T(8,128)S(1)}, u32[]{:S(2)}, u32[]{:S(2)}) collective-permute-start(f32[136,128]{1,0:T(8,128)S(1)} %add.120), channel_id=1, source_target_pairs={{0,16},{16,0},{1,17},{17,1},{2,18},{18,2},{3,19},{19,3},{4,20},{20... | collective-permute-start | bytes 208904 | tf_op jit(solution)/shard_map/behind/weights/ppermute | solution.py:108
  127.7 7.7 %collective-permute-start.23 = (f32[136,128]{1,0:T(8,128)S(1)}, f32[136,128]{1,0:T(8,128)S(1)}, u32[]{:S(2)}, u32[]{:S(2)}) collective-permute-start(f32[136,128]{1,0:T(8,128)S(1)} %add.122), channel_id=1, source_target_pairs={{0,1},{1,0},{2,3},{3,2},{4,5},{5,4},{6,7},{7,6},{8,9},{9,8},{10,11... | collective-permute-start | bytes 208904 | tf_op jit(solution)/shard_map/scatter_col/weights/ppermute | solution.py:108
  128.8 6.6 %collective-permute-start.24 = (f32[136,128]{1,0:T(8,128)S(1)}, f32[136,128]{1,0:T(8,128)S(1)}, u32[]{:S(2)}, u32[]{:S(2)}) collective-permute-start(f32[136,128]{1,0:T(8,128)S(1)} %add.122), channel_id=1, source_target_pairs={{0,2},{1,3},{2,0},{3,1},{4,6},{5,7},{6,4},{7,5},{8,10},{9,11},{10,... | collective-permute-start | bytes 208904 | tf_op jit(solution)/shard_map/scatter_col/weights/ppermute | solution.py:108
  131.5 5.0 %collective-permute-start.25 = (f32[136,128]{1,0:T(8,128)S(1)}, f32[136,128]{1,0:T(8,128)S(1)}, u32[]{:S(2)}, u32[]{:S(2)}) collective-permute-start(f32[136,128]{1,0:T(8,128)S(1)} %add.122), channel_id=1, source_target_pairs={{0,3},{1,2},{2,1},{3,0},{4,7},{5,6},{6,5},{7,4},{8,11},{9,10},{10,... | collective-permute-start | bytes 208904 | tf_op jit(solution)/shard_map/scatter_col/weights/ppermute | solution.py:108
  131.6 4.9 %collective-permute-start.20 = (bf16[4,128,128]{2,1,0:T(8,128)(2,1)S(1)}, bf16[4,128,128]{2,1,0:T(8,128)(2,1)S(1)}, u32[]{:S(2)}, u32[]{:S(2)}) collective-permute-start(bf16[4,128,128]{2,1,0:T(8,128)(2,1)S(1)} %get-tuple-element.88), channel_id=1, source_target_pairs={{0,1},{1,0},{2,3},{3,2},{4,5},{5,4},{6,7},{7,6},{8,9},{9,8},{10,11... | collective-permute-start | bytes 393224 | tf_op jit(solution)/shard_map/scatter_col/ppermute | solution.py:108
  131.6 8.1 %collective-permute-start.21 = (bf16[4,128,128]{2,1,0:T(8,128)(2,1)S(1)}, bf16[4,128,128]{2,1,0:T(8,128)(2,1)S(1)}, u32[]{:S(2)}, u32[]{:S(2)}) collective-permute-start(bf16[4,128,128]{2,1,0:T(8,128)(2,1)S(1)} %get-tuple-element.89), channel_id=1, source_target_pairs={{0,2},{1,3},{2,0},{3,1},{4,6},{5,7},{6,4},{7,5},{8,10},{9,11},{10,... | collective-permute-start | bytes 393224 | tf_op jit(solution)/shard_map/scatter_col/ppermute | solution.py:108
  135.4 7.2 %collective-permute-start.22 = (bf16[4,128,128]{2,1,0:T(8,128)(2,1)S(1)}, bf16[4,128,128]{2,1,0:T(8,128)(2,1)S(1)}, u32[]{:S(2)}, u32[]{:S(2)}) collective-permute-start(bf16[4,128,128]{2,1,0:T(8,128)(2,1)S(1)} %get-tuple-element.90), channel_id=1, source_target_pairs={{0,3},{1,2},{2,1},{3,0},{4,7},{5,6},{6,5},{7,4},{8,11},{9,10},{10,... | collective-permute-start | bytes 393224 | tf_op jit(solution)/shard_map/scatter_col/ppermute | solution.py:108
  142.6 7.3 %collective-permute-start.27 = (f32[136,128]{1,0:T(8,128)S(1)}, f32[136,128]{1,0:T(8,128)S(1)}, u32[]{:S(2)}, u32[]{:S(2)}) collective-permute-start(f32[136,128]{1,0:T(8,128)S(1)} %add_add_fusion.1), channel_id=1, source_target_pairs={{0,32},{32,0},{64,96},{96,64},{128,160},{160,128},{192,224},{224,1... | collective-permute-start | bytes 208904 | tf_op jit(solution)/shard_map/weights/ppermute | solution.py:108
  143.8 6.1 %collective-permute-start.28 = (f32[136,128]{1,0:T(8,128)S(1)}, f32[136,128]{1,0:T(8,128)S(1)}, u32[]{:S(2)}, u32[]{:S(2)}) collective-permute-start(f32[136,128]{1,0:T(8,128)S(1)} %add_add_fusion.1), channel_id=1, source_target_pairs={{0,64},{32,96},{64,0},{96,32},{128,192},{160,224},{192,128},{224,1... | collective-permute-start | bytes 208904 | tf_op jit(solution)/shard_map/weights/ppermute | solution.py:108
  146.1 7.8 %collective-permute-start.29 = (f32[136,128]{1,0:T(8,128)S(1)}, f32[136,128]{1,0:T(8,128)S(1)}, u32[]{:S(2)}, u32[]{:S(2)}) collective-permute-start(f32[136,128]{1,0:T(8,128)S(1)} %add_add_fusion.1), channel_id=1, source_target_pairs={{0,96},{32,64},{64,32},{96,0},{128,224},{160,192},{192,160},{224,1... | collective-permute-start | bytes 208904 | tf_op jit(solution)/shard_map/weights/ppermute | solution.py:108
  146.3 7.7 %collective-permute-start.26 = (bf16[2,128,128]{2,1,0:T(8,128)(2,1)S(1)}, bf16[2,128,128]{2,1,0:T(8,128)(2,1)S(1)}, u32[]{:S(2)}, u32[]{:S(2)}) collective-permute-start(bf16[2,128,128]{2,1,0:T(8,128)(2,1)S(1)} %slice.24), channel_id=1, source_target_pairs={{0,4},{4,0},{1,5},{5,1},{2,6},{6,2},{3,7},{7,3},{8,12},{12,8},{9,1... | collective-permute-start | bytes 196616 | tf_op jit(solution)/shard_map/scatter_col/ppermute | solution.py:108
  153.9 1.9 %collective-permute-start.30 = (f32[136,128]{1,0:T(8,128)S(1)}, f32[136,128]{1,0:T(8,128)S(1)}, u32[]{:S(2)}, u32[]{:S(2)}) collective-permute-start(f32[136,128]{1,0:T(8,128)S(1)} %add_add_fusion), channel_id=1, source_target_pairs={{0,8},{8,0},{1,9},{9,1},{2,10},{10,2},{3,11},{11,3},{4,12},{12,4},... | collective-permute-start | bytes 208904 | tf_op jit(solution)/shard_map/weights/ppermute | solution.py:108

commit v4 on v3

--- a/solution.py
+++ b/solution.py
@@ -62,14 +62,14 @@
     keep_ref[...] = acc_ref[:32]
 
 
-def behind_kernel(src_ref, slot_ref, count_ref, g0, g1, tiles_hbm,
+def behind_kernel(src_ref, slot_ref, count_ref, g0, g1, g2, g3, tiles_hbm,
                   keep_ref, s1, s2, s3, field_ref, acc_ref, tiles_ref, sems):
     n = g0.shape[0]
 
     def prepare():
-        field_ref[:n] = g0[...]
-        field_ref[n : 2 * n] = g1[...]
-        field_ref[2 * n] = jnp.zeros_like(field_ref[2 * n])
+        for k, g in enumerate((g0, g1, g2, g3)):
+            field_ref[k * n : (k + 1) * n] = g[...]
+        field_ref[4 * n] = jnp.zeros_like(field_ref[4 * n])
 
     def product(t):
         return jnp.dot(field_ref[slot_ref[t]], tiles_ref[t], preferred_element_type=jnp.float32)
@@ -97,7 +97,7 @@
         ],
         compiler_params=pltpu.CompilerParams(vmem_limit_bytes=VMEM_LIMIT),
         cost_estimate=pl.CostEstimate(
-            flops=16 * n * TILE**3, bytes_accessed=n * TILE * TILE * 2, transcendentals=0
+            flops=(16 if name == "ahead" else 2) * n * TILE**3, bytes_accessed=n * TILE * TILE * 2, transcendentals=0
         ),
         name=name,
     )(src, slot, count, *parts, pltpu.with_memory_space_constraint(tiles, pltpu.HBM))
@@ -121,34 +121,38 @@
     return wide * (1.0 / HALF_SCALE) if x.dtype == jnp.float16 else wide
 
 
-def aggregate(field, copies, tiles, src, slot, count, exact, side):
+def aggregate(field, copies, tiles, src, into, out_of, count, exact, side):
     sent = jnp.float32 if exact else jnp.bfloat16
     with jax.named_scope("gather_row"):
-        g0 = lax.all_to_all(copies, ("z", "xl"), 0, 0, tiled=True).reshape(-1, TILE, TILE)
+        g00 = lax.all_to_all(copies, "z", 0, 0, tiled=True).reshape(-1, TILE, TILE)
     with jax.named_scope("gather_col"):
         (other,) = side(0, flip(field, "xh"))
         pair = jnp.stack([field, other])
         cols = side(1, pair, *(flip(pair, "y", k) for k in (1, 2, 3)))
+    g00, *cols = tie(g00, *cols)
+    with jax.named_scope("gather_row"):
+        g01 = flip(g00, "xl")
+        g10 = flip(g00, "co")
     with jax.named_scope("ahead"):
         keep, send = products(
-            ahead_kernel, cols, tiles, src, slot, count, 16, 64, ((32, jnp.float32), (32, sent)), "ahead"
+            ahead_kernel, cols, tiles, src, into, count, 16, 64, ((32, jnp.float32), (32, sent)), "ahead"
         )
         keep, send = side(2, keep, send)
     with jax.named_scope("scatter_row"):
         both = pack(keep + unpack(flip(pack(send, exact), "co")), exact)
-    g0, both = tie(*side(3, g0), both)
-    with jax.named_scope("scatter_row"):
+        (both,) = side(3, both)
         first = lax.all_to_all(both.reshape(16, -1, TILE), ("z", "xl"), 0, 0, tiled=True)
+    g01, _ = tie(g01, both)
     with jax.named_scope("gather_row"):
-        (g1,) = side(4, flip(g0, "co"))
+        (g11,) = side(4, flip(g01, "co"))
     with jax.named_scope("behind"):
         back, *sends = products(
-            behind_kernel, (g0, g1), tiles, src, slot, count, 64, 16, ((4, jnp.float32),) + ((4, sent),) * 3, "behind"
+            behind_kernel, (g00, g01, g10, g11), tiles, src, out_of, count, 64, 16, ((4, jnp.float32),) + ((4, jnp.bfloat16),) * 3, "behind"
         )
         back, *sends = side(5, back, *sends)
     with jax.named_scope("scatter_col"):
         for k in (1, 2, 3):
-            back = back + unpack(flip(pack(sends[k - 1], exact), "y", k))
+            back = back + unpack(flip(sends[k - 1], "y", k))
         (back,) = side(6, back)
         last = flip(pack(back[2:], exact), "xh")
     (last,) = side(7, last)
@@ -169,7 +173,7 @@
 def prepare(features):
     return pl.pallas_call(
         prepare_kernel,
-        out_shape=jax.ShapeDtypeStruct((16, 2, TILE, TILE), jnp.bfloat16),
+        out_shape=jax.ShapeDtypeStruct((8, 2, TILE, TILE), jnp.bfloat16),
         compiler_params=pltpu.CompilerParams(vmem_limit_bytes=VMEM_LIMIT),
         name="prepare",
     )(features)
@@ -209,7 +213,7 @@
         out_shape=[
             jax.ShapeDtypeStruct(nodes, jnp.bfloat16),
             jax.ShapeDtypeStruct(nodes, jnp.bfloat16),
-            jax.ShapeDtypeStruct((16, 2, TILE, TILE), jnp.bfloat16),
+            jax.ShapeDtypeStruct((8, 2, TILE, TILE), jnp.bfloat16),
             jax.ShapeDtypeStruct(nodes, jnp.float32),
             jax.ShapeDtypeStruct((2, TILE + 8, TILE), jnp.float32),
         ],
@@ -244,7 +248,7 @@
     )(co, *args)
 
 
-STEPS = ((("co", 1),), (("xh", 1),), (), (("z", 4),), (), (("xl", 1),), (("y", 1, 2, 3),), (("z", 1, 2, 3),))
+STEPS = ((("co", 1),), (("xh", 1),), (), (("z", 1),), (), (("xl", 1),), (("y", 1, 2, 3),), (("z", 2, 4, 6),))
 
 
 def body(features, tiles, tile_src, tile_dst, tile_count, degree, w_self, w_neigh, bias, upstream):
@@ -256,12 +260,14 @@
     src = ((((src // 2) % 4) ^ y) * 2 + ((src // 8) ^ xh)) * 2 + src % 2
     src = jnp.where(live, src, 16)
     other = ((dst // 2) % 2) ^ co
-    slot = other * 32 + (dst // 4) * 2 + dst % 2
-    slot = jnp.where(live, slot, 64)
+    into = other * 32 + (dst // 4) * 2 + dst % 2
+    into = jnp.where(live, into, 64)
+    out_of = (other * 2 + (((dst // 4) % 2) ^ xl)) * 16 + (dst // 8) * 2 + dst % 2
+    out_of = jnp.where(live, out_of, 64)
     inverse = jnp.broadcast_to(1.0 / degree.astype(jnp.float32)[:, None], features.shape)
 
     blocks = features.reshape(-1, TILE, TILE)
-    parts = aggregate(blocks, prepare(features), held, src, slot, count, True, lambda k, *xs: xs)
+    parts = aggregate(blocks, prepare(features), held, src, into, out_of, count, True, lambda k, *xs: xs)
     hidden, scaled, copies, base, local = middle(
         total(*parts), inverse, features, upstream, w_self, w_neigh, bias.reshape(1, -1)
     )
@@ -280,7 +286,7 @@
             *xs, weights[0] = tie(*xs, w)
         return xs
 
-    parts = aggregate(scaled.reshape(-1, TILE, TILE), copies, held, src, slot, count, False, side)
+    parts = aggregate(scaled.reshape(-1, TILE, TILE), copies, held, src, into, out_of, count, False, side)
     with jax.named_scope("weights"):
         pair = jnp.stack([weights[0], flip(weights[0], "co")])
     grad_features, grad_self, grad_neigh, grad_bias = final(co.reshape(1), *parts, base, pair)

time: 157 us -> 157 us (level)
  waiting for transfers between devices: 58.6 us -> 53.1 us
  starting transfers between devices: 76.8 us -> 79.7 us
  other arithmetic: 3.73 us -> 5.77 us
    ppermute x31 -> x35, starting transfers between devices: 56 us -> 47.2 us  [flip(): return lax.ppermute(x, axis, [(i, i ^ d) for i in range(n)])]
    all_to_all x2, starting transfers between devices: 7.31 us -> 14.9 us  [aggregate(): lax.all_to_all(both.reshape(16, -1, TILE), ('z', 'xl'), 0, 0, tiled=True)]
    ppermute x31 -> x35, waiting for transfers between devices: 55 us -> 49.1 us  [flip(): return lax.ppermute(x, axis, [(i, i ^ d) for i in range(n)])]
    all_to_all x2, starting transfers between devices: 13.5 us -> 17.7 us  [aggregate(): g00 = lax.all_to_all(copies, 'z', 0, 0, tiled=True).reshape(-1, TILE, TILE)]
  transfers between devices with their start and end apart: 35 -> 39, of which waited for: 18 -> 25; matrix products, arithmetic and copies ran while one was open for 2% -> 3% of each run, Pallas kernels for 8% -> 4%
where the time goes in v4:
time: 157 us; the launch traced here: 156 us
  starting transfers between devices  79.7 us (51%)
  waiting for transfers between devices  53.1 us (34%)
  Pallas kernels  15.3 us (10%)
  other arithmetic  5.77 us (4%)
  between operations  1.62 us (1%)
    ppermute x35, waiting for transfers between devices, flip(): return lax.ppermute(x, axis, [(i, i ^ d) for i in range(n)])  49.1 us
    ppermute x35, starting transfers between devices, flip(): return lax.ppermute(x, axis, [(i, i ^ d) for i in range(n)])  47.2 us
    all_to_all x2, starting transfers between devices, aggregate(): g00 = lax.all_to_all(copies, 'z', 0, 0, tiled=True).reshape(-1, TILE, TILE)  17.7 us
    all_to_all x2, starting transfers between devices, aggregate(): lax.all_to_all(both.reshape(16, -1, TILE), ('z', 'xl'), 0, 0, tiled=True)  14.9 us
    pallas_call x4, Pallas kernels, products(): pl.pallas_call(kernel, in_specs=[pl.BlockSpec(memory_space=pltpu.SMEM)] *...  12.3 us
  transfers between devices with their start and end apart: 39, of which 25 were waited for; matrix products, arithmetic and copies ran while one was open for 3% of the time, Pallas kernels for 4%

profile of v4, /device:TPU:1, one launch (start us, length us, event | category | flops | bytes accessed | tf_op | source)
XLA Modules:
  0.0 156.5 jit_solution(15702347877553402182)
XLA Ops:
  0.6 0.8 copy-done
  1.5 0.9 prepare.1
  2.4 9.0 %all-to-all-start = ((bf16[8,2,128,128]{3,2,1,0:T(8,128)(2,1)}), bf16[8,2,128,128]{3,2,1,0:T(8,128)(2,1)S(1)}, u32[]{:S(2)}, u32[]{:S(2)}) async-start(bf16[8,2,128,128]{3,2,1,0:T(8,128)(2,1)} %prepare.1), calls=%async_computation | async-start | bytes 1048576 | tf_op jit(solution)/shard_map/gather_row/all_to_all | solution.py:127
  11.4 2.7 %collective-permute-start = (bf16[2,128,128]{2,1,0:T(8,128)(2,1)}, bf16[2,128,128]{2,1,0:T(8,128)(2,1)S(1)}, u32[]{:S(2)}, u32[]{:S(2)}) collective-permute-start(bf16[2,128,128]{2,1,0:T(8,128)(2,1)} %bitcast.93), channel_id=1, source_target_pairs={{0,4},{4,0},{1,5},{5,1},{2,6},{6,2},{3,7},{7,3},{8,12},{12,8},{9,1... | collective-permute-start | bytes 196616 | tf_op jit(solution)/shard_map/gather_col/ppermute | solution.py:108
  14.8 0.7 add_select_fusion.1
  15.5 0.8 collective-permute-done
  16.3 0.9 pad_maximum_fusion.1.f0
  17.1 1.4 collective-permute-start.1
  18.5 2.6 %collective-permute-start.2 = (bf16[2,2,128,128]{3,2,1,0:T(8,128)(2,1)S(1)}, bf16[2,2,128,128]{3,2,1,0:T(8,128)(2,1)S(1)}, u32[]{:S(2)}, u32[]{:S(2)}) collective-permute-start(bf16[2,2,128,128]{3,2,1,0:T(8,128)(2,1)S(1)} %pad_maximum_fusion.1.f0), channel_id=1, source_target_pairs={{0,2},{1,3},{2,0},{3,1},{4,6},{5,7},{6,4},{7,5},{8,10},{9,11},{10,... | collective-permute-start | bytes 393224 | tf_op jit(solution)/shard_map/gather_col/ppermute | solution.py:108
  21.1 0.7 fusion.2.src_ref
  21.8 3.2 %collective-permute-done.2.f2 = bf16[2,2,128,128]{3,2,1,0:T(8,128)(2,1)S(1)} collective-permute-done((bf16[2,2,128,128]{3,2,1,0:T(8,128)(2,1)S(1)}, bf16[2,2,128,128]{3,2,1,0:T(8,128)(2,1)S(1)}, u32[]{:S(2)}, u32[]{:S(2)}) %collective-permute-start.2) | collective-permute-done | bytes 131104 | tf_op jit(solution)/shard_map/gather_col/ppermute | solution.py:108
  25.0 1.6 collective-permute-done.3.f3
  26.6 2.8 %all-to-all-done = bf16[8,2,128,128]{3,2,1,0:T(8,128)(2,1)S(1)} async-done(((bf16[8,2,128,128]{3,2,1,0:T(8,128)(2,1)}), bf16[8,2,128,128]{3,2,1,0:T(8,128)(2,1)S(1)}, u32[]{:S(2)}, u32[]{:S(2)}) %all-to-all-start) | async-done | bytes 524320 | tf_op jit(solution)/shard_map/gather_row/all_to_all | solution.py:127
  29.4 3.1 %ahead.2 = (f32[32,128,128]{2,1,0:T(8,128)S(1)}, f32[32,128,128]{2,1,0:T(8,128)S(1)}) custom-call(s32[96]{0:T(128)S(1)} %fusion.2.src_ref, s32[96]{0:T(128)S(1)} %get-tuple-element.117.slot_ref, s32[1]{0:T(128)} %bitcast.83.count_ref, bf16[2,2,128,128]{3,2,1,0:T(8,128)(2,1)S(1)} %pad_maximum_fusion.1.f0, ...), custom_call_target="tpu_custom_call" | custom-call | flops 3221225472 | bytes 3145728 | tf_op jit(solution)/shard_map/ahead/ahead/pallas_call | solution.py:85
  33.2 2.6 %collective-permute-start.5 = (bf16[16,128,128]{2,1,0:T(8,128)(2,1)S(1)}, bf16[16,128,128]{2,1,0:T(8,128)(2,1)S(1)}, u32[]{:S(2)}, u32[]{:S(2)}) collective-permute-start(bf16[16,128,128]{2,1,0:T(8,128)(2,1)S(1)} %bitcast.90), channel_id=1, source_target_pairs={{0,16},{16,0},{1,17},{17,1},{2,18},{18,2},{3,19},{19,3},{4,20},{20... | collective-permute-start | bytes 1572872 | tf_op jit(solution)/shard_map/gather_row/ppermute | solution.py:108
  35.8 1.4 multiply_convert_fusion
  37.3 7.8 %all-to-all-start.1 = ((f16[16,256,128]{2,1,0:T(8,128)(2,1)}), f16[16,256,128]{2,1,0:T(8,128)(2,1)S(1)}, u32[]{:S(2)}, u32[]{:S(2)}) async-start(f16[16,256,128]{2,1,0:T(8,128)(2,1)} %bitcast.9), calls=%async_computation.1 | async-start | bytes 2097152 | tf_op jit(solution)/shard_map/scatter_row/all_to_all | solution.py:144
  45.0 0.7 collective-permute-start.6
  45.8 2.0 %collective-permute-done.5.g1 = bf16[16,128,128]{2,1,0:T(8,128)(2,1)S(1)} collective-permute-done((bf16[16,128,128]{2,1,0:T(8,128)(2,1)S(1)}, bf16[16,128,128]{2,1,0:T(8,128)(2,1)S(1)}, u32[]{:S(2)}, u32[]{:S(2)}) %collective-permute-start.5) | collective-permute-done | bytes 524320 | tf_op jit(solution)/shard_map/gather_row/ppermute | solution.py:108
  47.8 1.3 collective-permute-start.7
  49.1 1.5 collective-permute-done.7.g3
  50.6 3.0 %behind.2 = (f32[4,128,128]{2,1,0:T(8,128)S(1)}, bf16[4,128,128]{2,1,0:T(8,128)(2,1)S(1)}, bf16[4,128,128]{2,1,0:T(8,128)(2,1)S(1)}, bf16[4,128,128]{2,1,0:T(8,128)(2,1)S(1)}) custom-call(s32[96]{0:T(128)S(1)} %fusion.2.src_ref, s32[96]{0:T(128)S(1)} %add_select_fusion.slot_ref, s32[1]{0:T(128)} %bitcast.84.count_ref, bf16[16,128,128]{2,1,0:T(8,128)(2,1)S(1)} %bitcast.92, ...), custom_call_target="tpu_custom_call" | custom-call | flops 402653184 | bytes 3145728 | tf_op jit(solution)/shard_map/behind/behind/pallas_call | solution.py:85
  53.7 1.3 collective-permute-start.10
  55.1 0.6 collective-permute-start.8
  55.7 2.0 %collective-permute-start.9 = (bf16[4,128,128]{2,1,0:T(8,128)(2,1)S(1)}, bf16[4,128,128]{2,1,0:T(8,128)(2,1)S(1)}, u32[]{:S(2)}, u32[]{:S(2)}) collective-permute-start(bf16[4,128,128]{2,1,0:T(8,128)(2,1)S(1)} %get-tuple-element.71), channel_id=1, source_target_pairs={{0,2},{1,3},{2,0},{3,1},{4,6},{5,7},{6,4},{7,5},{8,10},{9,11},{10,... | collective-permute-start | bytes 393224 | tf_op jit(solution)/shard_map/scatter_col/ppermute | solution.py:108
  57.7 2.3 %collective-permute-done.10 = bf16[4,128,128]{2,1,0:T(8,128)(2,1)S(1)} collective-permute-done((bf16[4,128,128]{2,1,0:T(8,128)(2,1)S(1)}, bf16[4,128,128]{2,1,0:T(8,128)(2,1)S(1)}, u32[]{:S(2)}, u32[]{:S(2)}) %collective-permute-start.10) | collective-permute-done | bytes 131104 | tf_op jit(solution)/shard_map/scatter_col/ppermute | solution.py:108
  60.0 3.7 %collective-permute-done.9 = bf16[4,128,128]{2,1,0:T(8,128)(2,1)S(1)} collective-permute-done((bf16[4,128,128]{2,1,0:T(8,128)(2,1)S(1)}, bf16[4,128,128]{2,1,0:T(8,128)(2,1)S(1)}, u32[]{:S(2)}, u32[]{:S(2)}) %collective-permute-start.9) | collective-permute-done | bytes 131104 | tf_op jit(solution)/shard_map/scatter_col/ppermute | solution.py:108
  63.7 1.7 %collective-permute-start.11 = (f16[2,128,128]{2,1,0:T(8,128)(2,1)S(1)}, f16[2,128,128]{2,1,0:T(8,128)(2,1)S(1)}, u32[]{:S(2)}, u32[]{:S(2)}) collective-permute-start(f16[2,128,128]{2,1,0:T(8,128)(2,1)S(1)} %get-tuple-element.121), channel_id=1, source_target_pairs={{0,4},{4,0},{1,5},{5,1},{2,6},{6,2},{3,7},{7,3},{8,12},{12,8},{9,1... | collective-permute-start | bytes 196616 | tf_op jit(solution)/shard_map/scatter_col/ppermute | solution.py:108
  65.5 4.1 %collective-permute-done.11 = f16[2,128,128]{2,1,0:T(8,128)(2,1)S(1)} collective-permute-done((f16[2,128,128]{2,1,0:T(8,128)(2,1)S(1)}, f16[2,128,128]{2,1,0:T(8,128)(2,1)S(1)}, u32[]{:S(2)}, u32[]{:S(2)}) %collective-permute-start.11) | collective-permute-done | bytes 65568 | tf_op jit(solution)/shard_map/scatter_col/ppermute | solution.py:108
  69.6 1.2 all-to-all-done.1
  71.1 1.3 middle.1
  72.4 8.7 %all-to-all-start.2 = ((bf16[8,2,128,128]{3,2,1,0:T(8,128)(2,1)}), bf16[8,2,128,128]{3,2,1,0:T(8,128)(2,1)S(1)}, u32[]{:S(2)}, u32[]{:S(2)}) async-start(bf16[8,2,128,128]{3,2,1,0:T(8,128)(2,1)} %get-tuple-element.74), calls=%async_computation.2 | async-start | bytes 1048576 | tf_op jit(solution)/shard_map/gather_row/all_to_all | solution.py:127
  81.0 1.0 collective-permute-start.13
  82.1 0.8 collective-permute-start.12
  83.0 4.2 %collective-permute-done.12 = bf16[2,128,128]{2,1,0:T(8,128)(2,1)S(1)} collective-permute-done((bf16[2,128,128]{2,1,0:T(8,128)(2,1)S(1)}, bf16[2,128,128]{2,1,0:T(8,128)(2,1)S(1)}, u32[]{:S(2)}, u32[]{:S(2)}) %collective-permute-start.12) | collective-permute-done | bytes 65568 | tf_op jit(solution)/shard_map/gather_col/ppermute | solution.py:108
  87.2 0.9 collective-permute-start.14
  88.2 2.7 %collective-permute-start.15 = (bf16[2,2,128,128]{3,2,1,0:T(8,128)(2,1)S(1)}, bf16[2,2,128,128]{3,2,1,0:T(8,128)(2,1)S(1)}, u32[]{:S(2)}, u32[]{:S(2)}) collective-permute-start(bf16[2,2,128,128]{3,2,1,0:T(8,128)(2,1)S(1)} %pad_maximum_fusion.2.f0), channel_id=1, source_target_pairs={{0,2},{1,3},{2,0},{3,1},{4,6},{5,7},{6,4},{7,5},{8,10},{9,11},{10,... | collective-permute-start | bytes 393224 | tf_op jit(solution)/shard_map/gather_col/ppermute | solution.py:108
  91.2 0.8 collective-permute-start.17
  92.0 3.9 %collective-permute-done.17 = f32[136,128]{1,0:T(8,128)S(1)} collective-permute-done((f32[136,128]{1,0:T(8,128)S(1)}, f32[136,128]{1,0:T(8,128)S(1)}, u32[]{:S(2)}, u32[]{:S(2)}) %collective-permute-start.17) | collective-permute-done | bytes 69664 | tf_op jit(solution)/shard_map/gather_col/weights/ppermute | solution.py:108
  95.9 0.5 collective-permute-done.15.f2
  96.4 2.5 %collective-permute-done.16.f3 = bf16[2,2,128,128]{3,2,1,0:T(8,128)(2,1)S(1)} collective-permute-done((bf16[2,2,128,128]{3,2,1,0:T(8,128)(2,1)S(1)}, bf16[2,2,128,128]{3,2,1,0:T(8,128)(2,1)S(1)}, u32[]{:S(2)}, u32[]{:S(2)}) %collective-permute-start.16) | collective-permute-done | bytes 131104 | tf_op jit(solution)/shard_map/gather_col/ppermute | solution.py:108
  99.0 3.1 %ahead.3 = (f32[32,128,128]{2,1,0:T(8,128)S(1)}, bf16[32,128,128]{2,1,0:T(8,128)(2,1)S(1)}) custom-call(s32[96]{0:T(128)S(1)} %fusion.2.src_ref, s32[96]{0:T(128)S(1)} %get-tuple-element.117.slot_ref, s32[1]{0:T(128)} %bitcast.85.count_ref, bf16[2,2,128,128]{3,2,1,0:T(8,128)(2,1)S(1)} %pad_maximum_fusion.2.f0, ...), custom_call_target="tpu_custom_call" | custom-call | flops 3221225472 | bytes 3145728 | tf_op jit(solution)/shard_map/ahead/ahead/pallas_call | solution.py:85
  102.0 1.1 collective-permute-start.18
  103.2 1.6 %collective-permute-start.19 = (f32[136,128]{1,0:T(8,128)S(1)}, f32[136,128]{1,0:T(8,128)S(1)}, u32[]{:S(2)}, u32[]{:S(2)}) collective-permute-start(f32[136,128]{1,0:T(8,128)S(1)} %add.139), channel_id=1, source_target_pairs={{0,32},{32,0},{64,96},{96,64},{128,160},{160,128},{192,224},{224,1... | collective-permute-start | bytes 208904 | tf_op jit(solution)/shard_map/scatter_row/weights/ppermute | solution.py:108
  104.7 0.9 collective-permute-start.20
  105.7 1.4 collective-permute-done.19
  107.1 1.3 add_convert_fusion
  108.4 7.1 %all-to-all-start.3 = ((bf16[16,256,128]{2,1,0:T(8,128)(2,1)}), bf16[16,256,128]{2,1,0:T(8,128)(2,1)S(1)}, u32[]{:S(2)}, u32[]{:S(2)}) async-start(bf16[16,256,128]{2,1,0:T(8,128)(2,1)} %bitcast.20), calls=%async_computation.3 | async-start | bytes 2097152 | tf_op jit(solution)/shard_map/scatter_row/all_to_all | solution.py:144
  115.6 2.3 %collective-permute-done.20.g1 = bf16[16,128,128]{2,1,0:T(8,128)(2,1)S(1)} collective-permute-done((bf16[16,128,128]{2,1,0:T(8,128)(2,1)S(1)}, bf16[16,128,128]{2,1,0:T(8,128)(2,1)S(1)}, u32[]{:S(2)}, u32[]{:S(2)}) %collective-permute-start.20) | collective-permute-done | bytes 524320 | tf_op jit(solution)/shard_map/gather_row/ppermute | solution.py:108
  117.9 1.4 collective-permute-start.22
  119.3 1.5 collective-permute-done.22.g3
  120.9 1.4 collective-permute-start.23
  122.3 3.0 %behind.3 = (f32[4,128,128]{2,1,0:T(8,128)S(1)}, bf16[4,128,128]{2,1,0:T(8,128)(2,1)S(1)}, bf16[4,128,128]{2,1,0:T(8,128)(2,1)S(1)}, bf16[4,128,128]{2,1,0:T(8,128)(2,1)S(1)}) custom-call(s32[96]{0:T(128)S(1)} %fusion.2.src_ref, s32[96]{0:T(128)S(1)} %add_select_fusion.slot_ref, s32[1]{0:T(128)} %bitcast.86.count_ref, bf16[16,128,128]{2,1,0:T(8,128)(2,1)S(1)} %bitcast.89, ...), custom_call_target="tpu_custom_call" | custom-call | flops 402653184 | bytes 3145728 | tf_op jit(solution)/shard_map/behind/behind/pallas_call | solution.py:85
  125.5 3.4 %collective-permute-start.28 = (f32[136,128]{1,0:T(8,128)S(1)}, f32[136,128]{1,0:T(8,128)S(1)}, u32[]{:S(2)}, u32[]{:S(2)}) collective-permute-start(f32[136,128]{1,0:T(8,128)S(1)} %add.142), channel_id=1, source_target_pairs={{0,2},{1,3},{2,0},{3,1},{4,6},{5,7},{6,4},{7,5},{8,10},{9,11},{10,... | collective-permute-start | bytes 208904 | tf_op jit(solution)/shard_map/scatter_col/weights/ppermute | solution.py:108
  129.3 3.4 %collective-permute-start.25 = (bf16[4,128,128]{2,1,0:T(8,128)(2,1)S(1)}, bf16[4,128,128]{2,1,0:T(8,128)(2,1)S(1)}, u32[]{:S(2)}, u32[]{:S(2)}) collective-permute-start(bf16[4,128,128]{2,1,0:T(8,128)(2,1)S(1)} %get-tuple-element.105), channel_id=1, source_target_pairs={{0,2},{1,3},{2,0},{3,1},{4,6},{5,7},{6,4},{7,5},{8,10},{9,11},{10,... | collective-permute-start | bytes 393224 | tf_op jit(solution)/shard_map/scatter_col/ppermute | solution.py:108
  133.5 3.8 %collective-permute-done.25 = bf16[4,128,128]{2,1,0:T(8,128)(2,1)S(1)} collective-permute-done((bf16[4,128,128]{2,1,0:T(8,128)(2,1)S(1)}, bf16[4,128,128]{2,1,0:T(8,128)(2,1)S(1)}, u32[]{:S(2)}, u32[]{:S(2)}) %collective-permute-start.25) | collective-permute-done | bytes 131104 | tf_op jit(solution)/shard_map/scatter_col/ppermute | solution.py:108
  137.4 2.5 %collective-permute-done.26 = bf16[4,128,128]{2,1,0:T(8,128)(2,1)S(1)} collective-permute-done((bf16[4,128,128]{2,1,0:T(8,128)(2,1)S(1)}, bf16[4,128,128]{2,1,0:T(8,128)(2,1)S(1)}, u32[]{:S(2)}, u32[]{:S(2)}) %collective-permute-start.26) | collective-permute-done | bytes 131104 | tf_op jit(solution)/shard_map/scatter_col/ppermute | solution.py:108
  139.9 3.2 %collective-permute-start.31 = (f32[136,128]{1,0:T(8,128)S(1)}, f32[136,128]{1,0:T(8,128)S(1)}, u32[]{:S(2)}, u32[]{:S(2)}) collective-permute-start(f32[136,128]{1,0:T(8,128)S(1)} %add_add_fusion.1), channel_id=1, source_target_pairs={{0,64},{32,96},{64,0},{96,32},{128,192},{160,224},{192,128},{224,1... | collective-permute-start | bytes 208904 | tf_op jit(solution)/shard_map/weights/ppermute | solution.py:108
  143.1 4.1 %collective-permute-start.32 = (f32[136,128]{1,0:T(8,128)S(1)}, f32[136,128]{1,0:T(8,128)S(1)}, u32[]{:S(2)}, u32[]{:S(2)}) collective-permute-start(f32[136,128]{1,0:T(8,128)S(1)} %add_add_fusion.1), channel_id=1, source_target_pairs={{0,128},{32,160},{64,192},{96,224},{128,0},{160,32},{192,64},{224,... | collective-permute-start | bytes 208904 | tf_op jit(solution)/shard_map/weights/ppermute | solution.py:108
  147.5 3.0 %collective-permute-done.32 = f32[136,128]{1,0:T(8,128)S(1)} collective-permute-done((f32[136,128]{1,0:T(8,128)S(1)}, f32[136,128]{1,0:T(8,128)S(1)}, u32[]{:S(2)}, u32[]{:S(2)}) %collective-permute-start.32) | collective-permute-done | bytes 69664 | tf_op jit(solution)/shard_map/weights/ppermute | solution.py:108
  150.5 3.0 %collective-permute-done.33 = f32[136,128]{1,0:T(8,128)S(1)} collective-permute-done((f32[136,128]{1,0:T(8,128)S(1)}, f32[136,128]{1,0:T(8,128)S(1)}, u32[]{:S(2)}, u32[]{:S(2)}) %collective-permute-start.33) | collective-permute-done | bytes 69664 | tf_op jit(solution)/shard_map/weights/ppermute | solution.py:108
  153.5 1.3 collective-permute-start.34
  154.8 0.9 collective-permute-done.34
  155.7 0.8 final.1
  (63 shorter events, 3.5 us)
Async XLA Ops:
  0.6 0.8 copy-start
  2.4 27.0 %all-to-all-start = ((bf16[8,2,128,128]{3,2,1,0:T(8,128)(2,1)}), bf16[8,2,128,128]{3,2,1,0:T(8,128)(2,1)S(1)}, u32[]{:S(2)}, u32[]{:S(2)}) async-start(bf16[8,2,128,128]{3,2,1,0:T(8,128)(2,1)} %prepare.1), calls=%async_computation | async-start | bytes 1048576 | tf_op jit(solution)/shard_map/gather_row/all_to_all | solution.py:127
  11.4 4.8 %collective-permute-start = (bf16[2,128,128]{2,1,0:T(8,128)(2,1)}, bf16[2,128,128]{2,1,0:T(8,128)(2,1)S(1)}, u32[]{:S(2)}, u32[]{:S(2)}) collective-permute-start(bf16[2,128,128]{2,1,0:T(8,128)(2,1)} %bitcast.93), channel_id=1, source_target_pairs={{0,4},{4,0},{1,5},{5,1},{2,6},{6,2},{3,7},{7,3},{8,12},{12,8},{9,1... | collective-permute-start | bytes 196616 | tf_op jit(solution)/shard_map/gather_col/ppermute | solution.py:108
  17.1 4.7 %collective-permute-start.1 = (bf16[2,2,128,128]{3,2,1,0:T(8,128)(2,1)S(1)}, bf16[2,2,128,128]{3,2,1,0:T(8,128)(2,1)S(1)}, u32[]{:S(2)}, u32[]{:S(2)}) collective-permute-start(bf16[2,2,128,128]{3,2,1,0:T(8,128)(2,1)S(1)} %pad_maximum_fusion.1.f0), channel_id=1, source_target_pairs={{0,1},{1,0},{2,3},{3,2},{4,5},{5,4},{6,7},{7,6},{8,9},{9,8},{10,11... | collective-permute-start | bytes 393224 | tf_op jit(solution)/shard_map/gather_col/ppermute | solution.py:108
  18.5 6.6 %collective-permute-start.2 = (bf16[2,2,128,128]{3,2,1,0:T(8,128)(2,1)S(1)}, bf16[2,2,128,128]{3,2,1,0:T(8,128)(2,1)S(1)}, u32[]{:S(2)}, u32[]{:S(2)}) collective-permute-start(bf16[2,2,128,128]{3,2,1,0:T(8,128)(2,1)S(1)} %pad_maximum_fusion.1.f0), channel_id=1, source_target_pairs={{0,2},{1,3},{2,0},{3,1},{4,6},{5,7},{6,4},{7,5},{8,10},{9,11},{10,... | collective-permute-start | bytes 393224 | tf_op jit(solution)/shard_map/gather_col/ppermute | solution.py:108
  21.1 5.5 %collective-permute-start.3 = (bf16[2,2,128,128]{3,2,1,0:T(8,128)(2,1)S(1)}, bf16[2,2,128,128]{3,2,1,0:T(8,128)(2,1)S(1)}, u32[]{:S(2)}, u32[]{:S(2)}) collective-permute-start(bf16[2,2,128,128]{3,2,1,0:T(8,128)(2,1)S(1)} %pad_maximum_fusion.1.f0), channel_id=1, source_target_pairs={{0,3},{1,2},{2,1},{3,0},{4,7},{5,6},{6,5},{7,4},{8,11},{9,10},{10,... | collective-permute-start | bytes 393224 | tf_op jit(solution)/shard_map/gather_col/ppermute | solution.py:108
  32.8 3.0 %collective-permute-start.4 = (f16[32,128,128]{2,1,0:T(8,128)(2,1)S(1)}, f16[32,128,128]{2,1,0:T(8,128)(2,1)S(1)}, u32[]{:S(2)}, u32[]{:S(2)}) collective-permute-start(f16[32,128,128]{2,1,0:T(8,128)(2,1)S(1)} %multiply_convert_fusion.1), channel_id=1, source_target_pairs={{0,8},{8,0},{1,9},{9,1},{2,10},{10,2},{3,11},{11,3},{4,12},{12,4},... | collective-permute-start | bytes 3145736 | tf_op jit(solution)/shard_map/scatter_row/ppermute | solution.py:108
  33.2 14.5 %collective-permute-start.5 = (bf16[16,128,128]{2,1,0:T(8,128)(2,1)S(1)}, bf16[16,128,128]{2,1,0:T(8,128)(2,1)S(1)}, u32[]{:S(2)}, u32[]{:S(2)}) collective-permute-start(bf16[16,128,128]{2,1,0:T(8,128)(2,1)S(1)} %bitcast.90), channel_id=1, source_target_pairs={{0,16},{16,0},{1,17},{17,1},{2,18},{18,2},{3,19},{19,3},{4,20},{20... | collective-permute-start | bytes 1572872 | tf_op jit(solution)/shard_map/gather_row/ppermute | solution.py:108
  37.3 11.8 %copy-start.6 = (s32[1,1,96]{2,1,0:T(1,128)S(1)}, s32[1,1,96]{2,1,0:T(1,128)}, u32[]{:S(2)}) copy-start(s32[1,1,96]{2,1,0:T(1,128)} %param.13) | copy-start | bytes 1156
  37.3 33.4 %all-to-all-start.1 = ((f16[16,256,128]{2,1,0:T(8,128)(2,1)}), f16[16,256,128]{2,1,0:T(8,128)(2,1)S(1)}, u32[]{:S(2)}, u32[]{:S(2)}) async-start(f16[16,256,128]{2,1,0:T(8,128)(2,1)} %bitcast.9), calls=%async_computation.1 | async-start | bytes 2097152 | tf_op jit(solution)/shard_map/scatter_row/all_to_all | solution.py:144
  45.0 4.0 %collective-permute-start.6 = (bf16[16,128,128]{2,1,0:T(8,128)(2,1)S(1)}, bf16[16,128,128]{2,1,0:T(8,128)(2,1)S(1)}, u32[]{:S(2)}, u32[]{:S(2)}) collective-permute-start(bf16[16,128,128]{2,1,0:T(8,128)(2,1)S(1)} %bitcast.91), channel_id=1, source_target_pairs={{0,8},{8,0},{1,9},{9,1},{2,10},{10,2},{3,11},{11,3},{4,12},{12,4},... | collective-permute-start | bytes 1572872 | tf_op jit(solution)/shard_map/gather_row/ppermute | solution.py:108
  47.8 2.8 %collective-permute-start.7 = (bf16[16,128,128]{2,1,0:T(8,128)(2,1)S(1)}, bf16[16,128,128]{2,1,0:T(8,128)(2,1)S(1)}, u32[]{:S(2)}, u32[]{:S(2)}) collective-permute-start(bf16[16,128,128]{2,1,0:T(8,128)(2,1)S(1)} %collective-permute-done.5.g1), channel_id=1, source_target_pairs={{0,8},{8,0},{1,9},{9,1},{2,10},{10,2},{3,11},{11,3},{4,12},{12,4},... | collective-permute-start | bytes 1572872 | tf_op jit(solution)/shard_map/gather_row/ppermute | solution.py:108
  50.6 14.9 %copy-start.7 = (s32[256]{0:T(256)S(1)}, s32[256]{0:T(256)}, u32[]{:S(2)}) copy-start(s32[256]{0:T(256)} %param.15) | copy-start | bytes 3076
  53.6 17.4 %copy-start.1 = (bf16[256,128]{1,0:T(8,128)(2,1)S(1)}, bf16[256,128]{1,0:T(8,128)(2,1)}, u32[]{:S(2)}) copy-start(bf16[256,128]{1,0:T(8,128)(2,1)} %features_ref.3) | copy-start | bytes 196612
  53.7 17.4 %copy-start.2 = (bf16[256,128]{1,0:T(8,128)(2,1)S(1)}, bf16[256,128]{1,0:T(8,128)(2,1)}, u32[]{:S(2)}) copy-start(bf16[256,128]{1,0:T(8,128)(2,1)} %upstream_ref.1) | copy-start | bytes 196612
  53.7 17.4 %copy-start.3 = (bf16[128,128]{1,0:T(8,128)(2,1)S(1)}, bf16[128,128]{1,0:T(8,128)(2,1)}, u32[]{:S(2)}) copy-start(bf16[128,128]{1,0:T(8,128)(2,1)} %w_self_ref.1) | copy-start | bytes 98308
  53.7 17.4 %copy-start.4 = (bf16[128,128]{1,0:T(8,128)(2,1)S(1)}, bf16[128,128]{1,0:T(8,128)(2,1)}, u32[]{:S(2)}) copy-start(bf16[128,128]{1,0:T(8,128)(2,1)} %w_neigh_ref.1) | copy-start | bytes 98308
  53.7 17.4 %copy-start.5 = (f32[128]{0:T(128)S(1)}, f32[128]{0:T(128)}, u32[]{:S(2)}) copy-start(f32[128]{0:T(128)} %param.18) | copy-start | bytes 1540
  53.7 6.2 %collective-permute-start.10 = (bf16[4,128,128]{2,1,0:T(8,128)(2,1)S(1)}, bf16[4,128,128]{2,1,0:T(8,128)(2,1)S(1)}, u32[]{:S(2)}, u32[]{:S(2)}) collective-permute-start(bf16[4,128,128]{2,1,0:T(8,128)(2,1)S(1)} %get-tuple-element.72), channel_id=1, source_target_pairs={{0,3},{1,2},{2,1},{3,0},{4,7},{5,6},{6,5},{7,4},{8,11},{9,10},{10,... | collective-permute-start | bytes 393224 | tf_op jit(solution)/shard_map/scatter_col/ppermute | solution.py:108
  55.1 4.9 %collective-permute-start.8 = (bf16[4,128,128]{2,1,0:T(8,128)(2,1)S(1)}, bf16[4,128,128]{2,1,0:T(8,128)(2,1)S(1)}, u32[]{:S(2)}, u32[]{:S(2)}) collective-permute-start(bf16[4,128,128]{2,1,0:T(8,128)(2,1)S(1)} %get-tuple-element.70), channel_id=1, source_target_pairs={{0,1},{1,0},{2,3},{3,2},{4,5},{5,4},{6,7},{7,6},{8,9},{9,8},{10,11... | collective-permute-start | bytes 393224 | tf_op jit(solution)/shard_map/scatter_col/ppermute | solution.py:108
  55.7 7.9 %collective-permute-start.9 = (bf16[4,128,128]{2,1,0:T(8,128)(2,1)S(1)}, bf16[4,128,128]{2,1,0:T(8,128)(2,1)S(1)}, u32[]{:S(2)}, u32[]{:S(2)}) collective-permute-start(bf16[4,128,128]{2,1,0:T(8,128)(2,1)S(1)} %get-tuple-element.71), channel_id=1, source_target_pairs={{0,2},{1,3},{2,0},{3,1},{4,6},{5,7},{6,4},{7,5},{8,10},{9,11},{10,... | collective-permute-start | bytes 393224 | tf_op jit(solution)/shard_map/scatter_col/ppermute | solution.py:108
  63.7 5.8 %collective-permute-start.11 = (f16[2,128,128]{2,1,0:T(8,128)(2,1)S(1)}, f16[2,128,128]{2,1,0:T(8,128)(2,1)S(1)}, u32[]{:S(2)}, u32[]{:S(2)}) collective-permute-start(f16[2,128,128]{2,1,0:T(8,128)(2,1)S(1)} %get-tuple-element.121), channel_id=1, source_target_pairs={{0,4},{4,0},{1,5},{5,1},{2,6},{6,2},{3,7},{7,3},{8,12},{12,8},{9,1... | collective-permute-start | bytes 196616 | tf_op jit(solution)/shard_map/scatter_col/ppermute | solution.py:108
  72.4 26.6 %all-to-all-start.2 = ((bf16[8,2,128,128]{3,2,1,0:T(8,128)(2,1)}), bf16[8,2,128,128]{3,2,1,0:T(8,128)(2,1)S(1)}, u32[]{:S(2)}, u32[]{:S(2)}) async-start(bf16[8,2,128,128]{3,2,1,0:T(8,128)(2,1)} %get-tuple-element.74), calls=%async_computation.2 | async-start | bytes 1048576 | tf_op jit(solution)/shard_map/gather_row/all_to_all | solution.py:127
  81.0 1.9 %collective-permute-start.13 = (f32[136,128]{1,0:T(8,128)S(1)}, f32[136,128]{1,0:T(8,128)S(1)}, u32[]{:S(2)}, u32[]{:S(2)}) collective-permute-start(f32[136,128]{1,0:T(8,128)S(1)} %dynamic-slice_bitcast_fusion), channel_id=1, source_target_pairs={{0,8},{8,0},{1,9},{9,1},{2,10},{10,2},{3,11},{11,3},{4,12},{12,4},... | collective-permute-start | bytes 208904 | tf_op jit(solution)/shard_map/gather_col/weights/ppermute | solution.py:108
  82.1 5.2 %collective-permute-start.12 = (bf16[2,128,128]{2,1,0:T(8,128)(2,1)S(1)}, bf16[2,128,128]{2,1,0:T(8,128)(2,1)S(1)}, u32[]{:S(2)}, u32[]{:S(2)}) collective-permute-start(bf16[2,128,128]{2,1,0:T(8,128)(2,1)S(1)} %bitcast.97), channel_id=1, source_target_pairs={{0,4},{4,0},{1,5},{5,1},{2,6},{6,2},{3,7},{7,3},{8,12},{12,8},{9,1... | collective-permute-start | bytes 196616 | tf_op jit(solution)/shard_map/gather_col/ppermute | solution.py:108
  87.2 8.6 %collective-permute-start.14 = (bf16[2,2,128,128]{3,2,1,0:T(8,128)(2,1)S(1)}, bf16[2,2,128,128]{3,2,1,0:T(8,128)(2,1)S(1)}, u32[]{:S(2)}, u32[]{:S(2)}) collective-permute-start(bf16[2,2,128,128]{3,2,1,0:T(8,128)(2,1)S(1)} %pad_maximum_fusion.2.f0), channel_id=1, source_target_pairs={{0,1},{1,0},{2,3},{3,2},{4,5},{5,4},{6,7},{7,6},{8,9},{9,8},{10,11... | collective-permute-start | bytes 393224 | tf_op jit(solution)/shard_map/gather_col/ppermute | solution.py:108
  88.2 8.2 %collective-permute-start.15 = (bf16[2,2,128,128]{3,2,1,0:T(8,128)(2,1)S(1)}, bf16[2,2,128,128]{3,2,1,0:T(8,128)(2,1)S(1)}, u32[]{:S(2)}, u32[]{:S(2)}) collective-permute-start(bf16[2,2,128,128]{3,2,1,0:T(8,128)(2,1)S(1)} %pad_maximum_fusion.2.f0), channel_id=1, source_target_pairs={{0,2},{1,3},{2,0},{3,1},{4,6},{5,7},{6,4},{7,5},{8,10},{9,11},{10,... | collective-permute-start | bytes 393224 | tf_op jit(solution)/shard_map/gather_col/ppermute | solution.py:108
  90.9 8.0 %collective-permute-start.16 = (bf16[2,2,128,128]{3,2,1,0:T(8,128)(2,1)S(1)}, bf16[2,2,128,128]{3,2,1,0:T(8,128)(2,1)S(1)}, u32[]{:S(2)}, u32[]{:S(2)}) collective-permute-start(bf16[2,2,128,128]{3,2,1,0:T(8,128)(2,1)S(1)} %pad_maximum_fusion.2.f0), channel_id=1, source_target_pairs={{0,3},{1,2},{2,1},{3,0},{4,7},{5,6},{6,5},{7,4},{8,11},{9,10},{10,... | collective-permute-start | bytes 393224 | tf_op jit(solution)/shard_map/gather_col/ppermute | solution.py:108
  91.2 4.7 %collective-permute-start.17 = (f32[136,128]{1,0:T(8,128)S(1)}, f32[136,128]{1,0:T(8,128)S(1)}, u32[]{:S(2)}, u32[]{:S(2)}) collective-permute-start(f32[136,128]{1,0:T(8,128)S(1)} %bitcast_add_fusion.2), channel_id=1, source_target_pairs={{0,4},{4,0},{1,5},{5,1},{2,6},{6,2},{3,7},{7,3},{8,12},{12,8},{9,1... | collective-permute-start | bytes 208904 | tf_op jit(solution)/shard_map/gather_col/weights/ppermute | solution.py:108
  102.0 5.1 %collective-permute-start.18 = (bf16[32,128,128]{2,1,0:T(8,128)(2,1)S(1)}, bf16[32,128,128]{2,1,0:T(8,128)(2,1)S(1)}, u32[]{:S(2)}, u32[]{:S(2)}) collective-permute-start(bf16[32,128,128]{2,1,0:T(8,128)(2,1)S(1)} %get-tuple-element.91), channel_id=1, source_target_pairs={{0,8},{8,0},{1,9},{9,1},{2,10},{10,2},{3,11},{11,3},{4,12},{12,4},... | collective-permute-start | bytes 3145736 | tf_op jit(solution)/shard_map/scatter_row/ppermute | solution.py:108
  103.2 3.9 %collective-permute-start.19 = (f32[136,128]{1,0:T(8,128)S(1)}, f32[136,128]{1,0:T(8,128)S(1)}, u32[]{:S(2)}, u32[]{:S(2)}) collective-permute-start(f32[136,128]{1,0:T(8,128)S(1)} %add.139), channel_id=1, source_target_pairs={{0,32},{32,0},{64,96},{96,64},{128,160},{160,128},{192,224},{224,1... | collective-permute-start | bytes 208904 | tf_op jit(solution)/shard_map/scatter_row/weights/ppermute | solution.py:108
  104.7 13.1 %collective-permute-start.20 = (bf16[16,128,128]{2,1,0:T(8,128)(2,1)S(1)}, bf16[16,128,128]{2,1,0:T(8,128)(2,1)S(1)}, u32[]{:S(2)}, u32[]{:S(2)}) collective-permute-start(bf16[16,128,128]{2,1,0:T(8,128)(2,1)S(1)} %bitcast.87), channel_id=1, source_target_pairs={{0,16},{16,0},{1,17},{17,1},{2,18},{18,2},{3,19},{19,3},{4,20},{20... | collective-permute-start | bytes 1572872 | tf_op jit(solution)/shard_map/gather_row/ppermute | solution.py:108
  108.4 47.2 %all-to-all-start.3 = ((bf16[16,256,128]{2,1,0:T(8,128)(2,1)}), bf16[16,256,128]{2,1,0:T(8,128)(2,1)S(1)}, u32[]{:S(2)}, u32[]{:S(2)}) async-start(bf16[16,256,128]{2,1,0:T(8,128)(2,1)} %bitcast.20), calls=%async_computation.3 | async-start | bytes 2097152 | tf_op jit(solution)/shard_map/scatter_row/all_to_all | solution.py:144
  117.9 3.0 %collective-permute-start.22 = (bf16[16,128,128]{2,1,0:T(8,128)(2,1)S(1)}, bf16[16,128,128]{2,1,0:T(8,128)(2,1)S(1)}, u32[]{:S(2)}, u32[]{:S(2)}) collective-permute-start(bf16[16,128,128]{2,1,0:T(8,128)(2,1)S(1)} %collective-permute-done.20.g1), channel_id=1, source_target_pairs={{0,8},{8,0},{1,9},{9,1},{2,10},{10,2},{3,11},{11,3},{4,12},{12,4},... | collective-permute-start | bytes 1572872 | tf_op jit(solution)/shard_map/gather_row/ppermute | solution.py:108
  119.3 3.0 %collective-permute-start.21 = (bf16[16,128,128]{2,1,0:T(8,128)(2,1)S(1)}, bf16[16,128,128]{2,1,0:T(8,128)(2,1)S(1)}, u32[]{:S(2)}, u32[]{:S(2)}) collective-permute-start(bf16[16,128,128]{2,1,0:T(8,128)(2,1)S(1)} %bitcast.88), channel_id=1, source_target_pairs={{0,8},{8,0},{1,9},{9,1},{2,10},{10,2},{3,11},{11,3},{4,12},{12,4},... | collective-permute-start | bytes 1572872 | tf_op jit(solution)/shard_map/gather_row/ppermute | solution.py:108
  120.9 4.5 %collective-permute-start.23 = (f32[136,128]{1,0:T(8,128)S(1)}, f32[136,128]{1,0:T(8,128)S(1)}, u32[]{:S(2)}, u32[]{:S(2)}) collective-permute-start(f32[136,128]{1,0:T(8,128)S(1)} %add.141), channel_id=1, source_target_pairs={{0,16},{16,0},{1,17},{17,1},{2,18},{18,2},{3,19},{19,3},{4,20},{20... | collective-permute-start | bytes 208904 | tf_op jit(solution)/shard_map/behind/weights/ppermute | solution.py:108
  125.4 7.3 %collective-permute-start.27 = (f32[136,128]{1,0:T(8,128)S(1)}, f32[136,128]{1,0:T(8,128)S(1)}, u32[]{:S(2)}, u32[]{:S(2)}) collective-permute-start(f32[136,128]{1,0:T(8,128)S(1)} %add.142), channel_id=1, source_target_pairs={{0,1},{1,0},{2,3},{3,2},{4,5},{5,4},{6,7},{7,6},{8,9},{9,8},{10,11... | collective-permute-start | bytes 208904 | tf_op jit(solution)/shard_map/scatter_col/weights/ppermute | solution.py:108
  125.5 7.7 %collective-permute-start.28 = (f32[136,128]{1,0:T(8,128)S(1)}, f32[136,128]{1,0:T(8,128)S(1)}, u32[]{:S(2)}, u32[]{:S(2)}) collective-permute-start(f32[136,128]{1,0:T(8,128)S(1)} %add.142), channel_id=1, source_target_pairs={{0,2},{1,3},{2,0},{3,1},{4,6},{5,7},{6,4},{7,5},{8,10},{9,11},{10,... | collective-permute-start | bytes 208904 | tf_op jit(solution)/shard_map/scatter_col/weights/ppermute | solution.py:108
  128.8 4.7 %collective-permute-start.29 = (f32[136,128]{1,0:T(8,128)S(1)}, f32[136,128]{1,0:T(8,128)S(1)}, u32[]{:S(2)}, u32[]{:S(2)}) collective-permute-start(f32[136,128]{1,0:T(8,128)S(1)} %add.142), channel_id=1, source_target_pairs={{0,3},{1,2},{2,1},{3,0},{4,7},{5,6},{6,5},{7,4},{8,11},{9,10},{10,... | collective-permute-start | bytes 208904 | tf_op jit(solution)/shard_map/scatter_col/weights/ppermute | solution.py:108
  129.3 4.2 %collective-permute-start.24 = (bf16[4,128,128]{2,1,0:T(8,128)(2,1)S(1)}, bf16[4,128,128]{2,1,0:T(8,128)(2,1)S(1)}, u32[]{:S(2)}, u32[]{:S(2)}) collective-permute-start(bf16[4,128,128]{2,1,0:T(8,128)(2,1)S(1)} %get-tuple-element.104), channel_id=1, source_target_pairs={{0,1},{1,0},{2,3},{3,2},{4,5},{5,4},{6,7},{7,6},{8,9},{9,8},{10,11... | collective-permute-start | bytes 393224 | tf_op jit(solution)/shard_map/scatter_col/ppermute | solution.py:108
  129.3 8.1 %collective-permute-start.25 = (bf16[4,128,128]{2,1,0:T(8,128)(2,1)S(1)}, bf16[4,128,128]{2,1,0:T(8,128)(2,1)S(1)}, u32[]{:S(2)}, u32[]{:S(2)}) collective-permute-start(bf16[4,128,128]{2,1,0:T(8,128)(2,1)S(1)} %get-tuple-element.105), channel_id=1, source_target_pairs={{0,2},{1,3},{2,0},{3,1},{4,6},{5,7},{6,4},{7,5},{8,10},{9,11},{10,... | collective-permute-start | bytes 393224 | tf_op jit(solution)/shard_map/scatter_col/ppermute | solution.py:108
  132.7 7.2 %collective-permute-start.26 = (bf16[4,128,128]{2,1,0:T(8,128)(2,1)S(1)}, bf16[4,128,128]{2,1,0:T(8,128)(2,1)S(1)}, u32[]{:S(2)}, u32[]{:S(2)}) collective-permute-start(bf16[4,128,128]{2,1,0:T(8,128)(2,1)S(1)} %get-tuple-element.106), channel_id=1, source_target_pairs={{0,3},{1,2},{2,1},{3,0},{4,7},{5,6},{6,5},{7,4},{8,11},{9,10},{10,... | collective-permute-start | bytes 393224 | tf_op jit(solution)/shard_map/scatter_col/ppermute | solution.py:108
  139.9 7.5 %collective-permute-start.31 = (f32[136,128]{1,0:T(8,128)S(1)}, f32[136,128]{1,0:T(8,128)S(1)}, u32[]{:S(2)}, u32[]{:S(2)}) collective-permute-start(f32[136,128]{1,0:T(8,128)S(1)} %add_add_fusion.1), channel_id=1, source_target_pairs={{0,64},{32,96},{64,0},{96,32},{128,192},{160,224},{192,128},{224,1... | collective-permute-start | bytes 208904 | tf_op jit(solution)/shard_map/weights/ppermute | solution.py:108
  143.1 7.4 %collective-permute-start.32 = (f32[136,128]{1,0:T(8,128)S(1)}, f32[136,128]{1,0:T(8,128)S(1)}, u32[]{:S(2)}, u32[]{:S(2)}) collective-permute-start(f32[136,128]{1,0:T(8,128)S(1)} %add_add_fusion.1), channel_id=1, source_target_pairs={{0,128},{32,160},{64,192},{96,224},{128,0},{160,32},{192,64},{224,... | collective-permute-start | bytes 208904 | tf_op jit(solution)/shard_map/weights/ppermute | solution.py:108
  147.2 6.3 %collective-permute-start.33 = (f32[136,128]{1,0:T(8,128)S(1)}, f32[136,128]{1,0:T(8,128)S(1)}, u32[]{:S(2)}, u32[]{:S(2)}) collective-permute-start(f32[136,128]{1,0:T(8,128)S(1)} %add_add_fusion.1), channel_id=1, source_target_pairs={{0,192},{32,224},{64,128},{96,160},{128,64},{160,96},{192,0},{224,... | collective-permute-start | bytes 208904 | tf_op jit(solution)/shard_map/weights/ppermute | solution.py:108
  147.4 6.1 %collective-permute-start.30 = (bf16[2,128,128]{2,1,0:T(8,128)(2,1)S(1)}, bf16[2,128,128]{2,1,0:T(8,128)(2,1)S(1)}, u32[]{:S(2)}, u32[]{:S(2)}) collective-permute-start(bf16[2,128,128]{2,1,0:T(8,128)(2,1)S(1)} %slice.24), channel_id=1, source_target_pairs={{0,4},{4,0},{1,5},{5,1},{2,6},{6,2},{3,7},{7,3},{8,12},{12,8},{9,1... | collective-permute-start | bytes 196616 | tf_op jit(solution)/shard_map/scatter_col/ppermute | solution.py:108
  153.5 2.2 %collective-permute-start.34 = (f32[136,128]{1,0:T(8,128)S(1)}, f32[136,128]{1,0:T(8,128)S(1)}, u32[]{:S(2)}, u32[]{:S(2)}) collective-permute-start(f32[136,128]{1,0:T(8,128)S(1)} %add_add_fusion), channel_id=1, source_target_pairs={{0,8},{8,0},{1,9},{9,1},{2,10},{10,2},{3,11},{11,3},{4,12},{12,4},... | collective-permute-start | bytes 208904 | tf_op jit(solution)/shard_map/weights/ppermute | solution.py:108

commit v5 on v3

--- a/solution.py
+++ b/solution.py
@@ -244,7 +244,7 @@
     )(co, *args)
 
 
-STEPS = ((("co", 1),), (("xh", 1),), (), (("z", 4),), (), (("xl", 1),), (("y", 1, 2, 3),), (("z", 1, 2, 3),))
+STEPS = ((("co", 1),), (("xh", 1),), (), (("z", 6),), (), (("xl", 1),), (("y", 1, 2, 3),), (("z", 1, 2, 3),))
 
 
 def body(features, tiles, tile_src, tile_dst, tile_count, degree, w_self, w_neigh, bias, upstream):

time: 157 us -> 157 us (level)
  Pallas kernels: 15 us -> 20.5 us
  waiting for transfers between devices: 58.6 us -> 54 us
    ppermute x31, waiting for transfers between devices: 55 us -> 48 us  [flip(): return lax.ppermute(x, axis, [(i, i ^ d) for i in range(n)])]
    pallas_call x4, Pallas kernels: 11.5 us -> 17 us  [products(): pl.pallas_call(kernel, in_specs=[pl.BlockSpec(memory_space=pltpu.SMEM)] *...]
    ppermute x31, starting transfers between devices: 56 us -> 52.8 us  [flip(): return lax.ppermute(x, axis, [(i, i ^ d) for i in range(n)])]
    all_to_all x2, starting transfers between devices: 7.31 us -> 9.5 us  [aggregate(): lax.all_to_all(both.reshape(16, -1, TILE), ('z', 'xl'), 0, 0, tiled=True)]
    all_to_all x2, waiting for transfers between devices: 0.01 us -> 2 us  [aggregate(): lax.all_to_all(both.reshape(16, -1, TILE), ('z', 'xl'), 0, 0, tiled=True)]
  transfers between devices with their start and end apart: 35 -> 35, of which waited for: 18 -> 20; matrix products, arithmetic and copies ran while one was open for 2% -> 2% of each run, Pallas kernels for 8% -> 12%
where the time goes in v5:
time: 157 us
  starting transfers between devices  75.7 us (48%)
  waiting for transfers between devices  54 us (34%)
  Pallas kernels  20.5 us (13%)
  other arithmetic  3.73 us (2%)
  between operations  1.69 us (1%)
    ppermute x31, starting transfers between devices, flip(): return lax.ppermute(x, axis, [(i, i ^ d) for i in range(n)])  52.8 us
    ppermute x31, waiting for transfers between devices, flip(): return lax.ppermute(x, axis, [(i, i ^ d) for i in range(n)])  48 us
    pallas_call x4, Pallas kernels, products(): pl.pallas_call(kernel, in_specs=[pl.BlockSpec(memory_space=pltpu.SMEM)] *...  17 us
    all_to_all x2, starting transfers between devices, aggregate(): lax.all_to_all(copies, ('z', 'xl'), 0, 0, tiled=True)  13.4 us
    all_to_all x2, starting transfers between devices, aggregate(): lax.all_to_all(both.reshape(16, -1, TILE), ('z', 'xl'), 0, 0, tiled=True)  9.5 us
    all_to_all x2, waiting for transfers between devices, aggregate(): lax.all_to_all(copies, ('z', 'xl'), 0, 0, tiled=True)  4 us
  transfers between devices with their start and end apart: 35, of which 20 were waited for; matrix products, arithmetic and copies ran while one was open for 2% of the time, Pallas kernels for 12%

profile of v5, /device:TPU:1, one launch (start us, length us, event | category | flops | bytes accessed | tf_op | source)
XLA Modules:
  0.0 156.7 jit_solution(11361095838007359011)
XLA Ops:
  0.7 3.7 %collective-permute-start = (bf16[2,128,128]{2,1,0:T(8,128)(2,1)}, bf16[2,128,128]{2,1,0:T(8,128)(2,1)S(1)}, u32[]{:S(2)}, u32[]{:S(2)}) collective-permute-start(bf16[2,128,128]{2,1,0:T(8,128)(2,1)} %bitcast.75), channel_id=1, source_target_pairs={{0,4},{4,0},{1,5},{5,1},{2,6},{6,2},{3,7},{7,3},{8,12},{12,8},{9,1... | collective-permute-start | bytes 196616 | tf_op jit(solution)/shard_map/gather_col/ppermute | solution.py:108
  4.3 0.9 copy-done
  5.2 1.2 prepare.1
  6.4 8.3 %all-to-all-start = ((bf16[16,2,128,128]{3,2,1,0:T(8,128)(2,1)}), bf16[16,2,128,128]{3,2,1,0:T(8,128)(2,1)S(1)}, u32[]{:S(2)}, u32[]{:S(2)}) async-start(bf16[16,2,128,128]{3,2,1,0:T(8,128)(2,1)} %prepare.1), calls=%async_computation | async-start | bytes 2097152 | tf_op jit(solution)/shard_map/gather_row/all_to_all | solution.py:127
  15.4 1.4 collective-permute-start.1
  16.8 2.6 %collective-permute-start.2 = (bf16[2,2,128,128]{3,2,1,0:T(8,128)(2,1)S(1)}, bf16[2,2,128,128]{3,2,1,0:T(8,128)(2,1)S(1)}, u32[]{:S(2)}, u32[]{:S(2)}) collective-permute-start(bf16[2,2,128,128]{3,2,1,0:T(8,128)(2,1)S(1)} %pad_maximum_fusion.1.f0), channel_id=1, source_target_pairs={{0,2},{1,3},{2,0},{3,1},{4,6},{5,7},{6,4},{7,5},{8,10},{9,11},{10,... | collective-permute-start | bytes 393224 | tf_op jit(solution)/shard_map/gather_col/ppermute | solution.py:108
  19.5 0.1 collective-permute-done.1.f1
  19.6 4.8 %collective-permute-done.2.f2 = bf16[2,2,128,128]{3,2,1,0:T(8,128)(2,1)S(1)} collective-permute-done((bf16[2,2,128,128]{3,2,1,0:T(8,128)(2,1)S(1)}, bf16[2,2,128,128]{3,2,1,0:T(8,128)(2,1)S(1)}, u32[]{:S(2)}, u32[]{:S(2)}) %collective-permute-start.2) | collective-permute-done | bytes 131104 | tf_op jit(solution)/shard_map/gather_col/ppermute | solution.py:108
  24.4 2.6 %collective-permute-done.3.f3 = bf16[2,2,128,128]{3,2,1,0:T(8,128)(2,1)S(1)} collective-permute-done((bf16[2,2,128,128]{3,2,1,0:T(8,128)(2,1)S(1)}, bf16[2,2,128,128]{3,2,1,0:T(8,128)(2,1)S(1)}, u32[]{:S(2)}, u32[]{:S(2)}) %collective-permute-start.3) | collective-permute-done | bytes 131104 | tf_op jit(solution)/shard_map/gather_col/ppermute | solution.py:108
  27.0 4.3 %ahead.2 = (f32[32,128,128]{2,1,0:T(8,128)S(1)}, f32[32,128,128]{2,1,0:T(8,128)S(1)}) custom-call(s32[96]{0:T(128)S(1)} %get-tuple-element.104.src_ref, s32[96]{0:T(128)S(1)} %get-tuple-element.103.slot_ref, s32[1]{0:T(128)} %bitcast.67.count_ref, bf16[2,2,128,128]{3,2,1,0:T(8,128)(2,1)S(1)} %pad_maximum_fusion.1.f0, ...), custom_call_target="tpu_custom_call" | custom-call | flops 3221225472 | bytes 3145728 | tf_op jit(solution)/shard_map/ahead/ahead/pallas_call | solution.py:85
  31.3 0.3 multiply_convert_fusion.1
  31.6 0.1 collective-permute-start.4
  31.7 2.6 %collective-permute-done.4 = f16[32,128,128]{2,1,0:T(8,128)(2,1)S(1)} collective-permute-done((f16[32,128,128]{2,1,0:T(8,128)(2,1)S(1)}, f16[32,128,128]{2,1,0:T(8,128)(2,1)S(1)}, u32[]{:S(2)}, u32[]{:S(2)}) %collective-permute-start.4) | collective-permute-done | bytes 1048608 | tf_op jit(solution)/shard_map/scatter_row/ppermute | solution.py:108
  34.3 1.4 multiply_convert_fusion
  35.7 4.0 %all-to-all-done = bf16[16,2,128,128]{3,2,1,0:T(8,128)(2,1)S(1)} async-done(((bf16[16,2,128,128]{3,2,1,0:T(8,128)(2,1)}), bf16[16,2,128,128]{3,2,1,0:T(8,128)(2,1)S(1)}, u32[]{:S(2)}, u32[]{:S(2)}) %all-to-all-start) | async-done | bytes 1048608 | tf_op jit(solution)/shard_map/gather_row/all_to_all | solution.py:127
  39.7 4.3 %collective-permute-start.5 = (bf16[32,128,128]{2,1,0:T(8,128)(2,1)S(1)}, bf16[32,128,128]{2,1,0:T(8,128)(2,1)S(1)}, u32[]{:S(2)}, u32[]{:S(2)}) collective-permute-start(bf16[32,128,128]{2,1,0:T(8,128)(2,1)S(1)} %bitcast.73), channel_id=1, source_target_pairs={{0,8},{8,0},{1,9},{9,1},{2,10},{10,2},{3,11},{11,3},{4,12},{12,4},... | collective-permute-start | bytes 3145736 | tf_op jit(solution)/shard_map/gather_row/ppermute | solution.py:108
  44.0 3.7 %all-to-all-start.1 = ((f16[16,256,128]{2,1,0:T(8,128)(2,1)}), f16[16,256,128]{2,1,0:T(8,128)(2,1)S(1)}, u32[]{:S(2)}, u32[]{:S(2)}) async-start(f16[16,256,128]{2,1,0:T(8,128)(2,1)} %bitcast.83), calls=%async_computation.1 | async-start | bytes 2097152 | tf_op jit(solution)/shard_map/scatter_row/all_to_all | solution.py:141
  47.7 4.3 %behind.2 = (f32[4,128,128]{2,1,0:T(8,128)S(1)}, f32[4,128,128]{2,1,0:T(8,128)S(1)}, f32[4,128,128]{2,1,0:T(8,128)S(1)}, f32[4,128,128]{2,1,0:T(8,128)S(1)}) custom-call(s32[96]{0:T(128)S(1)} %get-tuple-element.104.src_ref, s32[96]{0:T(128)S(1)} %get-tuple-element.103.slot_ref, s32[1]{0:T(128)} %bitcast.68.count_ref, bf16[32,128,128]{2,1,0:T(8,128)(2,1)S(1)} %bitcast.74, ...), custom_call_target="tpu_custom_call" | custom-call | flops 3221225472 | bytes 3145728 | tf_op jit(solution)/shard_map/behind/behind/pallas_call | solution.py:85
  52.0 0.1 collective-permute-start.6
  52.2 2.6 %collective-permute-start.7 = (f16[4,128,128]{2,1,0:T(8,128)(2,1)S(1)}, f16[4,128,128]{2,1,0:T(8,128)(2,1)S(1)}, u32[]{:S(2)}, u32[]{:S(2)}) collective-permute-start(f16[4,128,128]{2,1,0:T(8,128)(2,1)S(1)} %multiply_convert_fusion.3), channel_id=1, source_target_pairs={{0,2},{1,3},{2,0},{3,1},{4,6},{5,7},{6,4},{7,5},{8,10},{9,11},{10,... | collective-permute-start | bytes 393224 | tf_op jit(solution)/shard_map/scatter_col/ppermute | solution.py:108
  54.8 1.4 collective-permute-start.8
  56.2 1.1 collective-permute-done.6
  57.4 2.2 %collective-permute-done.7 = f16[4,128,128]{2,1,0:T(8,128)(2,1)S(1)} collective-permute-done((f16[4,128,128]{2,1,0:T(8,128)(2,1)S(1)}, f16[4,128,128]{2,1,0:T(8,128)(2,1)S(1)}, u32[]{:S(2)}, u32[]{:S(2)}) %collective-permute-start.7) | collective-permute-done | bytes 131104 | tf_op jit(solution)/shard_map/scatter_col/ppermute | solution.py:108
  59.6 2.8 %collective-permute-done.8 = f16[4,128,128]{2,1,0:T(8,128)(2,1)S(1)} collective-permute-done((f16[4,128,128]{2,1,0:T(8,128)(2,1)S(1)}, f16[4,128,128]{2,1,0:T(8,128)(2,1)S(1)}, u32[]{:S(2)}, u32[]{:S(2)}) %collective-permute-start.8) | collective-permute-done | bytes 131104 | tf_op jit(solution)/shard_map/scatter_col/ppermute | solution.py:108
  62.5 4.5 %collective-permute-start.9 = (f16[2,128,128]{2,1,0:T(8,128)(2,1)S(1)}, f16[2,128,128]{2,1,0:T(8,128)(2,1)S(1)}, u32[]{:S(2)}, u32[]{:S(2)}) collective-permute-start(f16[2,128,128]{2,1,0:T(8,128)(2,1)S(1)} %get-tuple-element.102), channel_id=1, source_target_pairs={{0,4},{4,0},{1,5},{5,1},{2,6},{6,2},{3,7},{7,3},{8,12},{12,8},{9,1... | collective-permute-start | bytes 196616 | tf_op jit(solution)/shard_map/scatter_col/ppermute | solution.py:108
  67.0 5.7 %collective-permute-done.9 = f16[2,128,128]{2,1,0:T(8,128)(2,1)S(1)} collective-permute-done((f16[2,128,128]{2,1,0:T(8,128)(2,1)S(1)}, f16[2,128,128]{2,1,0:T(8,128)(2,1)S(1)}, u32[]{:S(2)}, u32[]{:S(2)}) %collective-permute-start.9) | collective-permute-done | bytes 65568 | tf_op jit(solution)/shard_map/scatter_col/ppermute | solution.py:108
  72.7 2.0 %all-to-all-done.1 = f16[16,256,128]{2,1,0:T(8,128)(2,1)S(1)} async-done(((f16[16,256,128]{2,1,0:T(8,128)(2,1)}), f16[16,256,128]{2,1,0:T(8,128)(2,1)S(1)}, u32[]{:S(2)}, u32[]{:S(2)}) %all-to-all-start.1) | async-done | bytes 1048608 | tf_op jit(solution)/shard_map/scatter_row/all_to_all | solution.py:141
  74.7 0.2 multiply_reduce_fusion
  74.9 0.1 broadcast_in_dim.15.inverse_ref
  75.0 1.5 middle.1
  76.6 2.3 %collective-permute-start.11 = (f32[136,128]{1,0:T(8,128)S(1)}, f32[136,128]{1,0:T(8,128)S(1)}, u32[]{:S(2)}, u32[]{:S(2)}) collective-permute-start(f32[136,128]{1,0:T(8,128)S(1)} %dynamic-slice_bitcast_fusion), channel_id=1, source_target_pairs={{0,8},{8,0},{1,9},{9,1},{2,10},{10,2},{3,11},{11,3},{4,12},{12,4},... | collective-permute-start | bytes 208904 | tf_op jit(solution)/shard_map/gather_col/weights/ppermute | solution.py:108
  78.9 1.7 %collective-permute-start.10 = (bf16[2,128,128]{2,1,0:T(8,128)(2,1)S(1)}, bf16[2,128,128]{2,1,0:T(8,128)(2,1)S(1)}, u32[]{:S(2)}, u32[]{:S(2)}) collective-permute-start(bf16[2,128,128]{2,1,0:T(8,128)(2,1)S(1)} %bitcast.79), channel_id=1, source_target_pairs={{0,4},{4,0},{1,5},{5,1},{2,6},{6,2},{3,7},{7,3},{8,12},{12,8},{9,1... | collective-permute-start | bytes 196616 | tf_op jit(solution)/shard_map/gather_col/ppermute | solution.py:108
  80.7 5.1 %all-to-all-start.2 = ((bf16[16,2,128,128]{3,2,1,0:T(8,128)(2,1)}), bf16[16,2,128,128]{3,2,1,0:T(8,128)(2,1)S(1)}, u32[]{:S(2)}, u32[]{:S(2)}) async-start(bf16[16,2,128,128]{3,2,1,0:T(8,128)(2,1)} %get-tuple-element.62), calls=%async_computation.2 | async-start | bytes 2097152 | tf_op jit(solution)/shard_map/gather_row/all_to_all | solution.py:127
  85.8 0.7 collective-permute-start.12
  86.5 3.1 %collective-permute-start.13 = (bf16[2,2,128,128]{3,2,1,0:T(8,128)(2,1)S(1)}, bf16[2,2,128,128]{3,2,1,0:T(8,128)(2,1)S(1)}, u32[]{:S(2)}, u32[]{:S(2)}) collective-permute-start(bf16[2,2,128,128]{3,2,1,0:T(8,128)(2,1)S(1)} %pad_maximum_fusion.2.f0), channel_id=1, source_target_pairs={{0,2},{1,3},{2,0},{3,1},{4,6},{5,7},{6,4},{7,5},{8,10},{9,11},{10,... | collective-permute-start | bytes 393224 | tf_op jit(solution)/shard_map/gather_col/ppermute | solution.py:108
  89.6 0.2 collective-permute-start.14
  89.8 1.8 %collective-permute-start.15 = (f32[136,128]{1,0:T(8,128)S(1)}, f32[136,128]{1,0:T(8,128)S(1)}, u32[]{:S(2)}, u32[]{:S(2)}) collective-permute-start(f32[136,128]{1,0:T(8,128)S(1)} %bitcast_add_fusion.2), channel_id=1, source_target_pairs={{0,4},{4,0},{1,5},{5,1},{2,6},{6,2},{3,7},{7,3},{8,12},{12,8},{9,1... | collective-permute-start | bytes 208904 | tf_op jit(solution)/shard_map/gather_col/weights/ppermute | solution.py:108
  91.6 3.2 %collective-permute-done.15 = f32[136,128]{1,0:T(8,128)S(1)} collective-permute-done((f32[136,128]{1,0:T(8,128)S(1)}, f32[136,128]{1,0:T(8,128)S(1)}, u32[]{:S(2)}, u32[]{:S(2)}) %collective-permute-start.15) | collective-permute-done | bytes 69664 | tf_op jit(solution)/shard_map/gather_col/weights/ppermute | solution.py:108
  94.8 0.6 collective-permute-done.13.f2
  95.3 2.5 %collective-permute-done.14.f3 = bf16[2,2,128,128]{3,2,1,0:T(8,128)(2,1)S(1)} collective-permute-done((bf16[2,2,128,128]{3,2,1,0:T(8,128)(2,1)S(1)}, bf16[2,2,128,128]{3,2,1,0:T(8,128)(2,1)S(1)}, u32[]{:S(2)}, u32[]{:S(2)}) %collective-permute-start.14) | collective-permute-done | bytes 131104 | tf_op jit(solution)/shard_map/gather_col/ppermute | solution.py:108
  97.8 4.2 %ahead.3 = (f32[32,128,128]{2,1,0:T(8,128)S(1)}, bf16[32,128,128]{2,1,0:T(8,128)(2,1)S(1)}) custom-call(s32[96]{0:T(128)S(1)} %get-tuple-element.104.src_ref, s32[96]{0:T(128)S(1)} %get-tuple-element.103.slot_ref, s32[1]{0:T(128)} %bitcast.69.count_ref, bf16[2,2,128,128]{3,2,1,0:T(8,128)(2,1)S(1)} %pad_maximum_fusion.2.f0, ...), custom_call_target="tpu_custom_call" | custom-call | flops 3221225472 | bytes 3145728 | tf_op jit(solution)/shard_map/ahead/ahead/pallas_call | solution.py:85
  102.1 0.1 collective-permute-start.17
  102.2 3.1 %collective-permute-start.16 = (f32[136,128]{1,0:T(8,128)S(1)}, f32[136,128]{1,0:T(8,128)S(1)}, u32[]{:S(2)}, u32[]{:S(2)}) collective-permute-start(f32[136,128]{1,0:T(8,128)S(1)} %add.119), channel_id=1, source_target_pairs={{0,192},{32,224},{64,128},{96,160},{128,64},{160,96},{192,0},{224,... | collective-permute-start | bytes 208904 | tf_op jit(solution)/shard_map/weights/ppermute | solution.py:108
  105.3 8.2 %collective-permute-done.16 = f32[136,128]{1,0:T(8,128)S(1)} collective-permute-done((f32[136,128]{1,0:T(8,128)S(1)}, f32[136,128]{1,0:T(8,128)S(1)}, u32[]{:S(2)}, u32[]{:S(2)}) %collective-permute-start.16) | collective-permute-done | bytes 69664 | tf_op jit(solution)/shard_map/weights/ppermute | solution.py:108
  113.5 1.3 add_convert_fusion
  114.8 1.6 collective-permute-start.18
  116.4 5.9 %all-to-all-start.3 = ((bf16[16,256,128]{2,1,0:T(8,128)(2,1)}), bf16[16,256,128]{2,1,0:T(8,128)(2,1)S(1)}, u32[]{:S(2)}, u32[]{:S(2)}) async-start(bf16[16,256,128]{2,1,0:T(8,128)(2,1)} %bitcast.82), calls=%async_computation.3 | async-start | bytes 2097152 | tf_op jit(solution)/shard_map/scatter_row/all_to_all | solution.py:141
  122.3 1.4 collective-permute-start.19
  123.7 4.2 %behind.3 = (f32[4,128,128]{2,1,0:T(8,128)S(1)}, bf16[4,128,128]{2,1,0:T(8,128)(2,1)S(1)}, bf16[4,128,128]{2,1,0:T(8,128)(2,1)S(1)}, bf16[4,128,128]{2,1,0:T(8,128)(2,1)S(1)}) custom-call(s32[96]{0:T(128)S(1)} %get-tuple-element.104.src_ref, s32[96]{0:T(128)S(1)} %get-tuple-element.103.slot_ref, s32[1]{0:T(128)} %bitcast.70.count_ref, ...), custom_call_target="tpu_custom_call" | custom-call | flops 3221225472 | bytes 3145728 | tf_op jit(solution)/shard_map/behind/behind/pallas_call | solution.py:85
  128.0 0.1 collective-permute-start.23
  128.1 3.0 %collective-permute-start.24 = (f32[136,128]{1,0:T(8,128)S(1)}, f32[136,128]{1,0:T(8,128)S(1)}, u32[]{:S(2)}, u32[]{:S(2)}) collective-permute-start(f32[136,128]{1,0:T(8,128)S(1)} %add.122), channel_id=1, source_target_pairs={{0,2},{1,3},{2,0},{3,1},{4,6},{5,7},{6,4},{7,5},{8,10},{9,11},{10,... | collective-permute-start | bytes 208904 | tf_op jit(solution)/shard_map/scatter_col/weights/ppermute | solution.py:108
  131.0 0.9 collective-permute-start.25
  131.9 3.0 %collective-permute-start.21 = (bf16[4,128,128]{2,1,0:T(8,128)(2,1)S(1)}, bf16[4,128,128]{2,1,0:T(8,128)(2,1)S(1)}, u32[]{:S(2)}, u32[]{:S(2)}) collective-permute-start(bf16[4,128,128]{2,1,0:T(8,128)(2,1)S(1)} %get-tuple-element.89), channel_id=1, source_target_pairs={{0,2},{1,3},{2,0},{3,1},{4,6},{5,7},{6,4},{7,5},{8,10},{9,11},{10,... | collective-permute-start | bytes 393224 | tf_op jit(solution)/shard_map/scatter_col/ppermute | solution.py:108
  134.9 0.9 collective-permute-start.22
  135.8 0.7 collective-permute-done.25
  136.5 2.5 %collective-permute-done.21 = bf16[4,128,128]{2,1,0:T(8,128)(2,1)S(1)} collective-permute-done((bf16[4,128,128]{2,1,0:T(8,128)(2,1)S(1)}, bf16[4,128,128]{2,1,0:T(8,128)(2,1)S(1)}, u32[]{:S(2)}, u32[]{:S(2)}) %collective-permute-start.21) | collective-permute-done | bytes 131104 | tf_op jit(solution)/shard_map/scatter_col/ppermute | solution.py:108
  139.0 3.7 %collective-permute-done.22 = bf16[4,128,128]{2,1,0:T(8,128)(2,1)S(1)} collective-permute-done((bf16[4,128,128]{2,1,0:T(8,128)(2,1)S(1)}, bf16[4,128,128]{2,1,0:T(8,128)(2,1)S(1)}, u32[]{:S(2)}, u32[]{:S(2)}) %collective-permute-start.22) | collective-permute-done | bytes 131104 | tf_op jit(solution)/shard_map/scatter_col/ppermute | solution.py:108
  142.7 1.3 collective-permute-start.27
  144.0 2.4 %collective-permute-start.28 = (f32[136,128]{1,0:T(8,128)S(1)}, f32[136,128]{1,0:T(8,128)S(1)}, u32[]{:S(2)}, u32[]{:S(2)}) collective-permute-start(f32[136,128]{1,0:T(8,128)S(1)} %add_add_fusion.1), channel_id=1, source_target_pairs={{0,64},{32,96},{64,0},{96,32},{128,192},{160,224},{192,128},{224,1... | collective-permute-start | bytes 208904 | tf_op jit(solution)/shard_map/weights/ppermute | solution.py:108
  146.5 2.8 %collective-permute-start.26 = (bf16[2,128,128]{2,1,0:T(8,128)(2,1)S(1)}, bf16[2,128,128]{2,1,0:T(8,128)(2,1)S(1)}, u32[]{:S(2)}, u32[]{:S(2)}) collective-permute-start(bf16[2,128,128]{2,1,0:T(8,128)(2,1)S(1)} %slice.24), channel_id=1, source_target_pairs={{0,4},{4,0},{1,5},{5,1},{2,6},{6,2},{3,7},{7,3},{8,12},{12,8},{9,1... | collective-permute-start | bytes 196616 | tf_op jit(solution)/shard_map/scatter_col/ppermute | solution.py:108
  149.3 3.7 %collective-permute-done.29 = f32[136,128]{1,0:T(8,128)S(1)} collective-permute-done((f32[136,128]{1,0:T(8,128)S(1)}, f32[136,128]{1,0:T(8,128)S(1)}, u32[]{:S(2)}, u32[]{:S(2)}) %collective-permute-start.29) | collective-permute-done | bytes 69664 | tf_op jit(solution)/shard_map/weights/ppermute | solution.py:108
  153.1 1.9 %collective-permute-start.30 = (f32[136,128]{1,0:T(8,128)S(1)}, f32[136,128]{1,0:T(8,128)S(1)}, u32[]{:S(2)}, u32[]{:S(2)}) collective-permute-start(f32[136,128]{1,0:T(8,128)S(1)} %add_add_fusion), channel_id=1, source_target_pairs={{0,8},{8,0},{1,9},{9,1},{2,10},{10,2},{3,11},{11,3},{4,12},{12,4},... | collective-permute-start | bytes 208904 | tf_op jit(solution)/shard_map/weights/ppermute | solution.py:108
  155.0 0.9 collective-permute-done.30
  155.9 0.8 final.1
  (58 shorter events, 0.7 us)
Async XLA Ops:
  0.6 18.8 %copy-start.8 = (s32[1,1,96]{2,1,0:T(1,128)S(1)}, s32[1,1,96]{2,1,0:T(1,128)}, u32[]{:S(2)}) copy-start(s32[1,1,96]{2,1,0:T(1,128)} %param.12) | copy-start | bytes 1156
  0.6 18.8 %copy-start.7 = (s32[1,1,96]{2,1,0:T(1,128)S(1)}, s32[1,1,96]{2,1,0:T(1,128)}, u32[]{:S(2)}) copy-start(s32[1,1,96]{2,1,0:T(1,128)} %param.13) | copy-start | bytes 1156
  0.7 14.7 %collective-permute-start = (bf16[2,128,128]{2,1,0:T(8,128)(2,1)}, bf16[2,128,128]{2,1,0:T(8,128)(2,1)S(1)}, u32[]{:S(2)}, u32[]{:S(2)}) collective-permute-start(bf16[2,128,128]{2,1,0:T(8,128)(2,1)} %bitcast.75), channel_id=1, source_target_pairs={{0,4},{4,0},{1,5},{5,1},{2,6},{6,2},{3,7},{7,3},{8,12},{12,8},{9,1... | collective-permute-start | bytes 196616 | tf_op jit(solution)/shard_map/gather_col/ppermute | solution.py:108
  4.3 0.9 copy-start
  5.2 10.2 %copy-start.1 = (bf16[256,128]{1,0:T(8,128)(2,1)S(1)}, bf16[256,128]{1,0:T(8,128)(2,1)}, u32[]{:S(2)}) copy-start(bf16[256,128]{1,0:T(8,128)(2,1)} %features_ref.3) | copy-start | bytes 196612
  6.4 33.4 %all-to-all-start = ((bf16[16,2,128,128]{3,2,1,0:T(8,128)(2,1)}), bf16[16,2,128,128]{3,2,1,0:T(8,128)(2,1)S(1)}, u32[]{:S(2)}, u32[]{:S(2)}) async-start(bf16[16,2,128,128]{3,2,1,0:T(8,128)(2,1)} %prepare.1), calls=%async_computation | async-start | bytes 2097152 | tf_op jit(solution)/shard_map/gather_row/all_to_all | solution.py:127
  15.4 4.2 %collective-permute-start.1 = (bf16[2,2,128,128]{3,2,1,0:T(8,128)(2,1)S(1)}, bf16[2,2,128,128]{3,2,1,0:T(8,128)(2,1)S(1)}, u32[]{:S(2)}, u32[]{:S(2)}) collective-permute-start(bf16[2,2,128,128]{3,2,1,0:T(8,128)(2,1)S(1)} %pad_maximum_fusion.1.f0), channel_id=1, source_target_pairs={{0,1},{1,0},{2,3},{3,2},{4,5},{5,4},{6,7},{7,6},{8,9},{9,8},{10,11... | collective-permute-start | bytes 393224 | tf_op jit(solution)/shard_map/gather_col/ppermute | solution.py:108
  16.8 7.6 %collective-permute-start.2 = (bf16[2,2,128,128]{3,2,1,0:T(8,128)(2,1)S(1)}, bf16[2,2,128,128]{3,2,1,0:T(8,128)(2,1)S(1)}, u32[]{:S(2)}, u32[]{:S(2)}) collective-permute-start(bf16[2,2,128,128]{3,2,1,0:T(8,128)(2,1)S(1)} %pad_maximum_fusion.1.f0), channel_id=1, source_target_pairs={{0,2},{1,3},{2,0},{3,1},{4,6},{5,7},{6,4},{7,5},{8,10},{9,11},{10,... | collective-permute-start | bytes 393224 | tf_op jit(solution)/shard_map/gather_col/ppermute | solution.py:108
  19.4 7.6 %collective-permute-start.3 = (bf16[2,2,128,128]{3,2,1,0:T(8,128)(2,1)S(1)}, bf16[2,2,128,128]{3,2,1,0:T(8,128)(2,1)S(1)}, u32[]{:S(2)}, u32[]{:S(2)}) collective-permute-start(bf16[2,2,128,128]{3,2,1,0:T(8,128)(2,1)S(1)} %pad_maximum_fusion.1.f0), channel_id=1, source_target_pairs={{0,3},{1,2},{2,1},{3,0},{4,7},{5,6},{6,5},{7,4},{8,11},{9,10},{10,... | collective-permute-start | bytes 393224 | tf_op jit(solution)/shard_map/gather_col/ppermute | solution.py:108
  31.6 2.7 %collective-permute-start.4 = (f16[32,128,128]{2,1,0:T(8,128)(2,1)S(1)}, f16[32,128,128]{2,1,0:T(8,128)(2,1)S(1)}, u32[]{:S(2)}, u32[]{:S(2)}) collective-permute-start(f16[32,128,128]{2,1,0:T(8,128)(2,1)S(1)} %multiply_convert_fusion.1), channel_id=1, source_target_pairs={{0,8},{8,0},{1,9},{9,1},{2,10},{10,2},{3,11},{11,3},{4,12},{12,4},... | collective-permute-start | bytes 3145736 | tf_op jit(solution)/shard_map/scatter_row/ppermute | solution.py:108
  39.7 7.9 %collective-permute-start.5 = (bf16[32,128,128]{2,1,0:T(8,128)(2,1)S(1)}, bf16[32,128,128]{2,1,0:T(8,128)(2,1)S(1)}, u32[]{:S(2)}, u32[]{:S(2)}) collective-permute-start(bf16[32,128,128]{2,1,0:T(8,128)(2,1)S(1)} %bitcast.73), channel_id=1, source_target_pairs={{0,8},{8,0},{1,9},{9,1},{2,10},{10,2},{3,11},{11,3},{4,12},{12,4},... | collective-permute-start | bytes 3145736 | tf_op jit(solution)/shard_map/gather_row/ppermute | solution.py:108
  44.0 30.7 %all-to-all-start.1 = ((f16[16,256,128]{2,1,0:T(8,128)(2,1)}), f16[16,256,128]{2,1,0:T(8,128)(2,1)S(1)}, u32[]{:S(2)}, u32[]{:S(2)}) async-start(f16[16,256,128]{2,1,0:T(8,128)(2,1)} %bitcast.83), calls=%async_computation.1 | async-start | bytes 2097152 | tf_op jit(solution)/shard_map/scatter_row/all_to_all | solution.py:141
  52.0 15.0 %copy-start.6 = (s32[256]{0:T(256)S(1)}, s32[256]{0:T(256)}, u32[]{:S(2)}) copy-start(s32[256]{0:T(256)} %param.15) | copy-start | bytes 3076
  52.0 5.4 %collective-permute-start.6 = (f16[4,128,128]{2,1,0:T(8,128)(2,1)S(1)}, f16[4,128,128]{2,1,0:T(8,128)(2,1)S(1)}, u32[]{:S(2)}, u32[]{:S(2)}) collective-permute-start(f16[4,128,128]{2,1,0:T(8,128)(2,1)S(1)} %multiply_convert_fusion.4), channel_id=1, source_target_pairs={{0,1},{1,0},{2,3},{3,2},{4,5},{5,4},{6,7},{7,6},{8,9},{9,8},{10,11... | collective-permute-start | bytes 393224 | tf_op jit(solution)/shard_map/scatter_col/ppermute | solution.py:108
  52.1 22.9 %copy-start.2 = (bf16[256,128]{1,0:T(8,128)(2,1)S(1)}, bf16[256,128]{1,0:T(8,128)(2,1)}, u32[]{:S(2)}) copy-start(bf16[256,128]{1,0:T(8,128)(2,1)} %upstream_ref.1) | copy-start | bytes 196612
  52.1 22.9 %copy-start.3 = (bf16[128,128]{1,0:T(8,128)(2,1)S(1)}, bf16[128,128]{1,0:T(8,128)(2,1)}, u32[]{:S(2)}) copy-start(bf16[128,128]{1,0:T(8,128)(2,1)} %w_self_ref.1) | copy-start | bytes 98308
  52.1 22.9 %copy-start.4 = (bf16[128,128]{1,0:T(8,128)(2,1)S(1)}, bf16[128,128]{1,0:T(8,128)(2,1)}, u32[]{:S(2)}) copy-start(bf16[128,128]{1,0:T(8,128)(2,1)} %w_neigh_ref.1) | copy-start | bytes 98308
  52.2 22.9 %copy-start.5 = (f32[128]{0:T(128)S(1)}, f32[128]{0:T(128)}, u32[]{:S(2)}) copy-start(f32[128]{0:T(128)} %param.18) | copy-start | bytes 1540
  52.2 7.4 %collective-permute-start.7 = (f16[4,128,128]{2,1,0:T(8,128)(2,1)S(1)}, f16[4,128,128]{2,1,0:T(8,128)(2,1)S(1)}, u32[]{:S(2)}, u32[]{:S(2)}) collective-permute-start(f16[4,128,128]{2,1,0:T(8,128)(2,1)S(1)} %multiply_convert_fusion.3), channel_id=1, source_target_pairs={{0,2},{1,3},{2,0},{3,1},{4,6},{5,7},{6,4},{7,5},{8,10},{9,11},{10,... | collective-permute-start | bytes 393224 | tf_op jit(solution)/shard_map/scatter_col/ppermute | solution.py:108
  54.8 7.6 %collective-permute-start.8 = (f16[4,128,128]{2,1,0:T(8,128)(2,1)S(1)}, f16[4,128,128]{2,1,0:T(8,128)(2,1)S(1)}, u32[]{:S(2)}, u32[]{:S(2)}) collective-permute-start(f16[4,128,128]{2,1,0:T(8,128)(2,1)S(1)} %multiply_convert_fusion.2), channel_id=1, source_target_pairs={{0,3},{1,2},{2,1},{3,0},{4,7},{5,6},{6,5},{7,4},{8,11},{9,10},{10,... | collective-permute-start | bytes 393224 | tf_op jit(solution)/shard_map/scatter_col/ppermute | solution.py:108
  62.5 10.1 %collective-permute-start.9 = (f16[2,128,128]{2,1,0:T(8,128)(2,1)S(1)}, f16[2,128,128]{2,1,0:T(8,128)(2,1)S(1)}, u32[]{:S(2)}, u32[]{:S(2)}) collective-permute-start(f16[2,128,128]{2,1,0:T(8,128)(2,1)S(1)} %get-tuple-element.102), channel_id=1, source_target_pairs={{0,4},{4,0},{1,5},{5,1},{2,6},{6,2},{3,7},{7,3},{8,12},{12,8},{9,1... | collective-permute-start | bytes 196616 | tf_op jit(solution)/shard_map/scatter_col/ppermute | solution.py:108
  76.6 9.2 %collective-permute-start.11 = (f32[136,128]{1,0:T(8,128)S(1)}, f32[136,128]{1,0:T(8,128)S(1)}, u32[]{:S(2)}, u32[]{:S(2)}) collective-permute-start(f32[136,128]{1,0:T(8,128)S(1)} %dynamic-slice_bitcast_fusion), channel_id=1, source_target_pairs={{0,8},{8,0},{1,9},{9,1},{2,10},{10,2},{3,11},{11,3},{4,12},{12,4},... | collective-permute-start | bytes 208904 | tf_op jit(solution)/shard_map/gather_col/weights/ppermute | solution.py:108
  78.9 6.9 %collective-permute-start.10 = (bf16[2,128,128]{2,1,0:T(8,128)(2,1)S(1)}, bf16[2,128,128]{2,1,0:T(8,128)(2,1)S(1)}, u32[]{:S(2)}, u32[]{:S(2)}) collective-permute-start(bf16[2,128,128]{2,1,0:T(8,128)(2,1)S(1)} %bitcast.79), channel_id=1, source_target_pairs={{0,4},{4,0},{1,5},{5,1},{2,6},{6,2},{3,7},{7,3},{8,12},{12,8},{9,1... | collective-permute-start | bytes 196616 | tf_op jit(solution)/shard_map/gather_col/ppermute | solution.py:108
  80.7 34.2 %all-to-all-start.2 = ((bf16[16,2,128,128]{3,2,1,0:T(8,128)(2,1)}), bf16[16,2,128,128]{3,2,1,0:T(8,128)(2,1)S(1)}, u32[]{:S(2)}, u32[]{:S(2)}) async-start(bf16[16,2,128,128]{3,2,1,0:T(8,128)(2,1)} %get-tuple-element.62), calls=%async_computation.2 | async-start | bytes 2097152 | tf_op jit(solution)/shard_map/gather_row/all_to_all | solution.py:127
  85.8 8.9 %collective-permute-start.12 = (bf16[2,2,128,128]{3,2,1,0:T(8,128)(2,1)S(1)}, bf16[2,2,128,128]{3,2,1,0:T(8,128)(2,1)S(1)}, u32[]{:S(2)}, u32[]{:S(2)}) collective-permute-start(bf16[2,2,128,128]{3,2,1,0:T(8,128)(2,1)S(1)} %pad_maximum_fusion.2.f0), channel_id=1, source_target_pairs={{0,1},{1,0},{2,3},{3,2},{4,5},{5,4},{6,7},{7,6},{8,9},{9,8},{10,11... | collective-permute-start | bytes 393224 | tf_op jit(solution)/shard_map/gather_col/ppermute | solution.py:108
  86.5 8.8 %collective-permute-start.13 = (bf16[2,2,128,128]{3,2,1,0:T(8,128)(2,1)S(1)}, bf16[2,2,128,128]{3,2,1,0:T(8,128)(2,1)S(1)}, u32[]{:S(2)}, u32[]{:S(2)}) collective-permute-start(bf16[2,2,128,128]{3,2,1,0:T(8,128)(2,1)S(1)} %pad_maximum_fusion.2.f0), channel_id=1, source_target_pairs={{0,2},{1,3},{2,0},{3,1},{4,6},{5,7},{6,4},{7,5},{8,10},{9,11},{10,... | collective-permute-start | bytes 393224 | tf_op jit(solution)/shard_map/gather_col/ppermute | solution.py:108
  89.6 8.3 %collective-permute-start.14 = (bf16[2,2,128,128]{3,2,1,0:T(8,128)(2,1)S(1)}, bf16[2,2,128,128]{3,2,1,0:T(8,128)(2,1)S(1)}, u32[]{:S(2)}, u32[]{:S(2)}) collective-permute-start(bf16[2,2,128,128]{3,2,1,0:T(8,128)(2,1)S(1)} %pad_maximum_fusion.2.f0), channel_id=1, source_target_pairs={{0,3},{1,2},{2,1},{3,0},{4,7},{5,6},{6,5},{7,4},{8,11},{9,10},{10,... | collective-permute-start | bytes 393224 | tf_op jit(solution)/shard_map/gather_col/ppermute | solution.py:108
  89.8 5.0 %collective-permute-start.15 = (f32[136,128]{1,0:T(8,128)S(1)}, f32[136,128]{1,0:T(8,128)S(1)}, u32[]{:S(2)}, u32[]{:S(2)}) collective-permute-start(f32[136,128]{1,0:T(8,128)S(1)} %bitcast_add_fusion.2), channel_id=1, source_target_pairs={{0,4},{4,0},{1,5},{5,1},{2,6},{6,2},{3,7},{7,3},{8,12},{12,8},{9,1... | collective-permute-start | bytes 208904 | tf_op jit(solution)/shard_map/gather_col/weights/ppermute | solution.py:108
  102.1 11.4 %collective-permute-start.17 = (bf16[32,128,128]{2,1,0:T(8,128)(2,1)S(1)}, bf16[32,128,128]{2,1,0:T(8,128)(2,1)S(1)}, u32[]{:S(2)}, u32[]{:S(2)}) collective-permute-start(bf16[32,128,128]{2,1,0:T(8,128)(2,1)S(1)} %get-tuple-element.77), channel_id=1, source_target_pairs={{0,8},{8,0},{1,9},{9,1},{2,10},{10,2},{3,11},{11,3},{4,12},{12,4},... | collective-permute-start | bytes 3145736 | tf_op jit(solution)/shard_map/scatter_row/ppermute | solution.py:108
  102.2 11.3 %collective-permute-start.16 = (f32[136,128]{1,0:T(8,128)S(1)}, f32[136,128]{1,0:T(8,128)S(1)}, u32[]{:S(2)}, u32[]{:S(2)}) collective-permute-start(f32[136,128]{1,0:T(8,128)S(1)} %add.119), channel_id=1, source_target_pairs={{0,192},{32,224},{64,128},{96,160},{128,64},{160,96},{192,0},{224,... | collective-permute-start | bytes 208904 | tf_op jit(solution)/shard_map/weights/ppermute | solution.py:108
  114.8 7.4 %collective-permute-start.18 = (bf16[32,128,128]{2,1,0:T(8,128)(2,1)S(1)}, bf16[32,128,128]{2,1,0:T(8,128)(2,1)S(1)}, u32[]{:S(2)}, u32[]{:S(2)}) collective-permute-start(bf16[32,128,128]{2,1,0:T(8,128)(2,1)S(1)} %bitcast.71), channel_id=1, source_target_pairs={{0,8},{8,0},{1,9},{9,1},{2,10},{10,2},{3,11},{11,3},{4,12},{12,4},... | collective-permute-start | bytes 3145736 | tf_op jit(solution)/shard_map/gather_row/ppermute | solution.py:108
  116.4 39.5 %all-to-all-start.3 = ((bf16[16,256,128]{2,1,0:T(8,128)(2,1)}), bf16[16,256,128]{2,1,0:T(8,128)(2,1)S(1)}, u32[]{:S(2)}, u32[]{:S(2)}) async-start(bf16[16,256,128]{2,1,0:T(8,128)(2,1)} %bitcast.82), calls=%async_computation.3 | async-start | bytes 2097152 | tf_op jit(solution)/shard_map/scatter_row/all_to_all | solution.py:141
  122.3 5.7 %collective-permute-start.19 = (f32[136,128]{1,0:T(8,128)S(1)}, f32[136,128]{1,0:T(8,128)S(1)}, u32[]{:S(2)}, u32[]{:S(2)}) collective-permute-start(f32[136,128]{1,0:T(8,128)S(1)} %add.120), channel_id=1, source_target_pairs={{0,16},{16,0},{1,17},{17,1},{2,18},{18,2},{3,19},{19,3},{4,20},{20... | collective-permute-start | bytes 208904 | tf_op jit(solution)/shard_map/behind/weights/ppermute | solution.py:108
  128.0 6.9 %collective-permute-start.23 = (f32[136,128]{1,0:T(8,128)S(1)}, f32[136,128]{1,0:T(8,128)S(1)}, u32[]{:S(2)}, u32[]{:S(2)}) collective-permute-start(f32[136,128]{1,0:T(8,128)S(1)} %add.122), channel_id=1, source_target_pairs={{0,1},{1,0},{2,3},{3,2},{4,5},{5,4},{6,7},{7,6},{8,9},{9,8},{10,11... | collective-permute-start | bytes 208904 | tf_op jit(solution)/shard_map/scatter_col/weights/ppermute | solution.py:108
  128.1 7.7 %collective-permute-start.24 = (f32[136,128]{1,0:T(8,128)S(1)}, f32[136,128]{1,0:T(8,128)S(1)}, u32[]{:S(2)}, u32[]{:S(2)}) collective-permute-start(f32[136,128]{1,0:T(8,128)S(1)} %add.122), channel_id=1, source_target_pairs={{0,2},{1,3},{2,0},{3,1},{4,6},{5,7},{6,4},{7,5},{8,10},{9,11},{10,... | collective-permute-start | bytes 208904 | tf_op jit(solution)/shard_map/scatter_col/weights/ppermute | solution.py:108
  131.0 5.4 %collective-permute-start.25 = (f32[136,128]{1,0:T(8,128)S(1)}, f32[136,128]{1,0:T(8,128)S(1)}, u32[]{:S(2)}, u32[]{:S(2)}) collective-permute-start(f32[136,128]{1,0:T(8,128)S(1)} %add.122), channel_id=1, source_target_pairs={{0,3},{1,2},{2,1},{3,0},{4,7},{5,6},{6,5},{7,4},{8,11},{9,10},{10,... | collective-permute-start | bytes 208904 | tf_op jit(solution)/shard_map/scatter_col/weights/ppermute | solution.py:108
  131.9 4.6 %collective-permute-start.20 = (bf16[4,128,128]{2,1,0:T(8,128)(2,1)S(1)}, bf16[4,128,128]{2,1,0:T(8,128)(2,1)S(1)}, u32[]{:S(2)}, u32[]{:S(2)}) collective-permute-start(bf16[4,128,128]{2,1,0:T(8,128)(2,1)S(1)} %get-tuple-element.88), channel_id=1, source_target_pairs={{0,1},{1,0},{2,3},{3,2},{4,5},{5,4},{6,7},{7,6},{8,9},{9,8},{10,11... | collective-permute-start | bytes 393224 | tf_op jit(solution)/shard_map/scatter_col/ppermute | solution.py:108
  131.9 7.1 %collective-permute-start.21 = (bf16[4,128,128]{2,1,0:T(8,128)(2,1)S(1)}, bf16[4,128,128]{2,1,0:T(8,128)(2,1)S(1)}, u32[]{:S(2)}, u32[]{:S(2)}) collective-permute-start(bf16[4,128,128]{2,1,0:T(8,128)(2,1)S(1)} %get-tuple-element.89), channel_id=1, source_target_pairs={{0,2},{1,3},{2,0},{3,1},{4,6},{5,7},{6,4},{7,5},{8,10},{9,11},{10,... | collective-permute-start | bytes 393224 | tf_op jit(solution)/shard_map/scatter_col/ppermute | solution.py:108
  134.9 7.8 %collective-permute-start.22 = (bf16[4,128,128]{2,1,0:T(8,128)(2,1)S(1)}, bf16[4,128,128]{2,1,0:T(8,128)(2,1)S(1)}, u32[]{:S(2)}, u32[]{:S(2)}) collective-permute-start(bf16[4,128,128]{2,1,0:T(8,128)(2,1)S(1)} %get-tuple-element.90), channel_id=1, source_target_pairs={{0,3},{1,2},{2,1},{3,0},{4,7},{5,6},{6,5},{7,4},{8,11},{9,10},{10,... | collective-permute-start | bytes 393224 | tf_op jit(solution)/shard_map/scatter_col/ppermute | solution.py:108
  142.7 6.5 %collective-permute-start.27 = (f32[136,128]{1,0:T(8,128)S(1)}, f32[136,128]{1,0:T(8,128)S(1)}, u32[]{:S(2)}, u32[]{:S(2)}) collective-permute-start(f32[136,128]{1,0:T(8,128)S(1)} %add_add_fusion.1), channel_id=1, source_target_pairs={{0,32},{32,0},{64,96},{96,64},{128,160},{160,128},{192,224},{224,1... | collective-permute-start | bytes 208904 | tf_op jit(solution)/shard_map/weights/ppermute | solution.py:108
  144.0 5.3 %collective-permute-start.28 = (f32[136,128]{1,0:T(8,128)S(1)}, f32[136,128]{1,0:T(8,128)S(1)}, u32[]{:S(2)}, u32[]{:S(2)}) collective-permute-start(f32[136,128]{1,0:T(8,128)S(1)} %add_add_fusion.1), channel_id=1, source_target_pairs={{0,64},{32,96},{64,0},{96,32},{128,192},{160,224},{192,128},{224,1... | collective-permute-start | bytes 208904 | tf_op jit(solution)/shard_map/weights/ppermute | solution.py:108
  146.4 6.6 %collective-permute-start.29 = (f32[136,128]{1,0:T(8,128)S(1)}, f32[136,128]{1,0:T(8,128)S(1)}, u32[]{:S(2)}, u32[]{:S(2)}) collective-permute-start(f32[136,128]{1,0:T(8,128)S(1)} %add_add_fusion.1), channel_id=1, source_target_pairs={{0,96},{32,64},{64,32},{96,0},{128,224},{160,192},{192,160},{224,1... | collective-permute-start | bytes 208904 | tf_op jit(solution)/shard_map/weights/ppermute | solution.py:108
  146.5 6.6 %collective-permute-start.26 = (bf16[2,128,128]{2,1,0:T(8,128)(2,1)S(1)}, bf16[2,128,128]{2,1,0:T(8,128)(2,1)S(1)}, u32[]{:S(2)}, u32[]{:S(2)}) collective-permute-start(bf16[2,128,128]{2,1,0:T(8,128)(2,1)S(1)} %slice.24), channel_id=1, source_target_pairs={{0,4},{4,0},{1,5},{5,1},{2,6},{6,2},{3,7},{7,3},{8,12},{12,8},{9,1... | collective-permute-start | bytes 196616 | tf_op jit(solution)/shard_map/scatter_col/ppermute | solution.py:108
  153.1 2.8 %collective-permute-start.30 = (f32[136,128]{1,0:T(8,128)S(1)}, f32[136,128]{1,0:T(8,128)S(1)}, u32[]{:S(2)}, u32[]{:S(2)}) collective-permute-start(f32[136,128]{1,0:T(8,128)S(1)} %add_add_fusion), channel_id=1, source_target_pairs={{0,8},{8,0},{1,9},{9,1},{2,10},{10,2},{3,11},{11,3},{4,12},{12,4},... | collective-permute-start | bytes 208904 | tf_op jit(solution)/shard_map/weights/ppermute | solution.py:108

commit v6 on v4

--- a/solution.py
+++ b/solution.py
@@ -248,7 +248,7 @@
     )(co, *args)
 
 
-STEPS = ((("co", 1),), (("xh", 1),), (), (("z", 1),), (), (("xl", 1),), (("y", 1, 2, 3),), (("z", 2, 4, 6),))
+STEPS = ((("co", 1),), (("xh", 1),), (), (("z", 6),), (), (("xl", 1),), (("y", 1, 2, 3),), (("z", 1, 2, 3),))
 
 
 def body(features, tiles, tile_src, tile_dst, tile_count, degree, w_self, w_neigh, bias, upstream):

time: 157 us -> 156 us (level)
  starting transfers between devices: 79.7 us -> 87.9 us
  waiting for transfers between devices: 53.1 us -> 46.8 us
  Pallas kernels: 15.3 us -> 13.7 us
    ppermute x35, waiting for transfers between devices: 49.1 us -> 42.6 us  [flip(): return lax.ppermute(x, axis, [(i, i ^ d) for i in range(n)])]
    ppermute x35, starting transfers between devices: 47.2 us -> 53.6 us  [flip(): return lax.ppermute(x, axis, [(i, i ^ d) for i in range(n)])]
    all_to_all x2, starting transfers between devices: 14.9 us -> 17.2 us  [aggregate(): lax.all_to_all(both.reshape(16, -1, TILE), ('z', 'xl'), 0, 0, tiled=True)]
    pallas_call x4, Pallas kernels: 12.3 us -> 10.7 us  [products(): pl.pallas_call(kernel, in_specs=[pl.BlockSpec(memory_space=pltpu.SMEM)] *...]
  transfers between devices with their start and end apart: 39 -> 39, of which waited for: 25 -> 26; matrix products, arithmetic and copies ran while one was open for 3% -> 3% of each run, Pallas kernels for 4% -> 3%
where the time goes in v6:
time: 156 us; the launch traced here: 157 us
  starting transfers between devices  87.9 us (56%)
  waiting for transfers between devices  46.8 us (30%)
  Pallas kernels  13.7 us (9%)
  other arithmetic  5.77 us (4%)
  between operations  1.63 us (1%)
    ppermute x35, starting transfers between devices, flip(): return lax.ppermute(x, axis, [(i, i ^ d) for i in range(n)])  53.6 us
    ppermute x35, waiting for transfers between devices, flip(): return lax.ppermute(x, axis, [(i, i ^ d) for i in range(n)])  42.6 us
    all_to_all x2, starting transfers between devices, aggregate(): lax.all_to_all(both.reshape(16, -1, TILE), ('z', 'xl'), 0, 0, tiled=True)  17.2 us
    all_to_all x2, starting transfers between devices, aggregate(): g00 = lax.all_to_all(copies, 'z', 0, 0, tiled=True).reshape(-1, TILE, TILE)  17.1 us
    pallas_call x4, Pallas kernels, products(): pl.pallas_call(kernel, in_specs=[pl.BlockSpec(memory_space=pltpu.SMEM)] *...  10.7 us
    all_to_all x2, waiting for transfers between devices, aggregate(): g00 = lax.all_to_all(copies, 'z', 0, 0, tiled=True).reshape(-1, TILE, TILE)  4.25 us
  transfers between devices with their start and end apart: 39, of which 26 were waited for; matrix products, arithmetic and copies ran while one was open for 3% of the time, Pallas kernels for 3%

profile of v6, /device:TPU:1, one launch (start us, length us, event | category | flops | bytes accessed | tf_op | source)
XLA Modules:
  0.0 156.8 jit_solution(961759899813145211)
XLA Ops:
  0.6 0.8 copy-done
  1.5 0.9 prepare.1
  2.4 9.0 %all-to-all-start = ((bf16[8,2,128,128]{3,2,1,0:T(8,128)(2,1)}), bf16[8,2,128,128]{3,2,1,0:T(8,128)(2,1)S(1)}, u32[]{:S(2)}, u32[]{:S(2)}) async-start(bf16[8,2,128,128]{3,2,1,0:T(8,128)(2,1)} %prepare.1), calls=%async_computation | async-start | bytes 1048576 | tf_op jit(solution)/shard_map/gather_row/all_to_all | solution.py:127
  11.4 2.7 %collective-permute-start = (bf16[2,128,128]{2,1,0:T(8,128)(2,1)}, bf16[2,128,128]{2,1,0:T(8,128)(2,1)S(1)}, u32[]{:S(2)}, u32[]{:S(2)}) collective-permute-start(bf16[2,128,128]{2,1,0:T(8,128)(2,1)} %bitcast.93), channel_id=1, source_target_pairs={{0,4},{4,0},{1,5},{5,1},{2,6},{6,2},{3,7},{7,3},{8,12},{12,8},{9,1... | collective-permute-start | bytes 196616 | tf_op jit(solution)/shard_map/gather_col/ppermute | solution.py:108
  15.5 0.8 collective-permute-done
  16.3 0.9 pad_maximum_fusion.1.f0
  17.1 1.4 collective-permute-start.1
  18.5 2.6 %collective-permute-start.2 = (bf16[2,2,128,128]{3,2,1,0:T(8,128)(2,1)S(1)}, bf16[2,2,128,128]{3,2,1,0:T(8,128)(2,1)S(1)}, u32[]{:S(2)}, u32[]{:S(2)}) collective-permute-start(bf16[2,2,128,128]{3,2,1,0:T(8,128)(2,1)S(1)} %pad_maximum_fusion.1.f0), channel_id=1, source_target_pairs={{0,2},{1,3},{2,0},{3,1},{4,6},{5,7},{6,4},{7,5},{8,10},{9,11},{10,... | collective-permute-start | bytes 393224 | tf_op jit(solution)/shard_map/gather_col/ppermute | solution.py:108
  21.8 3.2 %collective-permute-done.2.f2 = bf16[2,2,128,128]{3,2,1,0:T(8,128)(2,1)S(1)} collective-permute-done((bf16[2,2,128,128]{3,2,1,0:T(8,128)(2,1)S(1)}, bf16[2,2,128,128]{3,2,1,0:T(8,128)(2,1)S(1)}, u32[]{:S(2)}, u32[]{:S(2)}) %collective-permute-start.2) | collective-permute-done | bytes 131104 | tf_op jit(solution)/shard_map/gather_col/ppermute | solution.py:108
  25.0 1.6 collective-permute-done.3.f3
  26.6 2.8 %all-to-all-done = bf16[8,2,128,128]{3,2,1,0:T(8,128)(2,1)S(1)} async-done(((bf16[8,2,128,128]{3,2,1,0:T(8,128)(2,1)}), bf16[8,2,128,128]{3,2,1,0:T(8,128)(2,1)S(1)}, u32[]{:S(2)}, u32[]{:S(2)}) %all-to-all-start) | async-done | bytes 524320 | tf_op jit(solution)/shard_map/gather_row/all_to_all | solution.py:127
  29.4 2.7 %ahead.2 = (f32[32,128,128]{2,1,0:T(8,128)S(1)}, f32[32,128,128]{2,1,0:T(8,128)S(1)}) custom-call(s32[96]{0:T(128)S(1)} %fusion.2.src_ref, s32[96]{0:T(128)S(1)} %get-tuple-element.117.slot_ref, s32[1]{0:T(128)} %bitcast.83.count_ref, bf16[2,2,128,128]{3,2,1,0:T(8,128)(2,1)S(1)} %pad_maximum_fusion.1.f0, ...), custom_call_target="tpu_custom_call" | custom-call | flops 3221225472 | bytes 3145728 | tf_op jit(solution)/shard_map/ahead/ahead/pallas_call | solution.py:85
  32.4 1.5 collective-permute-start.4
  33.9 1.2 collective-permute-start.5
  35.1 1.1 collective-permute-done.4
  36.2 1.4 multiply_convert_fusion
  37.6 8.8 %all-to-all-start.1 = ((f16[16,256,128]{2,1,0:T(8,128)(2,1)}), f16[16,256,128]{2,1,0:T(8,128)(2,1)S(1)}, u32[]{:S(2)}, u32[]{:S(2)}) async-start(f16[16,256,128]{2,1,0:T(8,128)(2,1)} %bitcast.9), calls=%async_computation.1 | async-start | bytes 2097152 | tf_op jit(solution)/shard_map/scatter_row/all_to_all | solution.py:144
  46.4 0.7 collective-permute-start.6
  47.4 0.9 collective-permute-start.7
  48.7 1.1 collective-permute-done.7.g3
  49.8 2.7 %behind.2 = (f32[4,128,128]{2,1,0:T(8,128)S(1)}, bf16[4,128,128]{2,1,0:T(8,128)(2,1)S(1)}, bf16[4,128,128]{2,1,0:T(8,128)(2,1)S(1)}, bf16[4,128,128]{2,1,0:T(8,128)(2,1)S(1)}) custom-call(s32[96]{0:T(128)S(1)} %fusion.2.src_ref, s32[96]{0:T(128)S(1)} %add_select_fusion.slot_ref, s32[1]{0:T(128)} %bitcast.84.count_ref, bf16[16,128,128]{2,1,0:T(8,128)(2,1)S(1)} %bitcast.92, ...), custom_call_target="tpu_custom_call" | custom-call | flops 402653184 | bytes 3145728 | tf_op jit(solution)/shard_map/behind/behind/pallas_call | solution.py:85
  52.5 2.3 %collective-permute-start.10 = (bf16[4,128,128]{2,1,0:T(8,128)(2,1)S(1)}, bf16[4,128,128]{2,1,0:T(8,128)(2,1)S(1)}, u32[]{:S(2)}, u32[]{:S(2)}) collective-permute-start(bf16[4,128,128]{2,1,0:T(8,128)(2,1)S(1)} %get-tuple-element.72), channel_id=1, source_target_pairs={{0,3},{1,2},{2,1},{3,0},{4,7},{5,6},{6,5},{7,4},{8,11},{9,10},{10,... | collective-permute-start | bytes 393224 | tf_op jit(solution)/shard_map/scatter_col/ppermute | solution.py:108
  54.9 1.4 collective-permute-start.8
  56.3 1.0 collective-permute-start.9
  58.0 1.0 collective-permute-done.8
  59.0 3.4 %collective-permute-done.9 = bf16[4,128,128]{2,1,0:T(8,128)(2,1)S(1)} collective-permute-done((bf16[4,128,128]{2,1,0:T(8,128)(2,1)S(1)}, bf16[4,128,128]{2,1,0:T(8,128)(2,1)S(1)}, u32[]{:S(2)}, u32[]{:S(2)}) %collective-permute-start.9) | collective-permute-done | bytes 131104 | tf_op jit(solution)/shard_map/scatter_col/ppermute | solution.py:108
  62.5 4.9 %collective-permute-start.11 = (f16[2,128,128]{2,1,0:T(8,128)(2,1)S(1)}, f16[2,128,128]{2,1,0:T(8,128)(2,1)S(1)}, u32[]{:S(2)}, u32[]{:S(2)}) collective-permute-start(f16[2,128,128]{2,1,0:T(8,128)(2,1)S(1)} %get-tuple-element.121), channel_id=1, source_target_pairs={{0,4},{4,0},{1,5},{5,1},{2,6},{6,2},{3,7},{7,3},{8,12},{12,8},{9,1... | collective-permute-start | bytes 196616 | tf_op jit(solution)/shard_map/scatter_col/ppermute | solution.py:108
  67.5 5.0 %collective-permute-done.11 = f16[2,128,128]{2,1,0:T(8,128)(2,1)S(1)} collective-permute-done((f16[2,128,128]{2,1,0:T(8,128)(2,1)S(1)}, f16[2,128,128]{2,1,0:T(8,128)(2,1)S(1)}, u32[]{:S(2)}, u32[]{:S(2)}) %collective-permute-start.11) | collective-permute-done | bytes 65568 | tf_op jit(solution)/shard_map/scatter_col/ppermute | solution.py:108
  72.9 1.3 middle.1
  74.1 8.0 %all-to-all-start.2 = ((bf16[8,2,128,128]{3,2,1,0:T(8,128)(2,1)}), bf16[8,2,128,128]{3,2,1,0:T(8,128)(2,1)S(1)}, u32[]{:S(2)}, u32[]{:S(2)}) async-start(bf16[8,2,128,128]{3,2,1,0:T(8,128)(2,1)} %get-tuple-element.74), calls=%async_computation.2 | async-start | bytes 1048576 | tf_op jit(solution)/shard_map/gather_row/all_to_all | solution.py:127
  82.2 1.0 collective-permute-start.13
  83.2 0.8 collective-permute-start.12
  84.1 4.2 %collective-permute-done.12 = bf16[2,128,128]{2,1,0:T(8,128)(2,1)S(1)} collective-permute-done((bf16[2,128,128]{2,1,0:T(8,128)(2,1)S(1)}, bf16[2,128,128]{2,1,0:T(8,128)(2,1)S(1)}, u32[]{:S(2)}, u32[]{:S(2)}) %collective-permute-start.12) | collective-permute-done | bytes 65568 | tf_op jit(solution)/shard_map/gather_col/ppermute | solution.py:108
  88.5 2.2 %collective-permute-start.15 = (bf16[2,2,128,128]{3,2,1,0:T(8,128)(2,1)S(1)}, bf16[2,2,128,128]{3,2,1,0:T(8,128)(2,1)S(1)}, u32[]{:S(2)}, u32[]{:S(2)}) collective-permute-start(bf16[2,2,128,128]{3,2,1,0:T(8,128)(2,1)S(1)} %pad_maximum_fusion.2.f0), channel_id=1, source_target_pairs={{0,2},{1,3},{2,0},{3,1},{4,6},{5,7},{6,4},{7,5},{8,10},{9,11},{10,... | collective-permute-start | bytes 393224 | tf_op jit(solution)/shard_map/gather_col/ppermute | solution.py:108
  90.7 1.7 %collective-permute-start.16 = (bf16[2,2,128,128]{3,2,1,0:T(8,128)(2,1)S(1)}, bf16[2,2,128,128]{3,2,1,0:T(8,128)(2,1)S(1)}, u32[]{:S(2)}, u32[]{:S(2)}) collective-permute-start(bf16[2,2,128,128]{3,2,1,0:T(8,128)(2,1)S(1)} %pad_maximum_fusion.2.f0), channel_id=1, source_target_pairs={{0,3},{1,2},{2,1},{3,0},{4,7},{5,6},{6,5},{7,4},{8,11},{9,10},{10,... | collective-permute-start | bytes 393224 | tf_op jit(solution)/shard_map/gather_col/ppermute | solution.py:108
  92.3 0.8 collective-permute-start.17
  93.1 4.2 %collective-permute-done.17 = f32[136,128]{1,0:T(8,128)S(1)} collective-permute-done((f32[136,128]{1,0:T(8,128)S(1)}, f32[136,128]{1,0:T(8,128)S(1)}, u32[]{:S(2)}, u32[]{:S(2)}) %collective-permute-start.17) | collective-permute-done | bytes 69664 | tf_op jit(solution)/shard_map/gather_col/weights/ppermute | solution.py:108
  97.3 1.3 collective-permute-done.16.f3
  98.7 1.5 all-to-all-done.2
  100.1 2.7 %ahead.3 = (f32[32,128,128]{2,1,0:T(8,128)S(1)}, bf16[32,128,128]{2,1,0:T(8,128)(2,1)S(1)}) custom-call(s32[96]{0:T(128)S(1)} %fusion.2.src_ref, s32[96]{0:T(128)S(1)} %get-tuple-element.117.slot_ref, s32[1]{0:T(128)} %bitcast.85.count_ref, bf16[2,2,128,128]{3,2,1,0:T(8,128)(2,1)S(1)} %pad_maximum_fusion.2.f0, ...), custom_call_target="tpu_custom_call" | custom-call | flops 3221225472 | bytes 3145728 | tf_op jit(solution)/shard_map/ahead/ahead/pallas_call | solution.py:85
  102.8 1.5 collective-permute-start.18
  104.3 2.4 %collective-permute-start.19 = (f32[136,128]{1,0:T(8,128)S(1)}, f32[136,128]{1,0:T(8,128)S(1)}, u32[]{:S(2)}, u32[]{:S(2)}) collective-permute-start(f32[136,128]{1,0:T(8,128)S(1)} %add.139), channel_id=1, source_target_pairs={{0,192},{32,224},{64,128},{96,160},{128,64},{160,96},{192,0},{224,... | collective-permute-start | bytes 208904 | tf_op jit(solution)/shard_map/scatter_row/weights/ppermute | solution.py:108
  106.6 2.1 %collective-permute-start.20 = (bf16[16,128,128]{2,1,0:T(8,128)(2,1)S(1)}, bf16[16,128,128]{2,1,0:T(8,128)(2,1)S(1)}, u32[]{:S(2)}, u32[]{:S(2)}) collective-permute-start(bf16[16,128,128]{2,1,0:T(8,128)(2,1)S(1)} %bitcast.87), channel_id=1, source_target_pairs={{0,16},{16,0},{1,17},{17,1},{2,18},{18,2},{3,19},{19,3},{4,20},{20... | collective-permute-start | bytes 1572872 | tf_op jit(solution)/shard_map/gather_row/ppermute | solution.py:108
  108.7 1.4 collective-permute-done.19
  110.1 1.3 add_convert_fusion
  111.5 8.4 %all-to-all-start.3 = ((bf16[16,256,128]{2,1,0:T(8,128)(2,1)}), bf16[16,256,128]{2,1,0:T(8,128)(2,1)S(1)}, u32[]{:S(2)}, u32[]{:S(2)}) async-start(bf16[16,256,128]{2,1,0:T(8,128)(2,1)} %bitcast.20), calls=%async_computation.3 | async-start | bytes 2097152 | tf_op jit(solution)/shard_map/scatter_row/all_to_all | solution.py:144
  119.9 0.8 collective-permute-done.20.g1
  120.7 0.9 collective-permute-start.22
  121.6 1.5 collective-permute-done.22.g3
  123.2 1.5 collective-permute-start.23
  124.6 2.7 %behind.3 = (f32[4,128,128]{2,1,0:T(8,128)S(1)}, bf16[4,128,128]{2,1,0:T(8,128)(2,1)S(1)}, bf16[4,128,128]{2,1,0:T(8,128)(2,1)S(1)}, bf16[4,128,128]{2,1,0:T(8,128)(2,1)S(1)}) custom-call(s32[96]{0:T(128)S(1)} %fusion.2.src_ref, s32[96]{0:T(128)S(1)} %add_select_fusion.slot_ref, s32[1]{0:T(128)} %bitcast.86.count_ref, bf16[16,128,128]{2,1,0:T(8,128)(2,1)S(1)} %bitcast.89, ...), custom_call_target="tpu_custom_call" | custom-call | flops 402653184 | bytes 3145728 | tf_op jit(solution)/shard_map/behind/behind/pallas_call | solution.py:85
  127.4 4.5 %collective-permute-start.28 = (f32[136,128]{1,0:T(8,128)S(1)}, f32[136,128]{1,0:T(8,128)S(1)}, u32[]{:S(2)}, u32[]{:S(2)}) collective-permute-start(f32[136,128]{1,0:T(8,128)S(1)} %add.142), channel_id=1, source_target_pairs={{0,2},{1,3},{2,0},{3,1},{4,6},{5,7},{6,4},{7,5},{8,10},{9,11},{10,... | collective-permute-start | bytes 208904 | tf_op jit(solution)/shard_map/scatter_col/weights/ppermute | solution.py:108
  131.9 3.9 %collective-permute-start.25 = (bf16[4,128,128]{2,1,0:T(8,128)(2,1)S(1)}, bf16[4,128,128]{2,1,0:T(8,128)(2,1)S(1)}, u32[]{:S(2)}, u32[]{:S(2)}) collective-permute-start(bf16[4,128,128]{2,1,0:T(8,128)(2,1)S(1)} %get-tuple-element.105), channel_id=1, source_target_pairs={{0,2},{1,3},{2,0},{3,1},{4,6},{5,7},{6,4},{7,5},{8,10},{9,11},{10,... | collective-permute-start | bytes 393224 | tf_op jit(solution)/shard_map/scatter_col/ppermute | solution.py:108
  135.8 1.1 collective-permute-done.29
  136.9 3.4 %collective-permute-done.25 = bf16[4,128,128]{2,1,0:T(8,128)(2,1)S(1)} collective-permute-done((bf16[4,128,128]{2,1,0:T(8,128)(2,1)S(1)}, bf16[4,128,128]{2,1,0:T(8,128)(2,1)S(1)}, u32[]{:S(2)}, u32[]{:S(2)}) %collective-permute-start.25) | collective-permute-done | bytes 131104 | tf_op jit(solution)/shard_map/scatter_col/ppermute | solution.py:108
  140.3 2.6 %collective-permute-done.26 = bf16[4,128,128]{2,1,0:T(8,128)(2,1)S(1)} collective-permute-done((bf16[4,128,128]{2,1,0:T(8,128)(2,1)S(1)}, bf16[4,128,128]{2,1,0:T(8,128)(2,1)S(1)}, u32[]{:S(2)}, u32[]{:S(2)}) %collective-permute-start.26) | collective-permute-done | bytes 131104 | tf_op jit(solution)/shard_map/scatter_col/ppermute | solution.py:108
  143.0 1.3 collective-permute-start.32
  144.3 2.3 %collective-permute-start.33 = (f32[136,128]{1,0:T(8,128)S(1)}, f32[136,128]{1,0:T(8,128)S(1)}, u32[]{:S(2)}, u32[]{:S(2)}) collective-permute-start(f32[136,128]{1,0:T(8,128)S(1)} %add_add_fusion.1), channel_id=1, source_target_pairs={{0,96},{32,64},{64,32},{96,0},{128,224},{160,192},{192,160},{224,1... | collective-permute-start | bytes 208904 | tf_op jit(solution)/shard_map/weights/ppermute | solution.py:108
  146.6 2.4 %collective-permute-start.30 = (bf16[2,128,128]{2,1,0:T(8,128)(2,1)S(1)}, bf16[2,128,128]{2,1,0:T(8,128)(2,1)S(1)}, u32[]{:S(2)}, u32[]{:S(2)}) collective-permute-start(bf16[2,128,128]{2,1,0:T(8,128)(2,1)S(1)} %slice.24), channel_id=1, source_target_pairs={{0,4},{4,0},{1,5},{5,1},{2,6},{6,2},{3,7},{7,3},{8,12},{12,8},{9,1... | collective-permute-start | bytes 196616 | tf_op jit(solution)/shard_map/scatter_col/ppermute | solution.py:108
  148.9 0.9 collective-permute-done.33
  149.8 1.6 %collective-permute-done.30 = bf16[2,128,128]{2,1,0:T(8,128)(2,1)S(1)} collective-permute-done((bf16[2,128,128]{2,1,0:T(8,128)(2,1)S(1)}, bf16[2,128,128]{2,1,0:T(8,128)(2,1)S(1)}, u32[]{:S(2)}, u32[]{:S(2)}) %collective-permute-start.30) | collective-permute-done | bytes 65568 | tf_op jit(solution)/shard_map/scatter_col/ppermute | solution.py:108
  151.4 3.6 %collective-permute-start.34 = (f32[136,128]{1,0:T(8,128)S(1)}, f32[136,128]{1,0:T(8,128)S(1)}, u32[]{:S(2)}, u32[]{:S(2)}) collective-permute-start(f32[136,128]{1,0:T(8,128)S(1)} %add_add_fusion), channel_id=1, source_target_pairs={{0,8},{8,0},{1,9},{9,1},{2,10},{10,2},{3,11},{11,3},{4,12},{12,4},... | collective-permute-start | bytes 208904 | tf_op jit(solution)/shard_map/weights/ppermute | solution.py:108
  155.1 0.9 collective-permute-done.34
  156.0 0.8 final.1
  (63 shorter events, 4.1 us)
Async XLA Ops:
  0.6 0.8 copy-start
  2.4 27.0 %all-to-all-start = ((bf16[8,2,128,128]{3,2,1,0:T(8,128)(2,1)}), bf16[8,2,128,128]{3,2,1,0:T(8,128)(2,1)S(1)}, u32[]{:S(2)}, u32[]{:S(2)}) async-start(bf16[8,2,128,128]{3,2,1,0:T(8,128)(2,1)} %prepare.1), calls=%async_computation | async-start | bytes 1048576 | tf_op jit(solution)/shard_map/gather_row/all_to_all | solution.py:127
  11.4 4.8 %collective-permute-start = (bf16[2,128,128]{2,1,0:T(8,128)(2,1)}, bf16[2,128,128]{2,1,0:T(8,128)(2,1)S(1)}, u32[]{:S(2)}, u32[]{:S(2)}) collective-permute-start(bf16[2,128,128]{2,1,0:T(8,128)(2,1)} %bitcast.93), channel_id=1, source_target_pairs={{0,4},{4,0},{1,5},{5,1},{2,6},{6,2},{3,7},{7,3},{8,12},{12,8},{9,1... | collective-permute-start | bytes 196616 | tf_op jit(solution)/shard_map/gather_col/ppermute | solution.py:108
  17.1 4.7 %collective-permute-start.1 = (bf16[2,2,128,128]{3,2,1,0:T(8,128)(2,1)S(1)}, bf16[2,2,128,128]{3,2,1,0:T(8,128)(2,1)S(1)}, u32[]{:S(2)}, u32[]{:S(2)}) collective-permute-start(bf16[2,2,128,128]{3,2,1,0:T(8,128)(2,1)S(1)} %pad_maximum_fusion.1.f0), channel_id=1, source_target_pairs={{0,1},{1,0},{2,3},{3,2},{4,5},{5,4},{6,7},{7,6},{8,9},{9,8},{10,11... | collective-permute-start | bytes 393224 | tf_op jit(solution)/shard_map/gather_col/ppermute | solution.py:108
  18.5 6.6 %collective-permute-start.2 = (bf16[2,2,128,128]{3,2,1,0:T(8,128)(2,1)S(1)}, bf16[2,2,128,128]{3,2,1,0:T(8,128)(2,1)S(1)}, u32[]{:S(2)}, u32[]{:S(2)}) collective-permute-start(bf16[2,2,128,128]{3,2,1,0:T(8,128)(2,1)S(1)} %pad_maximum_fusion.1.f0), channel_id=1, source_target_pairs={{0,2},{1,3},{2,0},{3,1},{4,6},{5,7},{6,4},{7,5},{8,10},{9,11},{10,... | collective-permute-start | bytes 393224 | tf_op jit(solution)/shard_map/gather_col/ppermute | solution.py:108
  21.1 5.5 %collective-permute-start.3 = (bf16[2,2,128,128]{3,2,1,0:T(8,128)(2,1)S(1)}, bf16[2,2,128,128]{3,2,1,0:T(8,128)(2,1)S(1)}, u32[]{:S(2)}, u32[]{:S(2)}) collective-permute-start(bf16[2,2,128,128]{3,2,1,0:T(8,128)(2,1)S(1)} %pad_maximum_fusion.1.f0), channel_id=1, source_target_pairs={{0,3},{1,2},{2,1},{3,0},{4,7},{5,6},{6,5},{7,4},{8,11},{9,10},{10,... | collective-permute-start | bytes 393224 | tf_op jit(solution)/shard_map/gather_col/ppermute | solution.py:108
  32.4 3.8 %collective-permute-start.4 = (f16[32,128,128]{2,1,0:T(8,128)(2,1)S(1)}, f16[32,128,128]{2,1,0:T(8,128)(2,1)S(1)}, u32[]{:S(2)}, u32[]{:S(2)}) collective-permute-start(f16[32,128,128]{2,1,0:T(8,128)(2,1)S(1)} %multiply_convert_fusion.1), channel_id=1, source_target_pairs={{0,8},{8,0},{1,9},{9,1},{2,10},{10,2},{3,11},{11,3},{4,12},{12,4},... | collective-permute-start | bytes 3145736 | tf_op jit(solution)/shard_map/scatter_row/ppermute | solution.py:108
  33.9 13.5 %collective-permute-start.5 = (bf16[16,128,128]{2,1,0:T(8,128)(2,1)S(1)}, bf16[16,128,128]{2,1,0:T(8,128)(2,1)S(1)}, u32[]{:S(2)}, u32[]{:S(2)}) collective-permute-start(bf16[16,128,128]{2,1,0:T(8,128)(2,1)S(1)} %bitcast.90), channel_id=1, source_target_pairs={{0,16},{16,0},{1,17},{17,1},{2,18},{18,2},{3,19},{19,3},{4,20},{20... | collective-permute-start | bytes 1572872 | tf_op jit(solution)/shard_map/gather_row/ppermute | solution.py:108
  37.6 10.6 %copy-start.6 = (s32[1,1,96]{2,1,0:T(1,128)S(1)}, s32[1,1,96]{2,1,0:T(1,128)}, u32[]{:S(2)}) copy-start(s32[1,1,96]{2,1,0:T(1,128)} %param.13) | copy-start | bytes 1156
  37.6 34.8 %all-to-all-start.1 = ((f16[16,256,128]{2,1,0:T(8,128)(2,1)}), f16[16,256,128]{2,1,0:T(8,128)(2,1)S(1)}, u32[]{:S(2)}, u32[]{:S(2)}) async-start(f16[16,256,128]{2,1,0:T(8,128)(2,1)} %bitcast.9), calls=%async_computation.1 | async-start | bytes 2097152 | tf_op jit(solution)/shard_map/scatter_row/all_to_all | solution.py:144
  46.4 2.3 %collective-permute-start.6 = (bf16[16,128,128]{2,1,0:T(8,128)(2,1)S(1)}, bf16[16,128,128]{2,1,0:T(8,128)(2,1)S(1)}, u32[]{:S(2)}, u32[]{:S(2)}) collective-permute-start(bf16[16,128,128]{2,1,0:T(8,128)(2,1)S(1)} %bitcast.91), channel_id=1, source_target_pairs={{0,8},{8,0},{1,9},{9,1},{2,10},{10,2},{3,11},{11,3},{4,12},{12,4},... | collective-permute-start | bytes 1572872 | tf_op jit(solution)/shard_map/gather_row/ppermute | solution.py:108
  47.4 2.4 %collective-permute-start.7 = (bf16[16,128,128]{2,1,0:T(8,128)(2,1)S(1)}, bf16[16,128,128]{2,1,0:T(8,128)(2,1)S(1)}, u32[]{:S(2)}, u32[]{:S(2)}) collective-permute-start(bf16[16,128,128]{2,1,0:T(8,128)(2,1)S(1)} %collective-permute-done.5.g1), channel_id=1, source_target_pairs={{0,8},{8,0},{1,9},{9,1},{2,10},{10,2},{3,11},{11,3},{4,12},{12,4},... | collective-permute-start | bytes 1572872 | tf_op jit(solution)/shard_map/gather_row/ppermute | solution.py:108
  49.8 17.7 %copy-start.7 = (s32[256]{0:T(256)S(1)}, s32[256]{0:T(256)}, u32[]{:S(2)}) copy-start(s32[256]{0:T(256)} %param.15) | copy-start | bytes 3076
  52.5 20.3 %copy-start.1 = (bf16[256,128]{1,0:T(8,128)(2,1)S(1)}, bf16[256,128]{1,0:T(8,128)(2,1)}, u32[]{:S(2)}) copy-start(bf16[256,128]{1,0:T(8,128)(2,1)} %features_ref.3) | copy-start | bytes 196612
  52.5 20.3 %copy-start.2 = (bf16[256,128]{1,0:T(8,128)(2,1)S(1)}, bf16[256,128]{1,0:T(8,128)(2,1)}, u32[]{:S(2)}) copy-start(bf16[256,128]{1,0:T(8,128)(2,1)} %upstream_ref.1) | copy-start | bytes 196612
  52.5 20.3 %copy-start.3 = (bf16[128,128]{1,0:T(8,128)(2,1)S(1)}, bf16[128,128]{1,0:T(8,128)(2,1)}, u32[]{:S(2)}) copy-start(bf16[128,128]{1,0:T(8,128)(2,1)} %w_self_ref.1) | copy-start | bytes 98308
  52.5 20.3 %copy-start.4 = (bf16[128,128]{1,0:T(8,128)(2,1)S(1)}, bf16[128,128]{1,0:T(8,128)(2,1)}, u32[]{:S(2)}) copy-start(bf16[128,128]{1,0:T(8,128)(2,1)} %w_neigh_ref.1) | copy-start | bytes 98308
  52.5 20.3 %copy-start.5 = (f32[128]{0:T(128)S(1)}, f32[128]{0:T(128)}, u32[]{:S(2)}) copy-start(f32[128]{0:T(128)} %param.18) | copy-start | bytes 1540
  52.5 5.4 %collective-permute-start.10 = (bf16[4,128,128]{2,1,0:T(8,128)(2,1)S(1)}, bf16[4,128,128]{2,1,0:T(8,128)(2,1)S(1)}, u32[]{:S(2)}, u32[]{:S(2)}) collective-permute-start(bf16[4,128,128]{2,1,0:T(8,128)(2,1)S(1)} %get-tuple-element.72), channel_id=1, source_target_pairs={{0,3},{1,2},{2,1},{3,0},{4,7},{5,6},{6,5},{7,4},{8,11},{9,10},{10,... | collective-permute-start | bytes 393224 | tf_op jit(solution)/shard_map/scatter_col/ppermute | solution.py:108
  54.9 4.1 %collective-permute-start.8 = (bf16[4,128,128]{2,1,0:T(8,128)(2,1)S(1)}, bf16[4,128,128]{2,1,0:T(8,128)(2,1)S(1)}, u32[]{:S(2)}, u32[]{:S(2)}) collective-permute-start(bf16[4,128,128]{2,1,0:T(8,128)(2,1)S(1)} %get-tuple-element.70), channel_id=1, source_target_pairs={{0,1},{1,0},{2,3},{3,2},{4,5},{5,4},{6,7},{7,6},{8,9},{9,8},{10,11... | collective-permute-start | bytes 393224 | tf_op jit(solution)/shard_map/scatter_col/ppermute | solution.py:108
  56.3 6.2 %collective-permute-start.9 = (bf16[4,128,128]{2,1,0:T(8,128)(2,1)S(1)}, bf16[4,128,128]{2,1,0:T(8,128)(2,1)S(1)}, u32[]{:S(2)}, u32[]{:S(2)}) collective-permute-start(bf16[4,128,128]{2,1,0:T(8,128)(2,1)S(1)} %get-tuple-element.71), channel_id=1, source_target_pairs={{0,2},{1,3},{2,0},{3,1},{4,6},{5,7},{6,4},{7,5},{8,10},{9,11},{10,... | collective-permute-start | bytes 393224 | tf_op jit(solution)/shard_map/scatter_col/ppermute | solution.py:108
  62.5 9.9 %collective-permute-start.11 = (f16[2,128,128]{2,1,0:T(8,128)(2,1)S(1)}, f16[2,128,128]{2,1,0:T(8,128)(2,1)S(1)}, u32[]{:S(2)}, u32[]{:S(2)}) collective-permute-start(f16[2,128,128]{2,1,0:T(8,128)(2,1)S(1)} %get-tuple-element.121), channel_id=1, source_target_pairs={{0,4},{4,0},{1,5},{5,1},{2,6},{6,2},{3,7},{7,3},{8,12},{12,8},{9,1... | collective-permute-start | bytes 196616 | tf_op jit(solution)/shard_map/scatter_col/ppermute | solution.py:108
  74.1 26.0 %all-to-all-start.2 = ((bf16[8,2,128,128]{3,2,1,0:T(8,128)(2,1)}), bf16[8,2,128,128]{3,2,1,0:T(8,128)(2,1)S(1)}, u32[]{:S(2)}, u32[]{:S(2)}) async-start(bf16[8,2,128,128]{3,2,1,0:T(8,128)(2,1)} %get-tuple-element.74), calls=%async_computation.2 | async-start | bytes 1048576 | tf_op jit(solution)/shard_map/gather_row/all_to_all | solution.py:127
  82.2 1.9 %collective-permute-start.13 = (f32[136,128]{1,0:T(8,128)S(1)}, f32[136,128]{1,0:T(8,128)S(1)}, u32[]{:S(2)}, u32[]{:S(2)}) collective-permute-start(f32[136,128]{1,0:T(8,128)S(1)} %dynamic-slice_bitcast_fusion), channel_id=1, source_target_pairs={{0,8},{8,0},{1,9},{9,1},{2,10},{10,2},{3,11},{11,3},{4,12},{12,4},... | collective-permute-start | bytes 208904 | tf_op jit(solution)/shard_map/gather_col/weights/ppermute | solution.py:108
  83.2 5.2 %collective-permute-start.12 = (bf16[2,128,128]{2,1,0:T(8,128)(2,1)S(1)}, bf16[2,128,128]{2,1,0:T(8,128)(2,1)S(1)}, u32[]{:S(2)}, u32[]{:S(2)}) collective-permute-start(bf16[2,128,128]{2,1,0:T(8,128)(2,1)S(1)} %bitcast.97), channel_id=1, source_target_pairs={{0,4},{4,0},{1,5},{5,1},{2,6},{6,2},{3,7},{7,3},{8,12},{12,8},{9,1... | collective-permute-start | bytes 196616 | tf_op jit(solution)/shard_map/gather_col/ppermute | solution.py:108
  88.4 8.9 %collective-permute-start.14 = (bf16[2,2,128,128]{3,2,1,0:T(8,128)(2,1)S(1)}, bf16[2,2,128,128]{3,2,1,0:T(8,128)(2,1)S(1)}, u32[]{:S(2)}, u32[]{:S(2)}) collective-permute-start(bf16[2,2,128,128]{3,2,1,0:T(8,128)(2,1)S(1)} %pad_maximum_fusion.2.f0), channel_id=1, source_target_pairs={{0,1},{1,0},{2,3},{3,2},{4,5},{5,4},{6,7},{7,6},{8,9},{9,8},{10,11... | collective-permute-start | bytes 393224 | tf_op jit(solution)/shard_map/gather_col/ppermute | solution.py:108
  88.5 8.8 %collective-permute-start.15 = (bf16[2,2,128,128]{3,2,1,0:T(8,128)(2,1)S(1)}, bf16[2,2,128,128]{3,2,1,0:T(8,128)(2,1)S(1)}, u32[]{:S(2)}, u32[]{:S(2)}) collective-permute-start(bf16[2,2,128,128]{3,2,1,0:T(8,128)(2,1)S(1)} %pad_maximum_fusion.2.f0), channel_id=1, source_target_pairs={{0,2},{1,3},{2,0},{3,1},{4,6},{5,7},{6,4},{7,5},{8,10},{9,11},{10,... | collective-permute-start | bytes 393224 | tf_op jit(solution)/shard_map/gather_col/ppermute | solution.py:108
  90.7 8.0 %collective-permute-start.16 = (bf16[2,2,128,128]{3,2,1,0:T(8,128)(2,1)S(1)}, bf16[2,2,128,128]{3,2,1,0:T(8,128)(2,1)S(1)}, u32[]{:S(2)}, u32[]{:S(2)}) collective-permute-start(bf16[2,2,128,128]{3,2,1,0:T(8,128)(2,1)S(1)} %pad_maximum_fusion.2.f0), channel_id=1, source_target_pairs={{0,3},{1,2},{2,1},{3,0},{4,7},{5,6},{6,5},{7,4},{8,11},{9,10},{10,... | collective-permute-start | bytes 393224 | tf_op jit(solution)/shard_map/gather_col/ppermute | solution.py:108
  92.3 5.0 %collective-permute-start.17 = (f32[136,128]{1,0:T(8,128)S(1)}, f32[136,128]{1,0:T(8,128)S(1)}, u32[]{:S(2)}, u32[]{:S(2)}) collective-permute-start(f32[136,128]{1,0:T(8,128)S(1)} %bitcast_add_fusion.2), channel_id=1, source_target_pairs={{0,4},{4,0},{1,5},{5,1},{2,6},{6,2},{3,7},{7,3},{8,12},{12,8},{9,1... | collective-permute-start | bytes 208904 | tf_op jit(solution)/shard_map/gather_col/weights/ppermute | solution.py:108
  102.8 7.3 %collective-permute-start.18 = (bf16[32,128,128]{2,1,0:T(8,128)(2,1)S(1)}, bf16[32,128,128]{2,1,0:T(8,128)(2,1)S(1)}, u32[]{:S(2)}, u32[]{:S(2)}) collective-permute-start(bf16[32,128,128]{2,1,0:T(8,128)(2,1)S(1)} %get-tuple-element.91), channel_id=1, source_target_pairs={{0,8},{8,0},{1,9},{9,1},{2,10},{10,2},{3,11},{11,3},{4,12},{12,4},... | collective-permute-start | bytes 3145736 | tf_op jit(solution)/shard_map/scatter_row/ppermute | solution.py:108
  104.3 5.9 %collective-permute-start.19 = (f32[136,128]{1,0:T(8,128)S(1)}, f32[136,128]{1,0:T(8,128)S(1)}, u32[]{:S(2)}, u32[]{:S(2)}) collective-permute-start(f32[136,128]{1,0:T(8,128)S(1)} %add.139), channel_id=1, source_target_pairs={{0,192},{32,224},{64,128},{96,160},{128,64},{160,96},{192,0},{224,... | collective-permute-start | bytes 208904 | tf_op jit(solution)/shard_map/scatter_row/weights/ppermute | solution.py:108
  106.6 14.1 %collective-permute-start.20 = (bf16[16,128,128]{2,1,0:T(8,128)(2,1)S(1)}, bf16[16,128,128]{2,1,0:T(8,128)(2,1)S(1)}, u32[]{:S(2)}, u32[]{:S(2)}) collective-permute-start(bf16[16,128,128]{2,1,0:T(8,128)(2,1)S(1)} %bitcast.87), channel_id=1, source_target_pairs={{0,16},{16,0},{1,17},{17,1},{2,18},{18,2},{3,19},{19,3},{4,20},{20... | collective-permute-start | bytes 1572872 | tf_op jit(solution)/shard_map/gather_row/ppermute | solution.py:108
  111.5 44.5 %all-to-all-start.3 = ((bf16[16,256,128]{2,1,0:T(8,128)(2,1)}), bf16[16,256,128]{2,1,0:T(8,128)(2,1)S(1)}, u32[]{:S(2)}, u32[]{:S(2)}) async-start(bf16[16,256,128]{2,1,0:T(8,128)(2,1)} %bitcast.20), calls=%async_computation.3 | async-start | bytes 2097152 | tf_op jit(solution)/shard_map/scatter_row/all_to_all | solution.py:144
  120.7 2.4 %collective-permute-start.22 = (bf16[16,128,128]{2,1,0:T(8,128)(2,1)S(1)}, bf16[16,128,128]{2,1,0:T(8,128)(2,1)S(1)}, u32[]{:S(2)}, u32[]{:S(2)}) collective-permute-start(bf16[16,128,128]{2,1,0:T(8,128)(2,1)S(1)} %collective-permute-done.20.g1), channel_id=1, source_target_pairs={{0,8},{8,0},{1,9},{9,1},{2,10},{10,2},{3,11},{11,3},{4,12},{12,4},... | collective-permute-start | bytes 1572872 | tf_op jit(solution)/shard_map/gather_row/ppermute | solution.py:108
  121.6 3.0 %collective-permute-start.21 = (bf16[16,128,128]{2,1,0:T(8,128)(2,1)S(1)}, bf16[16,128,128]{2,1,0:T(8,128)(2,1)S(1)}, u32[]{:S(2)}, u32[]{:S(2)}) collective-permute-start(bf16[16,128,128]{2,1,0:T(8,128)(2,1)S(1)} %bitcast.88), channel_id=1, source_target_pairs={{0,8},{8,0},{1,9},{9,1},{2,10},{10,2},{3,11},{11,3},{4,12},{12,4},... | collective-permute-start | bytes 1572872 | tf_op jit(solution)/shard_map/gather_row/ppermute | solution.py:108
  123.2 4.1 %collective-permute-start.23 = (f32[136,128]{1,0:T(8,128)S(1)}, f32[136,128]{1,0:T(8,128)S(1)}, u32[]{:S(2)}, u32[]{:S(2)}) collective-permute-start(f32[136,128]{1,0:T(8,128)S(1)} %add.141), channel_id=1, source_target_pairs={{0,16},{16,0},{1,17},{17,1},{2,18},{18,2},{3,19},{19,3},{4,20},{20... | collective-permute-start | bytes 208904 | tf_op jit(solution)/shard_map/behind/weights/ppermute | solution.py:108
  127.3 8.5 %collective-permute-start.27 = (f32[136,128]{1,0:T(8,128)S(1)}, f32[136,128]{1,0:T(8,128)S(1)}, u32[]{:S(2)}, u32[]{:S(2)}) collective-permute-start(f32[136,128]{1,0:T(8,128)S(1)} %add.142), channel_id=1, source_target_pairs={{0,1},{1,0},{2,3},{3,2},{4,5},{5,4},{6,7},{7,6},{8,9},{9,8},{10,11... | collective-permute-start | bytes 208904 | tf_op jit(solution)/shard_map/scatter_col/weights/ppermute | solution.py:108
  127.4 8.4 %collective-permute-start.28 = (f32[136,128]{1,0:T(8,128)S(1)}, f32[136,128]{1,0:T(8,128)S(1)}, u32[]{:S(2)}, u32[]{:S(2)}) collective-permute-start(f32[136,128]{1,0:T(8,128)S(1)} %add.142), channel_id=1, source_target_pairs={{0,2},{1,3},{2,0},{3,1},{4,6},{5,7},{6,4},{7,5},{8,10},{9,11},{10,... | collective-permute-start | bytes 208904 | tf_op jit(solution)/shard_map/scatter_col/weights/ppermute | solution.py:108
  131.9 5.0 %collective-permute-start.29 = (f32[136,128]{1,0:T(8,128)S(1)}, f32[136,128]{1,0:T(8,128)S(1)}, u32[]{:S(2)}, u32[]{:S(2)}) collective-permute-start(f32[136,128]{1,0:T(8,128)S(1)} %add.142), channel_id=1, source_target_pairs={{0,3},{1,2},{2,1},{3,0},{4,7},{5,6},{6,5},{7,4},{8,11},{9,10},{10,... | collective-permute-start | bytes 208904 | tf_op jit(solution)/shard_map/scatter_col/weights/ppermute | solution.py:108
  131.9 5.0 %collective-permute-start.24 = (bf16[4,128,128]{2,1,0:T(8,128)(2,1)S(1)}, bf16[4,128,128]{2,1,0:T(8,128)(2,1)S(1)}, u32[]{:S(2)}, u32[]{:S(2)}) collective-permute-start(bf16[4,128,128]{2,1,0:T(8,128)(2,1)S(1)} %get-tuple-element.104), channel_id=1, source_target_pairs={{0,1},{1,0},{2,3},{3,2},{4,5},{5,4},{6,7},{7,6},{8,9},{9,8},{10,11... | collective-permute-start | bytes 393224 | tf_op jit(solution)/shard_map/scatter_col/ppermute | solution.py:108
  131.9 8.4 %collective-permute-start.25 = (bf16[4,128,128]{2,1,0:T(8,128)(2,1)S(1)}, bf16[4,128,128]{2,1,0:T(8,128)(2,1)S(1)}, u32[]{:S(2)}, u32[]{:S(2)}) collective-permute-start(bf16[4,128,128]{2,1,0:T(8,128)(2,1)S(1)} %get-tuple-element.105), channel_id=1, source_target_pairs={{0,2},{1,3},{2,0},{3,1},{4,6},{5,7},{6,4},{7,5},{8,10},{9,11},{10,... | collective-permute-start | bytes 393224 | tf_op jit(solution)/shard_map/scatter_col/ppermute | solution.py:108
  135.8 7.1 %collective-permute-start.26 = (bf16[4,128,128]{2,1,0:T(8,128)(2,1)S(1)}, bf16[4,128,128]{2,1,0:T(8,128)(2,1)S(1)}, u32[]{:S(2)}, u32[]{:S(2)}) collective-permute-start(bf16[4,128,128]{2,1,0:T(8,128)(2,1)S(1)} %get-tuple-element.106), channel_id=1, source_target_pairs={{0,3},{1,2},{2,1},{3,0},{4,7},{5,6},{6,5},{7,4},{8,11},{9,10},{10,... | collective-permute-start | bytes 393224 | tf_op jit(solution)/shard_map/scatter_col/ppermute | solution.py:108
  142.9 6.0 %collective-permute-start.31 = (f32[136,128]{1,0:T(8,128)S(1)}, f32[136,128]{1,0:T(8,128)S(1)}, u32[]{:S(2)}, u32[]{:S(2)}) collective-permute-start(f32[136,128]{1,0:T(8,128)S(1)} %add_add_fusion.1), channel_id=1, source_target_pairs={{0,32},{32,0},{64,96},{96,64},{128,160},{160,128},{192,224},{224,1... | collective-permute-start | bytes 208904 | tf_op jit(solution)/shard_map/weights/ppermute | solution.py:108
  143.0 5.9 %collective-permute-start.32 = (f32[136,128]{1,0:T(8,128)S(1)}, f32[136,128]{1,0:T(8,128)S(1)}, u32[]{:S(2)}, u32[]{:S(2)}) collective-permute-start(f32[136,128]{1,0:T(8,128)S(1)} %add_add_fusion.1), channel_id=1, source_target_pairs={{0,64},{32,96},{64,0},{96,32},{128,192},{160,224},{192,128},{224,1... | collective-permute-start | bytes 208904 | tf_op jit(solution)/shard_map/weights/ppermute | solution.py:108
  144.3 5.5 %collective-permute-start.33 = (f32[136,128]{1,0:T(8,128)S(1)}, f32[136,128]{1,0:T(8,128)S(1)}, u32[]{:S(2)}, u32[]{:S(2)}) collective-permute-start(f32[136,128]{1,0:T(8,128)S(1)} %add_add_fusion.1), channel_id=1, source_target_pairs={{0,96},{32,64},{64,32},{96,0},{128,224},{160,192},{192,160},{224,1... | collective-permute-start | bytes 208904 | tf_op jit(solution)/shard_map/weights/ppermute | solution.py:108
  146.6 4.8 %collective-permute-start.30 = (bf16[2,128,128]{2,1,0:T(8,128)(2,1)S(1)}, bf16[2,128,128]{2,1,0:T(8,128)(2,1)S(1)}, u32[]{:S(2)}, u32[]{:S(2)}) collective-permute-start(bf16[2,128,128]{2,1,0:T(8,128)(2,1)S(1)} %slice.24), channel_id=1, source_target_pairs={{0,4},{4,0},{1,5},{5,1},{2,6},{6,2},{3,7},{7,3},{8,12},{12,8},{9,1... | collective-permute-start | bytes 196616 | tf_op jit(solution)/shard_map/scatter_col/ppermute | solution.py:108
  151.4 4.5 %collective-permute-start.34 = (f32[136,128]{1,0:T(8,128)S(1)}, f32[136,128]{1,0:T(8,128)S(1)}, u32[]{:S(2)}, u32[]{:S(2)}) collective-permute-start(f32[136,128]{1,0:T(8,128)S(1)} %add_add_fusion), channel_id=1, source_target_pairs={{0,8},{8,0},{1,9},{9,1},{2,10},{10,2},{3,11},{11,3},{4,12},{12,4},... | collective-permute-start | bytes 208904 | tf_op jit(solution)/shard_map/weights/ppermute | solution.py:108
